TPU v7x, 128 devices: a whole 4x4x4 slice. The times are simulated.
128 devices in a mesh: ctx: 32 (over z, y, x_hi), fsdp: 4 (over x_lo, core).
Axes of the slice: x: 4 (x_hi: 2, x_lo: 2; x = x_hi * 2 + x_lo), y: 4, z: 4, core: 2. Of those that a mesh axis runs over, the one named last changes fastest.
Arguments:
- inputs: bfloat16 [4, 4096, 768], P('fsdp', 'ctx'), may hold values from -6 to 6
- qkv_weight: bfloat16 [1, 768, 2304], P(None, ('ctx', 'fsdp')), may hold values from -0.3125 to 0.3125
- qkv_bias: bfloat16 [1, 2304], P(None, ('ctx', 'fsdp')), may hold values from -3 to 3
- out_weight: bfloat16 [1, 768, 768], P(None, ('ctx', 'fsdp')), may hold values from -1.75 to 1.75
- out_bias: bfloat16 [1, 768], P(None, ('ctx', 'fsdp')), may hold values from -3 to 3
- up_weight: bfloat16 [1, 768, 3072], P(None, ('ctx', 'fsdp')), may hold values from -0.21875 to 0.21875
- up_bias: bfloat16 [1, 3072], P(None, ('ctx', 'fsdp')), may hold values from -3 to 3
- down_weight: bfloat16 [1, 3072, 768], P(None, ('ctx', 'fsdp')), may hold values from -0.109375 to 0.109375
- down_bias: bfloat16 [1, 768], P(None, ('ctx', 'fsdp')), may hold values from -3 to 3
- attn_gain: bfloat16 [1, 768], P(None, ('ctx', 'fsdp')), may hold values from 0.099609375 to 1.8984375
- attn_shift: bfloat16 [1, 768], P(None, ('ctx', 'fsdp')), may hold values from -2 to 2
- mlp_gain: bfloat16 [1, 768], P(None, ('ctx', 'fsdp')), may hold values from 0.099609375 to 1.8984375
- mlp_shift: bfloat16 [1, 768], P(None, ('ctx', 'fsdp')), may hold values from -2 to 2
- cotangent: bfloat16 [4, 4096, 768], P('fsdp', 'ctx'), may hold values from -6 to 6
Outputs:
- outputs: bfloat16 [4, 4096, 768], P('fsdp', 'ctx')
- input_grad: float32 [4, 4096, 768], P('fsdp', 'ctx')
- qkv_weight_grad: float32 [1, 768, 2304], P(None, ('ctx', 'fsdp'))
- qkv_bias_grad: float32 [1, 2304], P(None, ('ctx', 'fsdp'))
- out_weight_grad: float32 [1, 768, 768], P(None, ('ctx', 'fsdp'))
- out_bias_grad: float32 [1, 768], P(None, ('ctx', 'fsdp'))
- up_weight_grad: float32 [1, 768, 3072], P(None, ('ctx', 'fsdp'))
- up_bias_grad: float32 [1, 3072], P(None, ('ctx', 'fsdp'))
- down_weight_grad: float32 [1, 3072, 768], P(None, ('ctx', 'fsdp'))
- down_bias_grad: float32 [1, 768], P(None, ('ctx', 'fsdp'))
- attn_gain_grad: float32 [1, 768], P(None, ('ctx', 'fsdp'))
- attn_shift_grad: float32 [1, 768], P(None, ('ctx', 'fsdp'))
- mlp_gain_grad: float32 [1, 768], P(None, ('ctx', 'fsdp'))
- mlp_shift_grad: float32 [1, 768], P(None, ('ctx', 'fsdp'))
All inputs are finite; a program needn't handle non-finite values.
Results may differ from a plain program's by a relative error of at most 0.01225.
The roundings to bfloat16 on the way count: a program that leaves them out, or rounds other values in their place, can miss the bound.
Values may be sent and summed in bfloat16 or wider, within the bound.
A program may use at most 192 MiB of HBM per device.

v0:
```python
from functools import partial

import jax
import jax.numpy as jnp
from jax import lax
from jax.sharding import PartitionSpec as P

H = 12
HD = 64
ROT = 16
LAYERS = 1


score_scale = 0.125
far_below = -1e30


def for_sending(shard):
    return jax.tree.map(lambda a: a.astype(jnp.bfloat16) if a.dtype == jnp.float32 else a, shard)


def norm_rows(values, gain_row, shift_row):
    center = values - jnp.mean(values, axis=-1, keepdims=True)
    spread = jnp.mean(center * center, axis=-1, keepdims=True)
    return center * lax.rsqrt(spread + 1e-05) * gain_row + shift_row


def rotary_tables(positions):
    halves = ROT // 2
    frequency = 10000.0 ** (-2.0 * jnp.arange(halves, dtype=jnp.float32) / ROT)
    angle_table = positions[:, None] * frequency[None, :]
    return (jnp.cos(angle_table), jnp.sin(angle_table))


def rotate(heads_in, cosine_table, sinus_table):
    halves = ROT // 2
    front = heads_in[..., :halves]
    behind = heads_in[..., halves:ROT]
    cos_b = cosine_table[:, None, :]
    sin_b = sinus_table[:, None, :]
    return jnp.concatenate(
        [front * cos_b - behind * sin_b, behind * cos_b + front * sin_b, heads_in[..., ROT:]],
        axis=-1,
    )


def inner_first(left, right):
    return lax.dot_general(
        left, right, (((0,), (0,)), ((), ())), preferred_element_type=jnp.float32
    )


def inner_last(left, right):
    return lax.dot_general(
        left, right, (((1,), (1,)), ((), ())), preferred_element_type=jnp.float32
    )


def split_product(form, probs, other):
    upper_part = probs.astype(jnp.bfloat16)
    lower_part = (probs - upper_part.astype(jnp.float32)).astype(jnp.bfloat16)
    first = jnp.einsum(form, upper_part, other, preferred_element_type=jnp.float32)
    return first + jnp.einsum(form, lower_part, other, preferred_element_type=jnp.float32)


def scores_of(queries, query_offset, keys_part, key_offset):
    query_count = queries.shape[0]
    key_count = keys_part.shape[0]
    query_heads = queries.reshape(query_count, H, HD)
    key_heads = keys_part.reshape(key_count, H, HD)
    scores = (
        jnp.einsum("qhd,khd->hqk", query_heads, key_heads, preferred_element_type=jnp.float32)
        * score_scale
    )
    query_place = query_offset + jnp.arange(query_count, dtype=jnp.int32)
    key_place = key_offset + jnp.arange(key_count, dtype=jnp.int32)
    allowed = key_place[None, :] <= query_place[:, None]
    return jnp.where(allowed[None], scores, far_below)


def in_blocks(update, state_now, portion):
    row_count = portion[0].shape[0]
    sub_rows = 512
    turns = row_count // sub_rows

    def one_turn(turn_index, state_in):
        sub_part = tuple(
            (
                lax.dynamic_slice_in_dim(member, turn_index * sub_rows, sub_rows, 0)
                for member in portion
            )
        )
        return update(state_in, sub_part, turn_index * sub_rows)

    return lax.fori_loop(0, turns, one_turn, state_now)


def forward_update(queries, query_offset):
    query_count = queries.shape[0]

    def forward_compute(state_in, portion, key_offset):
        top_old, total_old, accum_old = state_in
        keys_part, values_part = portion
        scores = scores_of(queries, query_offset, keys_part, key_offset)
        top_new = jnp.maximum(top_old, jnp.max(scores, axis=-1))
        fading = jnp.exp(top_old - top_new)
        weights = jnp.exp(scores - top_new[..., None])
        value_heads = values_part.reshape(values_part.shape[0], H, HD)
        accum_new = accum_old * fading.T[..., None] + split_product(
            "hqk,khd->qhd", weights, value_heads
        )
        return (top_new, total_old * fading + jnp.sum(weights, axis=-1), accum_new)

    def update(state_in, portion, key_offset):
        return lax.cond(
            key_offset <= query_offset + query_count - 1,
            lambda state_arg: forward_compute(state_arg, portion, key_offset),
            lambda state_arg: state_arg,
            state_in,
        )

    return update


def query_grad_update(queries, grad_attended, query_offset, lse_rows, delta_rows):
    query_count = queries.shape[0]
    grad_heads = grad_attended.reshape(query_count, H, HD)

    def query_compute(state_in, portion, key_offset):
        keys_part, values_part = portion
        key_count = keys_part.shape[0]
        scores = scores_of(queries, query_offset, keys_part, key_offset)
        probability = jnp.exp(scores - lse_rows[..., None])
        grad_probs = jnp.einsum(
            "qhd,khd->hqk",
            grad_heads,
            values_part.reshape(key_count, H, HD),
            preferred_element_type=jnp.float32,
        )
        grad_scores = (probability * (grad_probs - delta_rows[..., None])).astype(jnp.bfloat16)
        return (
            state_in
            + jnp.einsum(
                "hqk,khd->qhd",
                grad_scores,
                keys_part.reshape(key_count, H, HD),
                preferred_element_type=jnp.float32,
            )
            * score_scale
        )

    def update(state_in, portion, key_offset):
        return lax.cond(
            key_offset <= query_offset + query_count - 1,
            lambda state_arg: query_compute(state_arg, portion, key_offset),
            lambda state_arg: state_arg,
            state_in,
        )

    return update


def key_grad_update(keys_here, values_here, key_offset, lse_all, delta_all):
    key_count = keys_here.shape[0]
    value_heads = values_here.reshape(key_count, H, HD)

    def key_compute(state_in, portion, query_offset):
        grad_keys, grad_values = state_in
        queries_part, grad_part = portion
        rows_now = queries_part.shape[0]
        lse_part = lax.dynamic_slice_in_dim(lse_all, query_offset, rows_now, 1)
        delta_part = lax.dynamic_slice_in_dim(delta_all, query_offset, rows_now, 1)
        scores = scores_of(queries_part, query_offset, keys_here, key_offset)
        probability = jnp.exp(scores - lse_part[..., None])
        grad_heads = grad_part.reshape(rows_now, H, HD)
        grad_values = grad_values + split_product("hqk,qhd->khd", probability, grad_heads)
        grad_probs = jnp.einsum(
            "qhd,khd->hqk", grad_heads, value_heads, preferred_element_type=jnp.float32
        )
        grad_scores = (probability * (grad_probs - delta_part[..., None])).astype(jnp.bfloat16)
        grad_keys = (
            grad_keys
            + jnp.einsum(
                "hqk,qhd->khd",
                grad_scores,
                queries_part.reshape(rows_now, H, HD),
                preferred_element_type=jnp.float32,
            )
            * score_scale
        )
        return (grad_keys, grad_values)

    def update(state_in, portion, query_offset):
        rows_now = portion[0].shape[0]
        return lax.cond(
            query_offset + rows_now - 1 >= key_offset,
            lambda state_arg: key_compute(state_arg, portion, query_offset),
            lambda state_arg: state_arg,
            state_in,
        )

    return update


def forward_layer(residual, gathered, cosine_table, sinus_table, query_offset):
    (
        w_qkv,
        b_qkv,
        w_out,
        b_out,
        w_up,
        b_up,
        w_down,
        b_down,
        gain_attn,
        shift_attn,
        gain_mlp,
        shift_mlp,
    ) = gathered
    block_rows = residual.shape[0]
    normed_attn = norm_rows(
        residual, gain_attn.astype(jnp.float32), shift_attn.astype(jnp.float32)
    ).astype(jnp.bfloat16)
    normed_mlp = norm_rows(
        residual, gain_mlp.astype(jnp.float32), shift_mlp.astype(jnp.float32)
    ).astype(jnp.bfloat16)
    qkv_rows = (
        jnp.dot(normed_attn, w_qkv, preferred_element_type=jnp.float32) + b_qkv.astype(jnp.float32)
    ).reshape(block_rows, 3, H, HD)
    queries = (
        rotate(qkv_rows[:, 0], cosine_table, sinus_table)
        .astype(jnp.bfloat16)
        .reshape(block_rows, H * HD)
    )
    keys_here = (
        rotate(qkv_rows[:, 1], cosine_table, sinus_table)
        .astype(jnp.bfloat16)
        .reshape(block_rows, H * HD)
    )
    values_here = qkv_rows[:, 2].astype(jnp.bfloat16).reshape(block_rows, H * HD)
    initial = (
        jnp.full((H, block_rows), far_below, jnp.float32),
        jnp.zeros((H, block_rows), jnp.float32),
        jnp.zeros((block_rows, H, HD), jnp.float32),
    )
    update = forward_update(queries, query_offset)
    top_row, total_row, accum = in_blocks(
        update,
        initial,
        (
            lax.all_gather(keys_here, "ctx", axis=0, tiled=True),
            lax.all_gather(values_here, "ctx", axis=0, tiled=True),
        ),
    )
    lse_rows = top_row + jnp.log(total_row)
    attended = (accum / total_row.T[..., None]).reshape(block_rows, H * HD)
    attended_low = attended.astype(jnp.bfloat16)
    branch_attn = jnp.dot(attended_low, w_out, preferred_element_type=jnp.float32) + b_out.astype(
        jnp.float32
    )
    upper = jnp.dot(normed_mlp, w_up, preferred_element_type=jnp.float32) + b_up.astype(jnp.float32)
    gelu_low = jax.nn.gelu(upper, approximate=False).astype(jnp.bfloat16)
    branch_mlp = jnp.dot(gelu_low, w_down, preferred_element_type=jnp.float32) + b_down.astype(
        jnp.float32
    )
    residual_next = residual + branch_attn + branch_mlp
    saved = (
        normed_attn,
        normed_mlp,
        queries,
        keys_here,
        values_here,
        attended,
        attended_low,
        lse_rows,
        upper,
        gelu_low,
        None,
    )
    return (residual_next, saved)


def backward_layer(grad_res, residual_in, gathered, saved, cosine_table, sinus_table, query_offset):
    (
        w_qkv,
        b_qkv,
        w_out,
        b_out,
        w_up,
        b_up,
        w_down,
        b_down,
        gain_attn,
        shift_attn,
        gain_mlp,
        shift_mlp,
    ) = gathered
    (
        normed_attn,
        normed_mlp,
        queries,
        keys_here,
        values_here,
        attended,
        attended_low,
        lse_rows,
        upper,
        gelu_low,
        keys_whole,
    ) = saved
    block_rows = grad_res.shape[0]
    grad_low = grad_res.astype(jnp.bfloat16)
    grad_branch_bias = jnp.sum(grad_low.astype(jnp.float32), axis=0)
    grad_attended = inner_last(grad_low, w_out).astype(jnp.bfloat16)
    grad_gelu = inner_last(grad_low, w_down)
    gelu_pull = jax.vjp(partial(jax.nn.gelu, approximate=False), upper)[1]
    grad_upper = gelu_pull(grad_gelu)[0].astype(jnp.bfloat16)
    grad_b_up = jnp.sum(grad_upper.astype(jnp.float32), axis=0)
    grad_normed_mlp = inner_last(grad_upper, w_up)
    delta_rows = jnp.sum(
        grad_attended.reshape(block_rows, H, HD).astype(jnp.float32)
        * attended.reshape(block_rows, H, HD),
        axis=-1,
    ).T
    lse_all, delta_all = (
        lax.all_gather(lse_rows, "ctx", axis=1, tiled=True),
        lax.all_gather(delta_rows, "ctx", axis=1, tiled=True),
    )
    zero_rows = jnp.zeros((block_rows, H, HD), jnp.float32)
    query_update = query_grad_update(queries, grad_attended, query_offset, lse_rows, delta_rows)
    grad_queries = in_blocks(
        query_update,
        zero_rows,
        (
            lax.all_gather(keys_here, "ctx", axis=0, tiled=True),
            lax.all_gather(values_here, "ctx", axis=0, tiled=True),
        ),
    )
    key_update = key_grad_update(keys_here, values_here, query_offset, lse_all, delta_all)
    grad_keys, grad_values = in_blocks(
        key_update,
        (zero_rows, zero_rows),
        (
            lax.all_gather(queries, "ctx", axis=0, tiled=True),
            lax.all_gather(grad_attended, "ctx", axis=0, tiled=True),
        ),
    )
    grad_q_turned = rotate(grad_queries, cosine_table, -sinus_table)
    grad_k_turned = rotate(grad_keys, cosine_table, -sinus_table)
    grad_qkv = (
        jnp.stack([grad_q_turned, grad_k_turned, grad_values], axis=1)
        .reshape(block_rows, 3 * H * HD)
        .astype(jnp.bfloat16)
    )
    grad_b_qkv = jnp.sum(grad_qkv.astype(jnp.float32), axis=0)
    grad_normed_attn = inner_last(grad_qkv, w_qkv)
    attn_pull = jax.vjp(
        norm_rows, residual_in, gain_attn.astype(jnp.float32), shift_attn.astype(jnp.float32)
    )[1]
    grad_x_attn, grad_gain_attn, grad_shift_attn = attn_pull(grad_normed_attn)
    mlp_pull = jax.vjp(
        norm_rows, residual_in, gain_mlp.astype(jnp.float32), shift_mlp.astype(jnp.float32)
    )[1]
    grad_x_mlp, grad_gain_mlp, grad_shift_mlp = mlp_pull(grad_normed_mlp)
    grad_input = grad_res + grad_x_attn + grad_x_mlp
    pairs = (normed_attn, attended_low, normed_mlp, gelu_low, grad_qkv, grad_low, grad_upper)
    smalls = (
        grad_b_qkv,
        grad_branch_bias,
        grad_b_up,
        grad_branch_bias,
        grad_gain_attn,
        grad_shift_attn,
        grad_gain_mlp,
        grad_shift_mlp,
    )
    return (grad_input, pairs, smalls)


def body(
    inputs,
    qkv_weight,
    qkv_bias,
    out_weight,
    out_bias,
    up_weight,
    up_bias,
    down_weight,
    down_bias,
    attn_gain,
    attn_shift,
    mlp_gain,
    mlp_shift,
    cotangent,
):
    block_rows = inputs.shape[1]
    query_offset = lax.axis_index("ctx") * block_rows
    positions = (query_offset + jnp.arange(block_rows, dtype=jnp.int32)).astype(jnp.float32)
    cosine_table, sinus_table = rotary_tables(positions)
    shards_all = (
        qkv_weight,
        qkv_bias,
        out_weight,
        out_bias,
        up_weight,
        up_bias,
        down_weight,
        down_bias,
        attn_gain,
        attn_shift,
        mlp_gain,
        mlp_shift,
    )
    residual = inputs[0].astype(jnp.float32)
    layer_index = 0
    shards_here = tuple((member[layer_index] for member in shards_all))
    gathered = jax.tree.map(
        lambda part, own: part.astype(own.dtype),
        lax.all_gather(for_sending(shards_here), ("ctx", "fsdp"), axis=0, tiled=True),
        shards_here,
    )
    residual_next, saved = forward_layer(
        residual, gathered, cosine_table, sinus_table, query_offset
    )
    stored = [(residual, gathered, saved)]
    outputs = residual_next.astype(jnp.bfloat16)[None]
    grad_res = cotangent[0].astype(jnp.float32)
    per_layer = []
    for layer_index in reversed(range(LAYERS)):
        residual_in, gathered_fwd, saved = stored[layer_index]
        shards_here = tuple((member[layer_index] for member in shards_all))
        gathered = jax.tree.map(
            lambda part, own: part.astype(own.dtype),
            lax.all_gather(for_sending(shards_here), ("ctx", "fsdp"), axis=0, tiled=True),
            shards_here,
        )
        grad_res, pairs, smalls = backward_layer(
            grad_res, residual_in, gathered, saved, cosine_table, sinus_table, query_offset
        )
        normed_attn, attended_low, normed_mlp, gelu_low, grad_qkv, grad_low, grad_upper = pairs
        grads_full = (
            inner_first(normed_attn, grad_qkv),
            smalls[0],
            inner_first(attended_low, grad_low),
            smalls[1],
            inner_first(normed_mlp, grad_upper),
            smalls[2],
            inner_first(gelu_low, grad_low),
            smalls[3],
            smalls[4],
            smalls[5],
            smalls[6],
            smalls[7],
        )
        grads_mine = (
            lax.psum_scatter(grads_full[0], ("ctx", "fsdp"), scatter_dimension=0, tiled=True),
            lax.psum_scatter(grads_full[1], ("ctx", "fsdp"), scatter_dimension=0, tiled=True),
            lax.psum_scatter(grads_full[2], ("ctx", "fsdp"), scatter_dimension=0, tiled=True),
            lax.psum_scatter(grads_full[3], ("ctx", "fsdp"), scatter_dimension=0, tiled=True),
            lax.psum_scatter(grads_full[4], ("ctx", "fsdp"), scatter_dimension=0, tiled=True),
            lax.psum_scatter(grads_full[5], ("ctx", "fsdp"), scatter_dimension=0, tiled=True),
            lax.psum_scatter(grads_full[6], ("ctx", "fsdp"), scatter_dimension=0, tiled=True),
            lax.psum_scatter(grads_full[7], ("ctx", "fsdp"), scatter_dimension=0, tiled=True),
            lax.psum_scatter(grads_full[8], ("ctx", "fsdp"), scatter_dimension=0, tiled=True),
            lax.psum_scatter(grads_full[9], ("ctx", "fsdp"), scatter_dimension=0, tiled=True),
            lax.psum_scatter(grads_full[10], ("ctx", "fsdp"), scatter_dimension=0, tiled=True),
            lax.psum_scatter(grads_full[11], ("ctx", "fsdp"), scatter_dimension=0, tiled=True),
        )
        per_layer.insert(0, grads_mine)
    stacked = tuple((jnp.stack([per_layer[0][member_index]]) for member_index in range(12)))
    return (
        outputs,
        grad_res[None],
        stacked[0],
        stacked[1],
        stacked[2],
        stacked[3],
        stacked[4],
        stacked[5],
        stacked[6],
        stacked[7],
        stacked[8],
        stacked[9],
        stacked[10],
        stacked[11],
    )


def solution(mesh):
    in_specs = (
        P("fsdp", "ctx", None),
        P(None, ("ctx", "fsdp"), None),
        P(None, ("ctx", "fsdp")),
        P(None, ("ctx", "fsdp"), None),
        P(None, ("ctx", "fsdp")),
        P(None, ("ctx", "fsdp"), None),
        P(None, ("ctx", "fsdp")),
        P(None, ("ctx", "fsdp"), None),
        P(None, ("ctx", "fsdp")),
        P(None, ("ctx", "fsdp")),
        P(None, ("ctx", "fsdp")),
        P(None, ("ctx", "fsdp")),
        P(None, ("ctx", "fsdp")),
        P("fsdp", "ctx", None),
    )
    out_specs = (
        P("fsdp", "ctx", None),
        P("fsdp", "ctx", None),
        P(None, ("ctx", "fsdp"), None),
        P(None, ("ctx", "fsdp")),
        P(None, ("ctx", "fsdp"), None),
        P(None, ("ctx", "fsdp")),
        P(None, ("ctx", "fsdp"), None),
        P(None, ("ctx", "fsdp")),
        P(None, ("ctx", "fsdp"), None),
        P(None, ("ctx", "fsdp")),
        P(None, ("ctx", "fsdp")),
        P(None, ("ctx", "fsdp")),
        P(None, ("ctx", "fsdp")),
        P(None, ("ctx", "fsdp")),
    )
    return jax.shard_map(body, mesh=mesh, in_specs=in_specs, out_specs=out_specs, check_vma=False)
```

profile of v0, /device:TPU:1, one launch (start us, length us, event | category | flops | bytes accessed | tf_op | source)
XLA Modules:
  0.0 1786.8 jit_solution(16986319130142868591)
XLA Ops:
  12.5 68.2 %all-gather.31.cloned.1.call-done = bf16[1,768,768]{2,0,1:T(2,128)(2,1)} async-done(((bf16[1,6,768]{2,0,1:T(2,128)(2,1)}), bf16[1,768,768]{2,0,1:T(2,128)(2,1)}) %all-gather.31.cloned.1.call-update) | async-done | bytes 1179664 | tf_op jit(solution)/shard_map/all_gather | solution.py:419
  85.7 63.7 %all-reduce.22 = (bf16[3072]{0:T(1024)(128)(2,1)S(1)}, bf16[768]{0:T(1024)(128)(2,1)S(1)}, bf16[768]{0:T(1024)(128)(2,1)S(1)}, bf16[768]{0:T(1024)(128)(2,1)}, b...) all-reduce(bf16[3072]{0:T(1024)(128)(2,1)S(1)} %dynamic-update-slic, ...), channel_id=11, replica_groups=mesh['ctx'=32,'fsdp'=4] {'ctx','fsdp'}, use_global_device_ids=true, to_apply=%add.6 | all-reduce | flops 9984 | bytes 39936
  157.9 64.6 %all-gather.33.cloned.1.call-done = bf16[1,768,3072]{2,0,1:T(2,128)(2,1)} async-done(((bf16[1,6,3072]{2,0,1:T(2,128)(2,1)}), bf16[1,768,3072]{2,0,1:T(2,128)(2,1)}) %all-gather.33.cloned.1.call-update) | async-done | bytes 4718608 | tf_op jit(solution)/shard_map/all_gather | solution.py:419
  222.6 10.4 multiply_convert_fusion.1
  241.3 48.8 %all-gather.35.cloned.1.call-done = bf16[1,3072,768]{2,1,0:T(8,128)(2,1)} async-done(((bf16[1,24,768]{2,1,0:T(8,128)(2,1)}), bf16[1,3072,768]{2,1,0:T(8,128)(2,1)}) %all-gather.35.cloned.1.call-update) | async-done | bytes 4718608 | tf_op jit(solution)/shard_map/all_gather | solution.py:419
  300.8 81.2 %all-gather.27.cloned.1.call-done = bf16[4096,768]{1,0:T(8,128)(2,1)} async-done(((bf16[128,768]{1,0:T(8,128)(2,1)}), bf16[4096,768]{1,0:T(8,128)(2,1)}) %all-gather.27.cloned.1.call-update) | async-done | bytes 6291472 | tf_op jit(solution)/shard_map/all_gather | solution.py:345
  382.1 9.1 copy.72
  391.2 102.6 %all-gather.21.cloned.1.call-done = bf16[4096,768]{0,1:T(8,128)(2,1)} async-done(((bf16[128,768]{0,1:T(8,128)(2,1)}), bf16[4096,768]{0,1:T(8,128)(2,1)}) %all-gather.21.cloned.1.call-update) | async-done | bytes 6291472 | tf_op jit(solution)/shard_map/all_gather | solution.py:251
  493.8 111.8 %all-gather.23.cloned.1.call-done = bf16[4096,768]{0,1:T(8,128)(2,1)} async-done(((bf16[128,768]{0,1:T(8,128)(2,1)}), bf16[4096,768]{0,1:T(8,128)(2,1)}) %all-gather.23.cloned.1.call-update) | async-done | bytes 6291472 | tf_op jit(solution)/shard_map/all_gather | solution.py:252
  613.8 7.3 while.57
  613.8 7.2 conditional.7
  622.8 170.6 %all_gather.77 = f32[12,4096]{1,0:T(8,128)} all-gather(f32[12,128]{1,0:T(8,128)S(1)} %get-tuple-element.1922), channel_id=1, replica_groups=mesh['ctx'=32,'fsdp'=4] {'ctx'}, dimensions={1}, use_global_device_ids=true | all-gather | bytes 202752 | tf_op jit(solution)/shard_map/all_gather | solution.py:326
  793.4 80.3 %all_gather.79 = f32[12,4096]{1,0:T(8,128)} all-gather(f32[12,128]{1,0:T(8,128)S(1)} %get-tuple-element.1921), channel_id=1, replica_groups=mesh['ctx'=32,'fsdp'=4] {'ctx'}, dimensions={1}, use_global_device_ids=true | all-gather | bytes 202752 | tf_op jit(solution)/shard_map/all_gather | solution.py:327
  874.5 77.1 %while.58 = (s32[]{:T(128)}, f32[128,12,64]{0,2,1:T(8,128)}, f32[128,12,64]{0,2,1:T(8,128)S(1)}, s32[]{:T(128)}, bf16[4096,768]{0,1:T(8,128)(2,1)}, /*index=5*/b...) while((s32[]{:T(128)}, f32[128,12,64]{0,2,1:T(8,128)}, ...), condition=%wide.region_16.17_spmd, body=%wide.region_13.16_spmd.sunk | while | flops 512426624 | bytes 29775264 | solution.py:95
  874.5 9.6 conditional.8
  884.1 9.7 conditional.8
  893.8 9.6 conditional.8
  903.5 9.6 conditional.8
  913.1 9.6 conditional.8
  922.7 9.6 conditional.8
  932.3 9.6 conditional.8
  941.9 9.6 conditional.8
  960.4 388.8 %fusion.145 = (f32[8,2304]{1,0:T(8,128)S(1)}, f32[8,768]{1,0:T(8,128)S(1)}, f32[8,3072]{1,0:T(8,128)S(1)}) fusion(f32[768,2304]{1,0:T(8,128)} %fusion.118, f32[768,768]{1,0:T(8,128)S(1)} %fusion.123, f32[768,3072]{1,0:T(8,128)} %fusion.138), kind=kCustom, calls=%all-reduce-scatter.3 | all-reduce-scatter fusion | flops 6291457 | bytes 19070976
  1357.9 5.8 fusion.46
  1368.9 9.0 collective-permute-start.41
  1385.6 11.0 collective-permute-start.44
  1396.6 8.7 collective-permute-start.45
  1502.3 63.1 %all-reduce.21 = (f32[2304]{0:T(1024)S(1)}, f32[768]{0:T(1024)S(1)}, f32[3072]{0:T(1024)S(1)}, f32[768]{0:T(1024)S(1)}, f32[768]{0:T(1024)S(1)}, /*index=5*/f32[768]{0:T(1024)S(1)}, f32[768]{0:T(1024)S(1)}) all-reduce(f32[2304]{0:T(1024)S(1)} %reduce_sum.155, ...), channel_id=15, replica_groups=mesh['ctx'=32,'fsdp'=4] {'ctx','fsdp'}, use_global_device_ids=true, to_apply=%region_23.24.clone | all-reduce | flops 9216 | bytes 73728
  1615.9 7.0 collective-permute-start.66
  1674.1 19.8 %concatenate.17 = f32[262,768]{1,0:T(8,128)S(1)} concatenate(f32[6,768]{1,0:T(8,128)S(1)} %copy-done.78, f32[8,768]{1,0:T(8,128)} %copy-done.116, f32[8,768]{1,0:T(8,128)} %collective-permute-done.61, f32[8,768]{1,0:T(8,128)} %copy-done.115, f32[8,768]{1,0:T(8,128)} %collective-permute-done.59, f32[8,768]{1,0:T(8,128)} %copy-done.114, f32[8,768]{1,0:T(8,128)} %copy-done.113, ...), dimensions={0} | concatenate | bytes 1609728
  1704.0 30.0 %concatenate.16 = f32[262,2304]{1,0:T(8,128)S(1)} concatenate(f32[6,2304]{1,0:T(8,128)S(1)} %collective-permute-done.31, f32[8,2304]{1,0:T(8,128)} %copy-done.69, f32[8,2304]{1,0:T(8,128)} %copy-done.67, f32[8,2304]{1,0:T(8,128)} %copy-done.66, f32[8,2304]{1,0:T(8,128)} %copy-done.65, f32[8,2304]{1,0:T(8,128)} %copy-done.64, f32[8,2304]{1,0:T(8,128)} %copy-done.63, ...), dimensions={0} | concatenate | bytes 4829184
  1746.6 31.5 %concatenate.18 = f32[262,3072]{1,0:T(8,128)S(1)} concatenate(f32[6,3072]{1,0:T(8,128)S(1)} %collective-permute-done.95, f32[8,3072]{1,0:T(8,128)} %collective-permute-done.94, f32[8,3072]{1,0:T(8,128)} %copy-done.46, f32[8,3072]{1,0:T(8,128)} %copy-done.45, f32[8,3072]{1,0:T(8,128)} %copy-done.44, f32[8,3072]{1,0:T(8,128)} %copy-done.43, f32[8,3072]{1,0:T(8,128)} %copy-done.42, ...), dimensions={0} | concatenate | bytes 6438912
  (713 shorter events, 393.3 us)
Async XLA Ops:
  7.3 73.4 %all-gather.31.cloned.1.call-start = ((), (), s32[]{:S(2)}) async-start(), calls=%async_computation.7 | async-start | bytes 2377728 | tf_op jit(solution)/shard_map/all_gather | solution.py:419
  8.8 142.3 %all-gather.29.cloned.1.call-start = ((), (), s32[]{:S(2)}) async-start(), calls=%async_computation.6 | async-start | bytes 7133184 | tf_op jit(solution)/shard_map/all_gather | solution.py:419
  10.3 212.3 %all-gather.33.cloned.1.call-start = ((), (), s32[]{:S(2)}) async-start(), calls=%async_computation.8 | async-start | bytes 9510912 | tf_op jit(solution)/shard_map/all_gather | solution.py:419
  11.8 278.2 %all-gather.35.cloned.1.call-start = ((), (), s32[]{:S(2)}) async-start(), calls=%async_computation.9 | async-start | bytes 4755456 | tf_op jit(solution)/shard_map/all_gather | solution.py:419
  12.4 369.6 %all-gather.27.cloned.1.call-start = ((), (), s32[]{:S(2)}) async-start(), calls=%async_computation.4 | async-start | bytes 6488064 | tf_op jit(solution)/shard_map/all_gather | solution.py:345
  83.7 410.1 %all-gather.21.cloned.1.call-start = ((), (), s32[]{:S(2)}) async-start(), calls=%async_computation.1 | async-start | bytes 6488064 | tf_op jit(solution)/shard_map/all_gather | solution.py:251
  156.0 449.6 %all-gather.23.cloned.1.call-start = ((), (), s32[]{:S(2)}) async-start(), calls=%async_computation.2 | async-start | bytes 6488064 | tf_op jit(solution)/shard_map/all_gather | solution.py:252
  156.8 716.8 %all-gather.25.cloned.1.call-start = ((), (), s32[]{:S(2)}) async-start(), calls=%async_computation.3 | async-start | bytes 6488064 | tf_op jit(solution)/shard_map/all_gather | solution.py:344
  157.6 1621.2 %reduce-scatter.8.cloned.1.call-start = ((), (), s32[]{:S(2)}) async-start(), calls=%async_computation.5 | async-start | bytes 9510912 | tf_op jit(solution)/shard_map/reduce_scatter | solution.py:462
  1367.6 29.0 %collective-permute-start.40 = (f32[8,768]{1,0:T(8,128)S(1)}, f32[8,768]{1,0:T(8,128)S(1)}, u32[]{:S(2)}, u32[]{:S(2)}) collective-permute-start(f32[8,768]{1,0:T(8,128)S(1)} %get-tuple-element.1339), channel_id=1, source_target_pairs={{0,9},{1,10},{2,11},{3,12},{4,13},{5,14},{6,15},{7,16},{8,17},{9,1... | collective-permute-start | bytes 73736
  1368.9 36.4 %collective-permute-start.41 = (f32[8,768]{1,0:T(8,128)S(1)}, f32[8,768]{1,0:T(8,128)S(1)}, u32[]{:S(2)}, u32[]{:S(2)}) collective-permute-start(f32[8,768]{1,0:T(8,128)S(1)} %get-tuple-element.1339), channel_id=1, source_target_pairs={{0,10},{1,11},{2,12},{3,13},{4,14},{5,15},{6,16},{7,17},{8,18},{9,... | collective-permute-start | bytes 73736
  1381.3 33.1 %collective-permute-start.42 = (f32[8,768]{1,0:T(8,128)S(1)}, f32[8,768]{1,0:T(8,128)S(1)}, u32[]{:S(2)}, u32[]{:S(2)}) collective-permute-start(f32[8,768]{1,0:T(8,128)S(1)} %get-tuple-element.1339), channel_id=1, source_target_pairs={{0,11},{1,12},{2,13},{3,14},{4,15},{5,16},{6,17},{7,18},{8,19},{9,... | collective-permute-start | bytes 73736
  1384.2 35.0 %collective-permute-start.43 = (f32[8,768]{1,0:T(8,128)S(1)}, f32[8,768]{1,0:T(8,128)S(1)}, u32[]{:S(2)}, u32[]{:S(2)}) collective-permute-start(f32[8,768]{1,0:T(8,128)S(1)} %get-tuple-element.1339), channel_id=1, source_target_pairs={{0,12},{1,13},{2,14},{3,15},{4,16},{5,17},{6,18},{7,19},{8,20},{9,... | collective-permute-start | bytes 73736
  1385.6 35.6 %collective-permute-start.44 = (f32[8,768]{1,0:T(8,128)S(1)}, f32[8,768]{1,0:T(8,128)S(1)}, u32[]{:S(2)}, u32[]{:S(2)}) collective-permute-start(f32[8,768]{1,0:T(8,128)S(1)} %get-tuple-element.1339), channel_id=1, source_target_pairs={{0,13},{1,14},{2,15},{3,16},{4,17},{5,18},{6,19},{7,20},{8,21},{9,... | collective-permute-start | bytes 73736
  1396.6 26.2 %collective-permute-start.45 = (f32[8,768]{1,0:T(8,128)S(1)}, f32[8,768]{1,0:T(8,128)S(1)}, u32[]{:S(2)}, u32[]{:S(2)}) collective-permute-start(f32[8,768]{1,0:T(8,128)S(1)} %get-tuple-element.1339), channel_id=1, source_target_pairs={{0,14},{1,15},{2,16},{3,17},{4,18},{5,19},{6,20},{7,21},{8,22},{9,... | collective-permute-start | bytes 73736
  1451.1 21.6 %collective-permute-start.1 = (f32[8,2304]{1,0:T(8,128)S(1)}, f32[8,2304]{1,0:T(8,128)S(1)}, u32[]{:S(2)}, u32[]{:S(2)}) collective-permute-start(f32[8,2304]{1,0:T(8,128)S(1)} %get-tuple-element.1338), channel_id=1, source_target_pairs={{0,2},{1,3},{2,4},{3,5},{4,6},{5,7},{6,8},{7,9},{8,10},{9,11},{10,... | collective-permute-start | bytes 221192
  1491.0 74.5 %collective-permute-start.2 = (f32[8,2304]{1,0:T(8,128)S(1)}, f32[8,2304]{1,0:T(8,128)S(1)}, u32[]{:S(2)}, u32[]{:S(2)}) collective-permute-start(f32[8,2304]{1,0:T(8,128)S(1)} %get-tuple-element.1338), channel_id=1, source_target_pairs={{0,3},{1,4},{2,5},{3,6},{4,7},{5,8},{6,9},{7,10},{8,11},{9,12},{10... | collective-permute-start | bytes 221192
  1494.3 75.0 %collective-permute-start.20 = (f32[8,2304]{1,0:T(8,128)S(1)}, f32[8,2304]{1,0:T(8,128)S(1)}, u32[]{:S(2)}, u32[]{:S(2)}) collective-permute-start(f32[8,2304]{1,0:T(8,128)S(1)} %get-tuple-element.1338), channel_id=1, source_target_pairs={{0,21},{1,22},{2,23},{3,24},{4,25},{5,26},{6,27},{7,28},{8,29},{9,... | collective-permute-start | bytes 221192
  1497.1 74.7 %collective-permute-start.21 = (f32[8,2304]{1,0:T(8,128)S(1)}, f32[8,2304]{1,0:T(8,128)S(1)}, u32[]{:S(2)}, u32[]{:S(2)}) collective-permute-start(f32[8,2304]{1,0:T(8,128)S(1)} %get-tuple-element.1338), channel_id=1, source_target_pairs={{0,22},{1,23},{2,24},{3,25},{4,26},{5,27},{6,28},{7,29},{8,30},{9,... | collective-permute-start | bytes 221192
  1498.5 77.7 %collective-permute-start.22 = (f32[8,2304]{1,0:T(8,128)S(1)}, f32[8,2304]{1,0:T(8,128)S(1)}, u32[]{:S(2)}, u32[]{:S(2)}) collective-permute-start(f32[8,2304]{1,0:T(8,128)S(1)} %get-tuple-element.1338), channel_id=1, source_target_pairs={{0,23},{1,24},{2,25},{3,26},{4,27},{5,28},{6,29},{7,30},{8,31},{9,... | collective-permute-start | bytes 221192
  1499.8 80.7 %collective-permute-start.23 = (f32[8,2304]{1,0:T(8,128)S(1)}, f32[8,2304]{1,0:T(8,128)S(1)}, u32[]{:S(2)}, u32[]{:S(2)}) collective-permute-start(f32[8,2304]{1,0:T(8,128)S(1)} %get-tuple-element.1338), channel_id=1, source_target_pairs={{0,24},{1,25},{2,26},{3,27},{4,28},{5,29},{6,30},{7,31},{8,32},{9,... | collective-permute-start | bytes 221192
  1598.2 30.0 %collective-permute-start.64 = (f32[8,3072]{1,0:T(8,128)S(1)}, f32[8,3072]{1,0:T(8,128)S(1)}, u32[]{:S(2)}, u32[]{:S(2)}) collective-permute-start(f32[8,3072]{1,0:T(8,128)S(1)} %get-tuple-element.1340), channel_id=1, source_target_pairs={{0,1},{1,2},{2,3},{3,4},{4,5},{5,6},{6,7},{7,8},{8,9},{9,10},{10,1... | collective-permute-start | bytes 294920
  1658.0 36.0 %collective-permute-start.80 = (f32[8,3072]{1,0:T(8,128)S(1)}, f32[8,3072]{1,0:T(8,128)S(1)}, u32[]{:S(2)}, u32[]{:S(2)}) collective-permute-start(f32[8,3072]{1,0:T(8,128)S(1)} %get-tuple-element.1340), channel_id=1, source_target_pairs={{0,17},{1,18},{2,19},{3,20},{4,21},{5,22},{6,23},{7,24},{8,25},{9,... | collective-permute-start | bytes 294920
  1660.6 37.0 %collective-permute-start.81 = (f32[8,3072]{1,0:T(8,128)S(1)}, f32[8,3072]{1,0:T(8,128)S(1)}, u32[]{:S(2)}, u32[]{:S(2)}) collective-permute-start(f32[8,3072]{1,0:T(8,128)S(1)} %get-tuple-element.1340), channel_id=1, source_target_pairs={{0,18},{1,19},{2,20},{3,21},{4,22},{5,23},{6,24},{7,25},{8,26},{9,... | collective-permute-start | bytes 294920
  1662.4 36.4 %collective-permute-start.82 = (f32[8,3072]{1,0:T(8,128)S(1)}, f32[8,3072]{1,0:T(8,128)S(1)}, u32[]{:S(2)}, u32[]{:S(2)}) collective-permute-start(f32[8,3072]{1,0:T(8,128)S(1)} %get-tuple-element.1340), channel_id=1, source_target_pairs={{0,19},{1,20},{2,21},{3,22},{4,23},{5,24},{6,25},{7,26},{8,27},{9,... | collective-permute-start | bytes 294920
  1665.7 34.5 %collective-permute-start.83 = (f32[8,3072]{1,0:T(8,128)S(1)}, f32[8,3072]{1,0:T(8,128)S(1)}, u32[]{:S(2)}, u32[]{:S(2)}) collective-permute-start(f32[8,3072]{1,0:T(8,128)S(1)} %get-tuple-element.1340), channel_id=1, source_target_pairs={{0,20},{1,21},{2,22},{3,23},{4,24},{5,25},{6,26},{7,27},{8,28},{9,... | collective-permute-start | bytes 294920
  1667.9 33.6 %collective-permute-start.84 = (f32[8,3072]{1,0:T(8,128)S(1)}, f32[8,3072]{1,0:T(8,128)S(1)}, u32[]{:S(2)}, u32[]{:S(2)}) collective-permute-start(f32[8,3072]{1,0:T(8,128)S(1)} %get-tuple-element.1340), channel_id=1, source_target_pairs={{0,21},{1,22},{2,23},{3,24},{4,25},{5,26},{6,27},{7,28},{8,29},{9,... | collective-permute-start | bytes 294920
  1693.9 40.0 %collective-permute-start.85 = (f32[8,3072]{1,0:T(8,128)S(1)}, f32[8,3072]{1,0:T(8,128)S(1)}, u32[]{:S(2)}, u32[]{:S(2)}) collective-permute-start(f32[8,3072]{1,0:T(8,128)S(1)} %get-tuple-element.1340), channel_id=1, source_target_pairs={{0,22},{1,23},{2,24},{3,25},{4,26},{5,27},{6,28},{7,29},{8,30},{9,... | collective-permute-start | bytes 294920
  1697.5 38.1 %collective-permute-start.86 = (f32[8,3072]{1,0:T(8,128)S(1)}, f32[8,3072]{1,0:T(8,128)S(1)}, u32[]{:S(2)}, u32[]{:S(2)}) collective-permute-start(f32[8,3072]{1,0:T(8,128)S(1)} %get-tuple-element.1340), channel_id=1, source_target_pairs={{0,23},{1,24},{2,25},{3,26},{4,27},{5,28},{6,29},{7,30},{8,31},{9,... | collective-permute-start | bytes 294920
  1698.9 38.1 %collective-permute-start.87 = (f32[8,3072]{1,0:T(8,128)S(1)}, f32[8,3072]{1,0:T(8,128)S(1)}, u32[]{:S(2)}, u32[]{:S(2)}) collective-permute-start(f32[8,3072]{1,0:T(8,128)S(1)} %get-tuple-element.1340), channel_id=1, source_target_pairs={{0,24},{1,25},{2,26},{3,27},{4,28},{5,29},{6,30},{7,31},{8,32},{9,... | collective-permute-start | bytes 294920
  1700.2 38.1 %collective-permute-start.88 = (f32[8,3072]{1,0:T(8,128)S(1)}, f32[8,3072]{1,0:T(8,128)S(1)}, u32[]{:S(2)}, u32[]{:S(2)}) collective-permute-start(f32[8,3072]{1,0:T(8,128)S(1)} %get-tuple-element.1340), channel_id=1, source_target_pairs={{0,25},{1,26},{2,27},{3,28},{4,29},{5,30},{6,31},{7,32},{8,33},{9,... | collective-permute-start | bytes 294920
  1701.5 39.6 %collective-permute-start.89 = (f32[8,3072]{1,0:T(8,128)S(1)}, f32[8,3072]{1,0:T(8,128)S(1)}, u32[]{:S(2)}, u32[]{:S(2)}) collective-permute-start(f32[8,3072]{1,0:T(8,128)S(1)} %get-tuple-element.1340), channel_id=1, source_target_pairs={{0,26},{1,27},{2,28},{3,29},{4,30},{5,31},{6,32},{7,33},{8,34},{9,... | collective-permute-start | bytes 294920
  (227 other events, 9453.1 us)
Sparse Core Ops, SparseCore 0:
  11.6 68.9 all-gather.30
  84.2 66.7 all-gather.28
  154.6 67.9 all-gather.32
  225.5 64.5 all-gather.34
  293.5 88.5 all-gather.26
  384.7 109.1 all-gather.20
  496.6 109.0 all-gather.22
  608.4 109.6 all-gather.24
  723.7 213.4 reduce-scatter.7
where the time goes:
time: 1800 us; the launch traced here: 1790 us
  blocking collectives  766 us (43%)
  waiting for transfers between devices  480 us (27%)
  starting transfers between devices  257 us (14%)
  local copies, waits for them, and re-layouts  145 us (8%)
  matrix products  110 us (6%)
    unnamed x3, blocking collectives  516 us
    unnamed x96, starting transfers between devices  256 us
    all_gather x4, waiting for transfers between devices, body(): lax.all_gather(for_sending(shards_here), ('ctx', 'fsdp'), axis=0, tiled=T...  182 us
    all_gather x1, blocking collectives, backward_layer(): lax.all_gather(lse_rows, 'ctx', axis=1, tiled=True)  171 us
    all_gather x1, waiting for transfers between devices, forward_layer(): lax.all_gather(values_here, 'ctx', axis=0, tiled=True)  112 us
    all_gather x1, waiting for transfers between devices, forward_layer(): lax.all_gather(keys_here, 'ctx', axis=0, tiled=True)  103 us
    unnamed x287, local copies, waits for them, and re-layouts  95.8 us
    all_gather x1, waiting for transfers between devices, backward_layer(): lax.all_gather(grad_attended, 'ctx', axis=0, tiled=True)  81.2 us
  transfers between devices with their start and end apart: 105, of which 7 were waited for; matrix products, arithmetic and copies ran while one was open for 36% of the time, Pallas kernels for 0%

commit v1 on v0

v1 whole, which is shorter than its diff:
```python
import functools

import jax
import jax.numpy as jnp
import numpy as np
from jax import lax
from jax.experimental import pallas as pl
from jax.experimental.pallas import tpu as pltpu
from jax.sharding import PartitionSpec as P

F32 = jnp.float32
BF16 = jnp.bfloat16
MESH = pl.DeviceIdType.MESH
VMEM = pl.BlockSpec(memory_space=pltpu.VMEM)
HBM = pl.BlockSpec(memory_space=pl.ANY)
MIB = 1024 * 1024

UP, KV, Q, A = 768, 384, 256, 1408
B = 768
W = A + B


def place():
    ctx, fs = lax.axis_index("ctx"), lax.axis_index("fsdp")
    z, y, xh = ctx // 8, (ctx // 2) % 4, ctx % 2
    xl, c = fs // 2, fs % 2
    return z, y, xh, xl, c


def dev(z, y, x, c):
    return (z * 8 + y * 2 + x // 2, (x % 2) * 2 + c)


def rcopy(src, dst, ss, rs, to):
    return pltpu.make_async_remote_copy(
        src_ref=src, dst_ref=dst, send_sem=ss, recv_sem=rs, device_id=to, device_id_type=MESH
    )


def mm(a, b):
    return jnp.dot(a, b, preferred_element_type=F32)


def mm_nt(a, b):
    return lax.dot_general(a, b, (((1,), (1,)), ((), ())), preferred_element_type=F32)


def mm_tn(a, b):
    return lax.dot_general(a, b, (((0,), (0,)), ((), ())), preferred_element_type=F32)


def params(**kw):
    return pltpu.CompilerParams(vmem_limit_bytes=60 * MIB, **kw)


def gather_kernel(
    x_ref, g_ref, wz_ref, wb_ref, xa, ga, wa, zbuf, chunk,
    sw_s, sw_r, loc, tz_s, tz_r, wz_s, wz_r, s1_s, s2_s, s3_s, ring_r, part_r,
):
    z, y, xh, xl, c = place()
    x = xh * 2 + xl
    swap_to = dev(z, y, c * 2 + xl, xh)
    zpeer = [dev((z + k) % 4, y, x, c) for k in range(4)]
    first = [dev(z, (y + k * c) % 4, (x + k * (1 - c)) % 4, c) for k in range(4)]
    second = [dev(z, (y + k * (1 - c)) % 4, (x + k * c) % 4, c) for k in range(4)]
    partner = dev(z, y, x, 1 - c)

    def slot(k1, k2):
        yy = (y + k1 * c + k2 * (1 - c)) % 4
        xx = (x + k1 * (1 - c) + k2 * c) % 4
        return yy * 8 + xx * 2 + c

    bar = pltpu.get_barrier_semaphore()
    for to in zpeer[1:] + first[1:] + second[1:] + [partner]:
        pl.semaphore_signal(bar, inc=1, device_id=to, device_id_type=MESH)

    @pl.when(xh != c)
    def _():
        pl.semaphore_signal(bar, inc=1, device_id=swap_to, device_id_type=MESH)

    pl.semaphore_wait(bar, 10 + (xh + c) % 2)

    zs = [rcopy(wz_ref.at[(z + k) % 4], zbuf.at[z], wz_s.at[k], wz_r.at[(4 - k) % 4], zpeer[k]) for k in range(1, 4)]
    for d in zs:
        d.start()
    swaps = [rcopy(x_ref, xa.at[z], sw_s.at[0], sw_r.at[0], swap_to),
             rcopy(g_ref, ga.at[z], sw_s.at[1], sw_r.at[1], swap_to)]
    stays = [pltpu.make_async_copy(x_ref, xa.at[z], loc.at[0]), pltpu.make_async_copy(g_ref, ga.at[z], loc.at[1])]

    @pl.when(xh != c)
    def _():
        swaps[0].start()
        swaps[1].start()

    @pl.when(xh == c)
    def _():
        stays[0].start()
        stays[1].start()

    zbuf[z] = wz_ref[z]
    chunk[:, A:] = wb_ref[...]
    for d in zs:
        d.wait()
    chunk[:, :A] = zbuf[...].reshape(32, A).astype(BF16)

    me = slot(0, 0)
    own = pltpu.make_async_copy(chunk, wa.at[me], loc.at[2])
    own.start()
    sends = []

    def send(src, where, ss, rs, to):
        d = rcopy(src, wa.at[where], ss, rs, to)
        d.start()
        sends.append(d)

    for k in range(1, 4):
        send(chunk, me, s1_s.at[k], ring_r.at[4 - k, 0], first[k])
    for k in range(1, 4):
        send(chunk, me, s2_s.at[0, k], ring_r.at[0, 4 - k], second[k])
    send(chunk, me, s3_s.at[0, 0], part_r.at[0, 0], partner)

    toks = []
    for t, arr in enumerate((xa, ga)):

        @pl.when(xh != c)
        def _():
            swaps[t].wait()

        @pl.when(xh == c)
        def _():
            stays[t].wait()

        for k in range(1, 4):
            d = rcopy(arr.at[z], arr.at[z], tz_s.at[t, k], tz_r.at[t, 4 - k], zpeer[k])
            d.start()
            toks.append(d)

    def arrived(k1, k2, rs):
        p = slot(k1, k2)
        rcopy(wa.at[p], wa.at[p], s3_s.at[k1, k2], rs, partner).wait_recv()
        return p

    for k1 in range(1, 4):
        p = arrived(k1, 0, ring_r.at[k1, 0])
        for k in range(1, 4):
            send(wa.at[p], p, s2_s.at[k1, k], ring_r.at[k1, 4 - k], second[k])
        send(wa.at[p], p, s3_s.at[k1, 0], part_r.at[k1, 0], partner)
    for k2 in range(1, 4):
        for k1 in range(4):
            p = arrived(k1, k2, ring_r.at[k1, k2])
            send(wa.at[p], p, s3_s.at[k1, k2], part_r.at[k1, k2], partner)
    for k1 in range(4):
        for k2 in range(4):
            arrived(k1, k2, part_r.at[k1, k2])
    for d in toks:
        d.wait()
    for d in sends:
        d.wait_send()
    own.wait()


def gather_all(x, g, wz, wb):
    dma = pltpu.SemaphoreType.DMA
    tok = jax.ShapeDtypeStruct((4, 128, 768), BF16)
    return pl.pallas_call(
        gather_kernel,
        out_shape=(tok, tok, jax.ShapeDtypeStruct((32, 32, W), BF16)),
        in_specs=[HBM, HBM, VMEM, VMEM],
        out_specs=(HBM, HBM, HBM),
        scratch_shapes=[
            pltpu.VMEM((4, 8, A), F32), pltpu.VMEM((32, W), BF16),
            dma((2,)), dma((2,)), dma((3,)), dma((2, 4)), dma((2, 4)), dma((4,)), dma((4,)),
            dma((4,)), dma((4, 4)), dma((4, 4)), dma((4, 4)), dma((4, 4)),
        ],
        compiler_params=params(collective_id=0, has_side_effects=True),
        name="gather_tokens_weights",
    )(x, g, wz, wb)


def turn(tile, cos, plus, minus):
    return tile * cos + pltpu.roll(tile, 8, 1) * plus + pltpu.roll(tile, 120, 1) * minus


def lanes_below(n):
    return lax.broadcasted_iota(jnp.int32, (128, 128), 1) < n


def front_kernel(
    x_ref, g_ref, w_ref, s_ref, s3_ref, vec_ref, qb_ref, cos_ref, sp_ref, sm_ref,
    kv_ref, qd_ref, na_ref, nm_ref, xh_ref, ow_ref, dw_ref, xp, qkv, dof, owf, dwf,
):
    xp[...] = mm(x_ref[...], s_ref[...])
    lane = lax.broadcasted_iota(jnp.int32, (1, 1024), 1)
    real = jnp.where(lane % 8 < 6, 1.0, 0.0).astype(F32)

    @pl.loop(0, 8)
    def _(i):
        r = pl.ds(pl.multiple_of(i * 64, 64), 64)
        v = xp[r, :]
        mean = jnp.sum(v, axis=1, keepdims=True) * (1.0 / 768.0)
        cen = (v - mean) * real
        var = jnp.sum(cen * cen, axis=1, keepdims=True) * (1.0 / 768.0)
        xh = cen * lax.rsqrt(var + 1e-5)
        xh_ref[r, :] = xh
        na_ref[r, :] = (xh * vec_ref[0:1, :] + vec_ref[1:2, :]).astype(BF16)
        nm_ref[r, :] = (xh * vec_ref[2:3, :] + vec_ref[3:4, :]).astype(BF16)

    qkv[...] = mm(na_ref[...], w_ref[:, :, UP:A].reshape(1024, A - UP)) + qb_ref[0:1, :]

    @pl.loop(0, 32)
    def _(p):
        rows = w_ref[p, :, A:].astype(F32)
        dwf[pl.ds(pl.multiple_of(p * 24, 8), 24), :] = rows[:24]
        owf[pl.ds(pl.multiple_of(p * 8, 8), 8), :] = rows[24:]

    ow_ref[...] = owf[...].astype(BF16)
    dw_ref[...] = dwf[...].astype(BF16)
    dof[...] = mm_nt(g_ref[...], ow_ref[...]).astype(BF16)
    for h in range(3):
        qd_ref[h, 512:, :] = mm_nt(dof[...], s3_ref[h]).astype(BF16)

    @pl.loop(0, 4)
    def _(i):
        r = pl.ds(pl.multiple_of(i * 128, 128), 128)
        cos, plus, minus = cos_ref[r, :], sp_ref[r, :], sm_ref[r, :]
        low = lanes_below(64)
        kc, kp, km = jnp.where(low, cos, 1.0), jnp.where(low, plus, 0.0), jnp.where(low, minus, 0.0)
        for h in range(3):
            kv_ref[h, r, :] = turn(qkv[r, 128 * h : 128 * h + 128], kc, kp, km).astype(BF16)
        q01 = turn(qkv[r, 384:512], cos, plus, minus).astype(BF16).astype(F32) * 0.125
        q2 = turn(qkv[r, 512:640], cos, plus, minus).astype(BF16).astype(F32) * 0.125
        qd_ref[0, r, :] = jnp.where(low, q01, 0.0).astype(BF16)
        qd_ref[1, r, :] = jnp.where(low, pltpu.roll(q01, 64, 1), 0.0).astype(BF16)
        qd_ref[2, r, :] = jnp.where(low, q2, 0.0).astype(BF16)


def front(x, g, w, s, s3, vec, qb, cos, plus, minus):
    sh = jax.ShapeDtypeStruct
    return pl.pallas_call(
        front_kernel,
        out_shape=(
            sh((3, 512, 128), BF16), sh((3, 1024, 128), BF16), sh((512, 1024), BF16), sh((512, 1024), BF16),
            sh((512, 1024), F32), sh((256, 768), BF16), sh((768, 768), BF16),
        ),
        in_specs=[VMEM] * 10,
        out_specs=(VMEM,) * 7,
        scratch_shapes=[
            pltpu.VMEM((512, 1024), F32), pltpu.VMEM((512, 640), F32), pltpu.VMEM((512, 256), BF16),
            pltpu.VMEM((256, 768), F32), pltpu.VMEM((768, 768), F32),
        ],
        compiler_params=params(),
        name="norms_qkv",
    )(x, g, w, s, s3, vec, qb, cos, plus, minus)


def mlp_kernel(
    nm_ref, g_ref, w_ref, dw_ref, xh_ref, vec_ref, ub_ref,
    part_ref, dxh_ref, gs_ref, dub_ref, dwup_ref, dwd_ref, up, hid, du,
):
    wup = w_ref[:, :, :UP].reshape(1024, UP)
    up[...] = mm(nm_ref[...], wup) + ub_ref[0:1, :]
    gs_ref[...] = jnp.zeros((8, 1024), F32)
    dub_ref[...] = jnp.zeros((8, UP), F32)

    @pl.loop(0, 8)
    def _(i):
        r = pl.ds(pl.multiple_of(i * 64, 64), 64)
        u = up[r, :]
        cdf = 0.5 * (1.0 + lax.erf(u * np.float32(np.sqrt(0.5))))
        pdf = jnp.exp(-0.5 * u * u) * np.float32(1.0 / np.sqrt(2.0 * np.pi))
        hid[r, :] = (u * cdf).astype(BF16)
        up[r, :] = cdf + u * pdf

    part_ref[...] = mm(hid[...], dw_ref[...])

    @pl.loop(0, 4)
    def _(i):
        r = pl.ds(pl.multiple_of(i * 128, 128), 128)
        d = (mm_nt(g_ref[r, :], dw_ref[...]) * up[r, :]).astype(BF16)
        du[r, :] = d
        dub_ref[0:1, :] += jnp.sum(d.astype(F32), axis=0, keepdims=True)

    @pl.loop(0, 4)
    def _(i):
        r = pl.ds(pl.multiple_of(i * 128, 128), 128)
        dn = mm_nt(du[r, :], wup)
        gs_ref[0:1, :] += jnp.sum(dn * xh_ref[r, :], axis=0, keepdims=True)
        gs_ref[1:2, :] += jnp.sum(dn, axis=0, keepdims=True)
        dxh_ref[r, :] = dn * vec_ref[2:3, :]

    dwup_ref[...] = mm_tn(nm_ref[...], du[...]).astype(BF16)
    dwd_ref[...] = mm_tn(hid[...], g_ref[...])


def mlp(nm, g, w, dw, xh, vec, ub):
    sh = jax.ShapeDtypeStruct
    return pl.pallas_call(
        mlp_kernel,
        out_shape=(
            sh((512, 768), F32), sh((512, 1024), F32), sh((8, 1024), F32), sh((8, UP), F32),
            sh((1024, UP), BF16), sh((768, 768), F32),
        ),
        in_specs=[VMEM] * 7,
        out_specs=(VMEM,) * 6,
        scratch_shapes=[pltpu.VMEM((512, UP), F32), pltpu.VMEM((512, UP), BF16), pltpu.VMEM((512, UP), BF16)],
        compiler_params=params(),
        name="feed_forward",
    )(nm, g, w, dw, xh, vec, ub)


def kv_kernel(kv_ref, out, loc, y_s, y_r, p_s, p_r):
    z, y, xh, xl, c = place()
    x = xh * 2 + xl
    peer = [dev(z, (y + k) % 4, x, c) for k in range(4)]
    partner = dev(z, y, x, 1 - c)
    bar = pltpu.get_barrier_semaphore()
    for to in peer[1:] + [partner]:
        pl.semaphore_signal(bar, inc=1, device_id=to, device_id_type=MESH)
    pl.semaphore_wait(bar, 4)
    me = out.at[:, :, 2 * y + c]
    sends = [rcopy(kv_ref, me, y_s.at[k], y_r.at[4 - k], peer[k]) for k in range(1, 4)]
    sends.append(rcopy(kv_ref, me, p_s.at[0], p_r.at[0], partner))
    for d in sends:
        d.start()
    own = pltpu.make_async_copy(kv_ref, me, loc.at[0])
    own.start()
    for k in (1, 3, 2):
        there = out.at[:, :, 2 * ((y + k) % 4) + c]
        rcopy(there, there, y_s.at[k], y_r.at[k], peer[k]).wait_recv()
        d = rcopy(there, there, p_s.at[k], p_r.at[k], partner)
        d.start()
        sends.append(d)
    for k in range(4):
        there = out.at[:, :, 2 * ((y + k) % 4) + 1 - c]
        rcopy(there, there, p_s.at[k], p_r.at[k], partner).wait_recv()
    for d in sends:
        d.wait_send()
    own.wait()


def gather_kv(kv):
    dma = pltpu.SemaphoreType.DMA
    return pl.pallas_call(
        kv_kernel,
        out_shape=jax.ShapeDtypeStruct((3, 4, 8, 128, 128), BF16),
        in_specs=[HBM],
        out_specs=HBM,
        scratch_shapes=[dma((1,)), dma((4,)), dma((4,)), dma((4,)), dma((4,))],
        compiler_params=params(collective_id=1, has_side_effects=True),
        name="gather_keys_values",
    )(kv)


def attention_kernel(qd_ref, kv_ref, o_ref, dq_ref, dkv_ref, s_scr, top, tot, acc, delta):
    z, y, xh, xl, c = place()
    start = (2 * y + c) * 128
    row = start + lax.broadcasted_iota(jnp.int32, (128, 256), 0)
    key = lax.broadcasted_iota(jnp.int32, (128, 256), 1)

    def chunks(body):
        for j in range(4):

            @pl.loop(0, 4)
            def _(t):
                body(j, 128 * j, t, pl.ds(pl.multiple_of(1024 * j + t * 256, 256), 256))

    def twice(a):
        return jnp.concatenate([a, a], axis=1)

    @pl.loop(0, 3)
    def _(h):
        top[...] = jnp.full((512, 128), -1e30, F32)
        tot[...] = jnp.zeros((512, 128), F32)
        acc[...] = jnp.zeros((512, 128), F32)

        def scores(j, r0, t, keys):
            s = mm_nt(qd_ref[h, r0:512, :], kv_ref[h, keys, :])
            head = jnp.where(key + t * 256 <= row, s[:128], -1e30)
            s_scr[r0 : r0 + 128, keys] = head
            top[r0 : r0 + 128, :] = jnp.maximum(top[r0 : r0 + 128, :], jnp.maximum(head[:, :128], head[:, 128:]))
            if j < 3:
                rest = s[128:]
                s_scr[r0 + 128 :, keys] = rest
                top[r0 + 128 :, :] = jnp.maximum(top[r0 + 128 :, :], jnp.maximum(rest[:, :128], rest[:, 128:]))

        chunks(scores)
        top[...] = jnp.broadcast_to(jnp.max(top[...], axis=1, keepdims=True), (512, 128))

        def weigh(j, r0, t, keys):
            p = jnp.exp(s_scr[r0:, keys] - twice(top[r0:, :]))
            s_scr[r0:, keys] = p
            tot[r0:, :] += p[:, :128] + p[:, 128:]
            acc[r0:, :] += mm(p.astype(BF16), kv_ref[h, keys, :])

        chunks(weigh)
        inv = 1.0 / jnp.broadcast_to(jnp.sum(tot[...], axis=1, keepdims=True), (512, 128))
        tot[...] = inv
        att = acc[...] * inv
        o_ref[h] = att.astype(BF16)
        delta[...] = jnp.broadcast_to(
            jnp.sum(att * qd_ref[h, 512:, :].astype(F32), axis=1, keepdims=True), (512, 128)
        )
        acc[...] = jnp.zeros((512, 128), F32)

        def back(j, r0, t, keys):
            kv = kv_ref[h, keys, :]
            p = s_scr[r0:, keys] * twice(tot[r0:, :])
            dp = mm_nt(qd_ref[h, 512 + r0 :, :], kv)
            ds = (p * (dp - twice(delta[r0:, :]))).astype(BF16)
            acc[r0:, :] += mm(ds, kv)
            d = mm_tn(qd_ref[h, r0:512, :], ds) + mm_tn(qd_ref[h, 512 + r0 :, :], p.astype(BF16))
            dkv_ref[8 * j + 2 * t, h] = d[:, :128].astype(BF16)
            dkv_ref[8 * j + 2 * t + 1, h] = d[:, 128:].astype(BF16)

        chunks(back)
        dq_ref[h] = acc[...]


def attention(qd, kv):
    sh = jax.ShapeDtypeStruct
    return pl.pallas_call(
        attention_kernel,
        out_shape=(sh((3, 512, 128), BF16), sh((3, 512, 128), F32), sh((32, 3, 128, 128), BF16)),
        in_specs=[VMEM] * 2,
        out_specs=(VMEM,) * 3,
        scratch_shapes=[pltpu.VMEM((512, 4096), F32)] + [pltpu.VMEM((512, 128), F32)] * 4,
        compiler_params=params(),
        name="attention",
    )(qd, kv)


def dkv_kernel(dkv, out, buf1, buf2, pair, p_s, p_r, y_s, y_r):
    z, y, xh, xl, c = place()
    x = xh * 2 + xl
    peer = [dev(z, (y + k) % 4, x, c) for k in range(4)]
    partner = dev(z, y, x, 1 - c)
    bar = pltpu.get_barrier_semaphore()
    for to in peer[1:] + [partner]:
        pl.semaphore_signal(bar, inc=1, device_id=to, device_id_type=MESH)
    pl.semaphore_wait(bar, 4)
    order = (2, 1, 3, 0)
    halves = [rcopy(dkv.at[:, (y + k) % 4, 1 - c], buf1.at[k], p_s.at[k], p_r.at[k], partner) for k in range(4)]
    for k in order:
        halves[k].start()
    sends = []
    for k in order:
        halves[k].wait_recv()
        yy = (y + k) % 4

        @pl.loop(0, 4)
        def _(i):
            pair[k, i] = (dkv[i, yy, c].astype(F32) + buf1[k, i].astype(F32)).astype(BF16)

        if k:
            d = rcopy(pair.at[k], buf2.at[4 - k], y_s.at[k], y_r.at[4 - k], peer[k])
            d.start()
            sends.append(d)
    for k in range(1, 4):
        rcopy(pair.at[k], buf2.at[k], y_s.at[k], y_r.at[k], peer[k]).wait_recv()

    @pl.loop(0, 4)
    def _(i):
        out[i] = pair[0, i].astype(F32) + buf2[1, i].astype(F32) + buf2[2, i].astype(F32) + buf2[3, i].astype(F32)

    for d in halves + sends:
        d.wait_send()


def sum_dkv(dkv):
    dma = pltpu.SemaphoreType.DMA
    buf = pltpu.VMEM((4, 4, 3, 128, 128), BF16)
    return pl.pallas_call(
        dkv_kernel,
        out_shape=jax.ShapeDtypeStruct((4, 3, 128, 128), F32),
        in_specs=[VMEM],
        out_specs=VMEM,
        scratch_shapes=[buf, buf, buf, dma((4,)), dma((4,)), dma((4,)), dma((4,))],
        compiler_params=params(collective_id=2, has_side_effects=True),
        name="sum_key_value_grads",
    )(dkv)


def back_kernel(
    o_ref, dq_ref, dkv_ref, na_ref, xh_ref, g_ref, w_ref, ow_ref, part_ref, dxm_ref, dwd_ref, s_ref, s3_ref,
    vec_ref, ob_ref, cos_ref, sp_ref, sm_ref,
    outp_ref, dxp_ref, dwq_ref, dwb_ref, gs_ref, dqb_ref, dqkv, dxh, att, dwo,
):
    dqb_ref[...] = jnp.zeros((8, 640), F32)
    gs_ref[...] = jnp.zeros((8, 1024), F32)

    @pl.loop(0, 4)
    def _(i):
        r = pl.ds(pl.multiple_of(i * 128, 128), 128)
        cos, plus, minus = cos_ref[r, :], -sp_ref[r, :], -sm_ref[r, :]
        low = lanes_below(64)
        kc, kp, km = jnp.where(low, cos, 1.0), jnp.where(low, plus, 0.0), jnp.where(low, minus, 0.0)
        for h in range(3):
            dqkv[r, 128 * h : 128 * h + 128] = turn(dkv_ref[i, h].T, kc, kp, km).astype(BF16)
        d0, d1, d2 = dq_ref[0, r, :] * 0.125, dq_ref[1, r, :] * 0.125, dq_ref[2, r, :] * 0.125
        d01 = jnp.where(low, d0, pltpu.roll(d1, 64, 1))
        dqkv[r, 384:512] = turn(d01, cos, plus, minus).astype(BF16)
        dqkv[r, 512:640] = turn(jnp.where(low, d2, 0.0), cos, plus, minus).astype(BF16)
        dqb_ref[0:1, :] += jnp.sum(dqkv[r, :].astype(F32), axis=0, keepdims=True)

    wq = w_ref[:, :, UP:A].reshape(1024, A - UP)

    @pl.loop(0, 4)
    def _(i):
        r = pl.ds(pl.multiple_of(i * 128, 128), 128)
        dn = mm_nt(dqkv[r, :], wq)
        gs_ref[0:1, :] += jnp.sum(dn * xh_ref[r, :], axis=0, keepdims=True)
        gs_ref[1:2, :] += jnp.sum(dn, axis=0, keepdims=True)
        dxh[r, :] = (dxm_ref[r, :] + dn * vec_ref[0:1, :]).astype(BF16)

    dxp_ref[...] = mm_nt(dxh[...], s_ref[...]).astype(BF16)
    dwq_ref[...] = mm_tn(na_ref[...], dqkv[...]).astype(BF16)
    att[...] = (mm(o_ref[0], s3_ref[0]) + mm(o_ref[1], s3_ref[1]) + mm(o_ref[2], s3_ref[2])).astype(BF16)
    outp_ref[...] = (part_ref[...] + mm(att[...], ow_ref[...]) + ob_ref[0:1, :]).astype(BF16)
    dwo[...] = mm_tn(att[...], g_ref[...])

    @pl.loop(0, 32)
    def _(p):
        rows = jnp.concatenate(
            [dwd_ref[pl.ds(pl.multiple_of(p * 24, 8), 24), :], dwo[pl.ds(pl.multiple_of(p * 8, 8), 8), :]], axis=0
        )
        dwb_ref[p] = rows.astype(BF16)


def back(*args):
    sh = jax.ShapeDtypeStruct
    return pl.pallas_call(
        back_kernel,
        out_shape=(
            sh((512, 768), BF16), sh((512, 768), BF16), sh((1024, 640), BF16), sh((32, 32, 768), BF16),
            sh((8, 1024), F32), sh((8, 640), F32),
        ),
        in_specs=[VMEM] * 18,
        out_specs=(VMEM,) * 6,
        scratch_shapes=[
            pltpu.VMEM((512, 640), BF16), pltpu.VMEM((512, 1024), BF16), pltpu.VMEM((512, 256), BF16),
            pltpu.VMEM((256, 768), F32),
        ],
        compiler_params=params(),
        name="backward",
    )(*args)


def sum_kernel(
    outp, dxp, dwup, dwq, dwb, small, ro, rd, ga, gb, pk, buf1, pair, buf2, quad, buf3, fin,
    t_s, t_r, loc, s1_s, s1_r, s2_s, s2_r, s3_s, s3_r, z_s, z_r,
):
    z, y, xh, xl, c = place()
    x = xh * 2 + xl
    zpeer = [dev((z + k) % 4, y, x, c) for k in range(4)]
    home = [dev((z + k) % 4, y, c * 2 + xl, xh) for k in range(4)]
    first = [dev(z, (y + k * (1 - c)) % 4, (x + k * c) % 4, c) for k in range(4)]
    second = [dev(z, (y + k * c) % 4, (x + k * (1 - c)) % 4, c) for k in range(4)]
    partner = dev(z, y, x, 1 - c)

    def slot(k1, k2, cc):
        yy = (y + k1 * (1 - cc) + k2 * cc) % 4
        xx = (x + k1 * cc + k2 * (1 - cc)) % 4
        return yy * 8 + xx * 2 + cc

    bar = pltpu.get_barrier_semaphore()
    for to in zpeer[1:] + first[1:] + second[1:] + [partner]:
        pl.semaphore_signal(bar, inc=1, device_id=to, device_id_type=MESH)

    @pl.when(xh != c)
    def _():
        for to in home:
            pl.semaphore_signal(bar, inc=1, device_id=to, device_id_type=MESH)

    pl.semaphore_wait(bar, 10 + 4 * ((xh + c) % 2))

    toks, stays = [], []
    for t, (src, dst) in enumerate(((outp, ro), (dxp, rd))):
        for k in range(4):
            toks.append(rcopy(src.at[(z + k) % 4], dst.at[z], t_s.at[t, k], t_r.at[t, k], home[k]))
        stays.append(pltpu.make_async_copy(src.at[z], dst.at[z], loc.at[t]))
    for i in (1, 2, 3, 5, 6, 7):
        toks[i].start()

    @pl.when(xh != c)
    def _():
        toks[0].start()
        toks[4].start()

    @pl.when(xh == c)
    def _():
        stays[0].start()
        stays[1].start()

    @pl.loop(0, 32)
    def _(p):
        r = pl.ds(pl.multiple_of(p * 32, 32), 32)
        pk[p, :, :128] = dwup[r, :128] + small[p]
        pk[p, :, 128:UP] = dwup[r, 128:]
        pk[p, :, UP:A] = dwq[r, :]
        pk[p, :, A:] = dwb[p]

    order = [(k1, k2) for k1 in (2, 1, 3, 0) for k2 in (2, 1, 3, 0)]
    sends = []
    for k1, k2 in order:
        d = rcopy(pk.at[slot(k1, k2, 1 - c)], buf1.at[k1, k2], s1_s.at[k1, k2], s1_r.at[k1, k2], partner)
        d.start()
        sends.append(d)
    for k1, k2 in order:
        mine = slot(k1, k2, c)
        rcopy(pk.at[mine], buf1.at[k1, k2], s1_s.at[k1, k2], s1_r.at[k1, k2], partner).wait_recv()
        pair[k1, k2] = (pk[mine].astype(F32) + buf1[k1, k2].astype(F32)).astype(BF16)
        if k1:
            d = rcopy(pair.at[k1, k2], buf2.at[4 - k1, k2], s2_s.at[k1, k2], s2_r.at[4 - k1, k2], first[k1])
            d.start()
            sends.append(d)
    for k2 in (2, 1, 3, 0):
        for k1 in range(1, 4):
            rcopy(pair.at[k1, k2], buf2.at[k1, k2], s2_s.at[k1, k2], s2_r.at[k1, k2], partner).wait_recv()
        total = (
            pair[0, k2].astype(F32) + buf2[1, k2].astype(F32) + buf2[2, k2].astype(F32) + buf2[3, k2].astype(F32)
        )
        if k2:
            quad[k2] = total.astype(BF16)
            d = rcopy(quad.at[k2], buf3.at[4 - k2], s3_s.at[k2], s3_r.at[4 - k2], second[k2])
            d.start()
            sends.append(d)
        else:
            fin[...] = total.reshape(4, 8, W)
    for k in range(1, 4):
        rcopy(quad.at[k], buf3.at[k], s3_s.at[k], s3_r.at[k], partner).wait_recv()
    total = fin[...].reshape(32, W) + buf3[1].astype(F32) + buf3[2].astype(F32) + buf3[3].astype(F32)
    fin[...] = total.reshape(4, 8, W)
    gb[...] = total[:, A:]
    zsends = []
    for k in range(1, 4):
        zz = (z + k) % 4
        d = rcopy(fin.at[zz, :, :A], ga.at[z], z_s.at[k], z_r.at[4 - k], zpeer[k])
        d.start()
        zsends.append(d)
    ga[z] = fin[z, :, :A]
    for d in zsends:
        d.wait()
    for i in (1, 2, 3, 5, 6, 7):
        toks[i].wait()

    @pl.when(xh != c)
    def _():
        toks[0].wait()
        toks[4].wait()

    @pl.when(xh == c)
    def _():
        stays[0].wait()
        stays[1].wait()

    for d in sends:
        d.wait_send()


def sum_all(outp, dxp, dwup, dwq, dwb, small):
    dma = pltpu.SemaphoreType.DMA
    sh = jax.ShapeDtypeStruct
    big = pltpu.VMEM((4, 4, 32, W), BF16)
    row = pltpu.VMEM((4, 32, W), BF16)
    tok = sh((4, 128, 768), BF16)
    return pl.pallas_call(
        sum_kernel,
        out_shape=(tok, tok, sh((4, 8, A), F32), sh((32, B), F32)),
        in_specs=[HBM, HBM, VMEM, VMEM, VMEM, VMEM],
        out_specs=(HBM, HBM, VMEM, VMEM),
        scratch_shapes=[
            pltpu.VMEM((32, 32, W), BF16), big, big, big, row, row, pltpu.VMEM((4, 8, W), F32),
            dma((2, 4)), dma((2, 4)), dma((2,)), dma((4, 4)), dma((4, 4)), dma((4, 4)), dma((4, 4)),
            dma((4,)), dma((4,)), dma((4,)), dma((4,)),
        ],
        compiler_params=params(collective_id=3, has_side_effects=True),
        name="sum_weight_grads",
    )(outp, dxp, dwup, dwq, dwb, small)


def permutations():
    j = np.arange(1024)
    nat = 192 * ((j // 8) % 4) + 6 * (j // 32) + j % 8
    s = (np.arange(768)[:, None] == nat[None, :]) & (j % 8 < 6)[None, :]
    i = np.arange(256)
    nat8 = 6 * (i // 8) + i % 8
    s3 = np.zeros((3, 128, 256), bool)
    for h in range(3):
        s3[h, 64:] = ((64 * h + np.arange(64))[:, None] == nat8[None, :]) & (i % 8 < 6)[None, :]
    return jnp.asarray(s, BF16), jnp.asarray(s3, BF16)


def rotary(first_block):
    f = 10000.0 ** (-2.0 * jnp.arange(8, dtype=F32) / 16)
    lane = np.arange(128) % 64
    freq = jnp.where(lane < 16, jnp.tile(f, 16), 0.0)
    pos = (first_block * 128 + 1024 * jnp.arange(4)[:, None] + jnp.arange(128)[None, :]).reshape(512).astype(F32)
    angle = pos[:, None] * freq[None, :]
    sin = jnp.sin(angle)
    return jnp.cos(angle), jnp.where(lane >= 8, sin, 0.0), jnp.where(lane < 8, -sin, 0.0)


def body(
    inputs, qkv_weight, qkv_bias, out_weight, out_bias, up_weight, up_bias, down_weight, down_bias,
    attn_gain, attn_shift, mlp_gain, mlp_shift, cotangent,
):
    z, y, xh, xl, c = place()
    x, g = inputs[0], cotangent[0]
    qkv5 = qkv_weight[0].reshape(6, 3, 4, 3, 64)
    kv_cols = jnp.stack([qkv5[:, 1], qkv5[:, 2]], axis=3).reshape(6, 4, KV)
    q_cols = qkv5[:, 0].reshape(6, 4, 192)
    rows = jnp.concatenate(
        [up_weight[0].reshape(6, 4, UP), kv_cols, q_cols, jnp.zeros((6, 4, 64), BF16)], axis=-1
    ).astype(F32)
    vectors = (qkv_bias, out_bias, up_bias, down_bias, attn_gain, attn_shift, mlp_gain, mlp_shift)
    mine = jnp.concatenate([v[0] for v in vectors] + [jnp.zeros((A - 78,), BF16)]).astype(F32)
    wz = jnp.concatenate(
        [rows.transpose(1, 0, 2), jnp.broadcast_to(mine, (4, 1, A)), jnp.zeros((4, 1, A), F32)], axis=1
    )
    wb = jnp.concatenate([down_weight[0], out_weight[0], jnp.zeros((2, 768), BF16)], axis=0)
    xa, ga, w = gather_all(x, g, wz, wb)
    xa, ga = xa.reshape(512, 768), ga.reshape(512, 768)

    rows = w.reshape(32, 4, 8, W)[:, :, 6, :128].astype(F32)

    def padded(at):
        return jnp.pad(rows[:, :, at : at + 6], ((0, 0), (0, 0), (0, 2))).reshape(1024)

    vec = jnp.stack([padded(54), padded(60), padded(66), padded(72)] + [jnp.zeros((1024,), F32)] * 4)
    whole = rows.transpose(1, 0, 2).reshape(128, 128)
    qb = lax.dynamic_index_in_dim(whole[:, :18].reshape(3, 4, 192), z, 1, False)
    kvb = jnp.stack([qb[1].reshape(3, 64), qb[2].reshape(3, 64)], axis=1).reshape(KV)
    qb = jnp.broadcast_to(jnp.concatenate([kvb, qb[0], jnp.zeros((64,), F32)])[None], (8, 640))
    ub = lax.dynamic_index_in_dim(whole[:, 24:48].reshape(4, UP), z, 0, True)
    ub = jnp.broadcast_to(ub, (8, UP))
    ob = (whole[:, 18:24] + whole[:, 48:54]).reshape(1, 768) * jnp.where(z == 0, 1.0, 0.0)
    ob = jnp.broadcast_to(ob, (8, 768))

    s, s3 = permutations()
    cos, plus, minus = rotary(2 * y + c)
    kv, qd, na, nm, xhat, ow, dw = front(xa, ga, w, s, s3, vec, qb, cos, plus, minus)
    kv_all = gather_kv(kv.reshape(3, 4, 128, 128)).reshape(3, 4096, 128)
    part, dxm, gs_m, dub, dwup, dwd = mlp(nm, ga, w, dw, xhat, vec, ub)
    o, dq, dkv = attention(qd, kv_all)
    dkv = sum_dkv(dkv.reshape(4, 4, 2, 3, 128, 128))
    outp, dxp, dwq, dwb, gs_a, dqb = back(
        o, dq, dkv, na, xhat, ga, w, ow, part, dxm, dwd, s, s3, vec, ob, cos, plus, minus
    )

    here = jnp.where(jnp.arange(4) == z, 1.0, 0.0).astype(F32)
    kvg = dqb[0, :KV].reshape(3, 2, 64)
    qkvg = jnp.stack([dqb[0, KV : KV + 192], kvg[:, 0].reshape(192), kvg[:, 1].reshape(192)])
    qkvg = (qkvg[:, None, :] * here[None, :, None]).reshape(128, 18)
    obg = jnp.sum(g.astype(F32), axis=0).reshape(128, 6)
    ubg = (dub[0:1] * here[:, None]).reshape(128, 24)
    by_dev = jnp.concatenate([qkvg, obg, ubg, obg], axis=1).reshape(4, 32, 54).transpose(1, 0, 2)
    norms = [v.reshape(32, 4, 8)[:, :, :6] for v in (gs_a[0], gs_a[1], gs_m[0], gs_m[1])]
    small = jnp.concatenate([by_dev] + norms + [jnp.zeros((32, 4, 50), F32)], axis=-1)
    small = jnp.pad(small[:, :, None, :], ((0, 0), (0, 0), (6, 1), (0, 0))).reshape(32, 32, 128).astype(BF16)
    ro, rd, grad_a, grad_b = sum_all(
        outp.reshape(4, 128, 768), dxp.reshape(4, 128, 768), dwup, dwq, dwb, small
    )

    xf, gf = x.astype(F32), g.astype(F32)
    outputs = (xf + jnp.sum(ro.astype(F32), axis=0)).astype(BF16)
    dxh = jnp.sum(rd.astype(F32), axis=0)
    cen = xf - jnp.mean(xf, axis=-1, keepdims=True)
    rstd = lax.rsqrt(jnp.mean(cen * cen, axis=-1, keepdims=True) + 1e-5)
    xn = cen * rstd
    dx = rstd * (dxh - jnp.mean(dxh, axis=-1, keepdims=True) - xn * jnp.mean(dxh * xn, axis=-1, keepdims=True))
    input_grad = gf + dx

    up_grad = grad_a[:, :6, :UP].transpose(1, 0, 2).reshape(6, 3072)
    kvg = grad_a[:, :6, UP : UP + KV].reshape(4, 6, 3, 2, 64).transpose(1, 3, 0, 2, 4).reshape(6, 2, 768)
    qg = grad_a[:, :6, UP + KV : UP + KV + 192].transpose(1, 0, 2).reshape(6, 1, 768)
    qkv_grad = jnp.concatenate([qg, kvg], axis=1).reshape(6, 2304)
    tiny = jnp.sum(grad_a[:, 6, :128], axis=0)
    cuts = np.cumsum([0, 18, 6, 24, 6, 6, 6, 6, 6])
    t = [tiny[a:b][None] for a, b in zip(cuts[:-1], cuts[1:])]
    return (
        outputs[None], input_grad[None], qkv_grad[None], t[0], grad_b[24:30][None], t[1], up_grad[None], t[2],
        grad_b[:24][None], t[3], t[4], t[5], t[6], t[7],
    )


def solution(mesh):
    tok = P("fsdp", "ctx", None)
    mat = P(None, ("ctx", "fsdp"), None)
    row = P(None, ("ctx", "fsdp"))
    in_specs = (tok, mat, row, mat, row, mat, row, mat, row, row, row, row, row, tok)
    out_specs = (tok, tok, mat, row, mat, row, mat, row, mat, row, row, row, row, row)
    return jax.shard_map(body, mesh=mesh, in_specs=in_specs, out_specs=out_specs, check_vma=False)
```

time: 1800 us -> 254 us (0.14)
  blocking collectives: 766 us -> 0 us
  waiting for transfers between devices: 480 us -> 0 us
  starting transfers between devices: 257 us -> 0 us
  Pallas kernels: 0 us -> 221 us
  local copies, waits for them, and re-layouts: 145 us -> 21.9 us
  matrix products: 110 us -> 0 us
    unnamed x3 -> x0, blocking collectives: 516 us -> none
    all_gather x8 -> x0, waiting for transfers between devices: 477 us -> none  [the longest x4 182 us: body(): lax.all_gather(for_sending(shards_here), ('ctx', 'fsdp'), axis=0, tiled=T...]
    unnamed x96 -> x0, starting transfers between devices: 256 us -> none
    all_gather x2 -> x0, blocking collectives: 251 us -> none  [the longest x1 171 us: backward_layer(): lax.all_gather(lse_rows, 'ctx', axis=1, tiled=True)]
    pallas_call x0 -> x8, Pallas kernels: none -> 221 us  [the longest x1 47 us: sum_all(): pl.pallas_call(sum_kernel, out_shape=(tok, tok, sh((4, 8, A), F32), sh((3...]
    dot_general x49 -> x0, matrix products: 110 us -> none  [the longest x8 30.5 us: key_compute(): jnp.einsum('hqk,qhd->khd', grad_scores, queries_part.reshape(rows_now, H,...]
    unnamed x287 -> x27, local copies, waits for them, and re-layouts: 95.8 us -> 1.61 us
    dynamic_slice x18 -> x1, local copies, waits for them, and re-layouts: 28.1 us -> 0.02 us  [body(): ub = lax.dynamic_index_in_dim(whole[:, 24:48].reshape(4, UP), z, 0, True)]
  transfers between devices with their start and end apart: 105 -> 0, of which waited for: 7 -> 0; matrix products, arithmetic and copies ran while one was open for 36% -> 0% of each run, Pallas kernels for 0% -> 0%
where the time goes in v1:
time: 254 us; the launch traced here: 253 us
  Pallas kernels  221 us (87%)
  local copies, waits for them, and re-layouts  21.9 us (9%)
  other arithmetic  8.59 us (3%)
    pallas_call x1, Pallas kernels, sum_all(): pl.pallas_call(sum_kernel, out_shape=(tok, tok, sh((4, 8, A), F32), sh((3...  47 us
    pallas_call x1, Pallas kernels, attention(): pl.pallas_call(attention_kernel, out_shape=(sh((3, 512, 128), BF16), sh((...  44.3 us
    pallas_call x1, Pallas kernels, gather_all(): pl.pallas_call(gather_kernel, out_shape=(tok, tok, jax.ShapeDtypeStruct((...  36.5 us
    pallas_call x1, Pallas kernels, sum_dkv(): pl.pallas_call(dkv_kernel, out_shape=jax.ShapeDtypeStruct((4, 3, 128, 128...  26.6 us
    pallas_call x1, Pallas kernels, gather_kv(): pl.pallas_call(kv_kernel, out_shape=jax.ShapeDtypeStruct((3, 4, 8, 128, 1...  23.5 us
    pallas_call x1, Pallas kernels, back(): pl.pallas_call(back_kernel, out_shape=(sh((512, 768), BF16), sh((512, 768...  15.8 us
    pallas_call x1, Pallas kernels, mlp(): pl.pallas_call(mlp_kernel, out_shape=(sh((512, 768), F32), sh((512, 1024)...  14.8 us
    pallas_call x1, Pallas kernels, front(): pl.pallas_call(front_kernel, out_shape=(sh((3, 512, 128), BF16), sh((3, 1...  12.7 us

profile of v1, /device:TPU:1, one launch (start us, length us, event | category | flops | bytes accessed | tf_op | source)
XLA Modules:
  0.0 252.7 jit_solution(11775464100331603798)
XLA Ops:
  0.7 5.4 %concatenate.30 = bf16[1408]{0:T(1024)(128)(2,1)S(1)} concatenate(bf16[18]{0:T(256)(128)(2,1)} %bitcast.114, bf16[6]{0:T(256)(128)(2,1)} %bitcast.115, bf16[24]{0:T(256)(128)(2,1)} %bitcast.116, bf16[6]{0:T(256)(128)(2,1)} %bitcast.117, bf16[6]{0:T(256)(128)(2,1)} %bitcast.118, bf16[6]{0:T(256)(128)(2,1)} %bitcast.119, bf16[6]{0:T(256)(128)(2,1)} %bitcast.120, ...), dimensions={0} | concatenate | bytes 5632 | tf_op jit(solution)/shard_map/concatenate | solution.py:716
  6.1 0.9 reshape_squeeze.29
  7.3 0.9 concatenate.29
  8.3 0.8 maximum_maximum_fusion.wz_ref
  9.2 1.4 maximum_maximum_fusion.1.wb_ref
  10.6 36.5 %gather_tokens_weights.1 = (bf16[4,128,768]{2,1,0:T(8,128)(2,1)}, bf16[4,128,768]{2,1,0:T(8,128)(2,1)}, bf16[32,32,2176]{2,1,0:T(8,128)(2,1)}) custom-call(bf16[128,768]{1,0:T(8,128)(2,1)} %bitcast.96, bf16[128,768]{1,0:T(8,128)(2,1)} %bitcast.98, f32[4,8,1408]{2,1,0:T(8,128)} %maximum_maximum_fusion.wz_ref, bf16[32,768]{1,0:T(8,128)(2,1)} %maximum_maximum_fusion.1.wb_ref), custom_call_target="tpu_custom_call" | custom-call | tf_op jit(solution)/shard_map/gather_tokens_weights/pallas_call | solution.py:165
  47.1 1.0 slice.182
  49.1 0.7 stack.17.vec_ref
  50.2 0.6 broadcast_in_dim.116.qb_ref
  51.1 1.9 fusion.13
  53.0 12.7 %norms_qkv.1 = (bf16[3,512,128]{2,1,0:T(8,128)(2,1)}, bf16[3,1024,128]{2,1,0:T(8,128)(2,1)}, bf16[512,1024]{1,0:T(8,128)(2,1)}, bf16[512,1024]{1,0:T(8,128)(2,1)...) custom-call(bf16[512,768]{1,0:T(8,128)(2,1)} %bitcast.101, bf16[512,768]{1,0:T(8,128)(2,1)} %bitcast.90, ...), custom_call_target="tpu_custom_call" | custom-call | tf_op jit(solution)/shard_map/norms_qkv/pallas_call | solution.py:239
  65.6 23.5 %gather_keys_values.1 = bf16[3,4,8,128,128]{4,3,2,1,0:T(8,128)(2,1)} custom-call(bf16[3,4,128,128]{3,2,1,0:T(8,128)(2,1)} %bitcast.102), custom_call_target="tpu_custom_call" | custom-call | tf_op jit(solution)/shard_map/gather_keys_values/pallas_call | solution.py:343
  89.1 44.3 %attention.1 = (bf16[3,512,128]{2,1,0:T(8,128)(2,1)}, f32[3,512,128]{2,1,0:T(8,128)}, bf16[32,3,128,128]{3,2,1,0:T(8,128)(2,1)}) custom-call(bf16[3,1024,128]{2,1,0:T(8,128)(2,1)} %get-tuple-element.46.qd_ref, bf16[3,4096,128]{2,1,0:T(8,128)(2,1)} %bitcast.89), custom_call_target="tpu_custom_call" | custom-call | tf_op jit(solution)/shard_map/attention/pallas_call | solution.py:421
  133.4 26.6 %sum_key_value_grads.1.dkv_ref = f32[4,3,128,128]{3,2,1,0:T(8,128)} custom-call(bf16[4,4,2,3,128,128]{5,4,3,2,1,0:T(8,128)(2,1)} %bitcast.97), custom_call_target="tpu_custom_call" | custom-call | tf_op jit(solution)/shard_map/sum_key_value_grads/pallas_call | solution.py:472
  160.2 0.6 broadcast_in_dim.122.ub_ref
  160.8 14.8 %feed_forward.1 = (f32[512,768]{1,0:T(8,128)}, f32[512,1024]{1,0:T(8,128)}, f32[8,1024]{1,0:T(8,128)}, f32[8,768]{1,0:T(8,128)}, bf16[1024,768]{1,0:T(8,128)(2,1)}, /*index=5*/f32[768,768]{1,0:T(8,128)}) custom-call(bf16[512,1024]{1,0:T(8,128)(2,1)} %get-tuple-element.54.nm_ref, bf16[512,768]{1,0:T(8,128)(2,1)} %bitcast.91, ...), custom_call_target="tpu_custom_call" | custom-call | tf_op jit(solution)/shard_map/feed_forward/pallas_call | solution.py:297
  175.8 0.6 broadcast_in_dim.123.ob_ref
  176.4 15.8 %backward.1 = (bf16[512,768]{1,0:T(8,128)(2,1)}, bf16[512,768]{1,0:T(8,128)(2,1)}, bf16[1024,640]{1,0:T(8,128)(2,1)}, bf16[32,32,768]{2,1,0:T(8,128)(2,1)}, f32[8,1024]{1,0:T(8,128)}, /*index=5*/f32[8,640]{1,0:T(8,128)}) custom-call(bf16[3,512,128]{2,1,0:T(8,128)(2,1)} %get-tuple-element.48.o_ref, f32[3,512,128]{2,1,0:T(8,128)} %get-tuple-element.49.dq_ref, ...), custom_call_target="tpu_custom_call" | custom-call | tf_op jit(solution)/shard_map/backward/pallas_call | solution.py:531
  192.4 0.8 slice_reduce_fusion.4
  193.4 0.7 slice_reduce_fusion.8
  194.4 0.7 slice.152
  195.4 0.8 convert.43
  196.9 0.8 pad_bitcast_fusion.small
  197.7 47.0 %sum_weight_grads.1 = (bf16[4,128,768]{2,1,0:T(8,128)(2,1)}, bf16[4,128,768]{2,1,0:T(8,128)(2,1)}, f32[4,8,1408]{2,1,0:T(8,128)}, f32[32,768]{1,0:T(8,128)}) custom-call(bf16[4,128,768]{2,1,0:T(8,128)(2,1)} %bitcast.99, bf16[4,128,768]{2,1,0:T(8,128)(2,1)} %bitcast.100, bf16[1024,768]{1,0:T(8,128)(2,1)} %get-tuple-element.61.dwup, ...), custom_call_target="tpu_custom_call" | custom-call | tf_op jit(solution)/shard_map/sum_weight_grads/pallas_call | solution.py:666
  244.7 1.5 convert_reduce_fusion
  246.9 0.9 fusion.10
  248.3 0.7 broadcast_in_dim_reshape.8
  249.5 0.6 copy.82
  250.2 0.6 slice_bitcast_fusion.3
  250.8 0.7 copy.83
  251.5 0.6 slice_bitcast_fusion.8
  252.1 0.6 slice_bitcast_fusion
  (116 shorter events, 5.7 us)
Async XLA Ops:
  0.6 8.5 %copy-start.5 = (bf16[1,24,768]{2,1,0:T(8,128)(2,1)S(1)}, bf16[1,24,768]{2,1,0:T(8,128)(2,1)}, u32[]{:S(2)}) copy-start(bf16[1,24,768]{2,1,0:T(8,128)(2,1)} %param.26) | copy-start | bytes 110596
  9.2 41.7 %copy-start.7 = (pred[16,8]{1,0:T(8,128)(4,1)S(1)}, pred[16,8]{1,0:T(8,128)(4,1)}, u32[]{:S(2)}) copy-start(pred[16,8]{1,0:T(8,128)(4,1)} %constant.134) | copy-start | bytes 388
  10.6 40.5 %copy-start.8 = (pred[128]{0:T(512)(128)(4,1)S(1)}, pred[128]{0:T(512)(128)(4,1)}, u32[]{:S(2)}) copy-start(pred[128]{0:T(512)(128)(4,1)} %constant.109.clone) | copy-start | bytes 388
  10.6 40.5 %copy-start.9 = (pred[128]{0:T(512)(128)(4,1)S(1)}, pred[128]{0:T(512)(128)(4,1)}, u32[]{:S(2)}) copy-start(pred[128]{0:T(512)(128)(4,1)} %constant.108.clone) | copy-start | bytes 388
  176.4 15.8 %copy-start.1 = (bf16[1,128,768]{2,1,0:T(8,128)(2,1)S(1)}, bf16[1,128,768]{2,1,0:T(8,128)(2,1)}, u32[]{:S(2)}) copy-start(bf16[1,128,768]{2,1,0:T(8,128)(2,1)} %param.32) | copy-start | bytes 589828
  176.4 20.0 %copy-start.6 = (f32[8,1024]{1,0:T(8,128)S(1)}, f32[8,1024]{1,0:T(8,128)}, u32[]{:S(2)}) copy-start(f32[8,1024]{1,0:T(8,128)} %get-tuple-element.67) | copy-start | bytes 98308
  197.7 48.5 %copy-start = (bf16[1,128,768]{2,1,0:T(8,128)(2,1)S(1)}, bf16[1,128,768]{2,1,0:T(8,128)(2,1)}, u32[]{:S(2)}) copy-start(bf16[1,128,768]{2,1,0:T(8,128)(2,1)} %param.19) | copy-start | bytes 589828
  244.7 2.1 copy-start.2
  246.7 1.1 copy-start.3
  246.9 2.7 %copy-start.4 = (f32[32,768]{1,0:T(8,128)S(1)}, f32[32,768]{1,0:T(8,128)}, u32[]{:S(2)}) copy-start(f32[32,768]{1,0:T(8,128)} %get-tuple-element.71) | copy-start | bytes 294916

commit v2 on v0

v2 whole, which is shorter than its diff:
```python
import functools

import jax
import jax.numpy as jnp
import numpy as np
from jax import lax
from jax.experimental import pallas as pl
from jax.experimental.pallas import tpu as pltpu
from jax.sharding import PartitionSpec as P

F32 = jnp.float32
BF16 = jnp.bfloat16
MESH = pl.DeviceIdType.MESH
VMEM = pl.BlockSpec(memory_space=pltpu.VMEM)
HBM = pl.BlockSpec(memory_space=pl.ANY)
MIB = 1024 * 1024

QKV, UP = 640, 768
WQ, WM = QKV + 256, 2 * UP
ZW = QKV + UP + 128
OFF = -1e30

def place():
    ctx, fs = lax.axis_index("ctx"), lax.axis_index("fsdp")
    z, y, xh = ctx // 8, (ctx // 2) % 4, ctx % 2
    xl, c = fs // 2, fs % 2
    return z, y, xh, xl, c


def dev(z, y, x, c):
    return (z * 8 + y * 2 + x // 2, (x % 2) * 2 + c)


def rcopy(src, dst, ss, rs, to):
    return pltpu.make_async_remote_copy(
        src_ref=src, dst_ref=dst, send_sem=ss, recv_sem=rs, device_id=to, device_id_type=MESH
    )


def mm(a, b):
    return jnp.dot(a, b, preferred_element_type=F32)


def mm_nt(a, b):
    return lax.dot_general(a, b, (((1,), (1,)), ((), ())), preferred_element_type=F32)


def mm_tn(a, b):
    return lax.dot_general(a, b, (((0,), (0,)), ((), ())), preferred_element_type=F32)


def params(**kw):
    return pltpu.CompilerParams(vmem_limit_bytes=60 * MIB, **kw)


def ids(shape, axis):
    return lax.broadcasted_iota(jnp.int32, shape, axis)


def div(n, d):
    return ((n.astype(F32) + 0.5) * np.float32(1.0 / d)).astype(jnp.int32)


def one_hot(mask):
    return jnp.where(mask, 1.0, 0.0).astype(BF16)


def vector_places(z):
    j = ids((1, 1024), 1)
    real = j % 8 < 6
    norms = [(j // 8 % 4 + 8 * (j // 32), [jnp.where(real, at + j % 8, -1)]) for at in (54, 60, 66, 72)]
    m = ids((1, QKV), 1)
    is_kv = m < 384
    kind = jnp.where(is_kv, jnp.where(m % 128 < 64, 1, 2), 0)
    col = kind * 768 + 192 * z + jnp.where(is_kv, 64 * (m // 128) + m % 64, m - 384)
    own = div(col, 18)
    qkv = ((own % 32) * 8 + own // 32, [jnp.where(m < 576, col - 18 * own, -1)])
    f = ids((1, UP), 1)
    p = div(f, 24)
    up = (p * 8 + z, [24 + f - 24 * p])
    own = div(f, 6)
    r = f - 6 * own
    out = ((own % 32) * 8 + own // 32, [18 + r, 48 + r])
    return norms, qkv, up, out


def lane_hot(lanes, n):
    lane = ids((128, n), 0)
    hit = lane == lanes[0]
    for more in lanes[1:]:
        hit = hit | (lane == more)
    return one_hot(hit)


def spread(packed, where):
    row, lanes = where
    n = row.shape[1]
    t = mm(packed, lane_hot(lanes, n))
    return jnp.sum(jnp.where(ids((256, n), 0) == row, t, 0.0), axis=0, keepdims=True)


def collect(vector, where):
    row, lanes = where
    n = row.shape[1]
    t = jnp.where(ids((256, n), 0) == row, vector, 0.0).astype(BF16)
    return mm_nt(t, lane_hot(lanes, n))


def turn(tile, cos, plus, minus):
    return tile * cos + pltpu.roll(tile, 8, 1) * plus + pltpu.roll(tile, 120, 1) * minus


def layer_kernel(
    x_ref, g_ref, qw_ref, uw_ref, ow_ref, dw_ref, sv_ref, cos_ref, sp_ref, sm_ref,
    ro, rd, zr, dn_out, o8_out,
    xa, ga, wq, wm, zs, zb, cq, cm, s, s3, big, xh, na, nm, vec, kv, qd, dkv, hid, du, part, dxh,
    ow, dw, att, dqkv, outp, dxp, fm, top, tot, acc, delta,
    kb1, kpair, kb2, mb1, mpair, mb2, mquad, mb3, qb1, qpair, qb2, qquad, qb3,
    swap_s, swap_r, loc, tz_s, tz_r, wz_s, wz_r,
    q1_s, q2_s, q3_s, qr_r, qp_r, m1_s, m2_s, m3_s, mr_r, mp_r,
    ky_s, ky_r, kp_s, kp_r, dp_s, dp_r, dy_s, dy_r,
    ma_s, ma_r, mb_s, mb_r, mc_s, mc_r, qa_s, qa_r, qb_s, qb_r, qc_s, qc_r, t_s, t_r, ze_s, ze_r,
):
    z, y, xhi, xl, c = place()
    x = xhi * 2 + xl
    zpeer = [dev((z + k) % 4, y, x, c) for k in range(4)]
    ypeer = [dev(z, (y + k) % 4, x, c) for k in range(4)]
    xpeer = [dev(z, y, (x + k) % 4, c) for k in range(4)]
    home = [dev((z + k) % 4, y, c * 2 + xl, xhi) for k in range(4)]
    first = [dev(z, (y + k * c) % 4, (x + k * (1 - c)) % 4, c) for k in range(4)]
    second = [dev(z, (y + k * (1 - c)) % 4, (x + k * c) % 4, c) for k in range(4)]
    partner = dev(z, y, x, 1 - c)
    swapped = xhi != c

    def slot(k1, k2):
        return (y + k1 * c + k2 * (1 - c)) % 4, (x + k1 * (1 - c) + k2 * c) % 4

    bar = pltpu.get_barrier_semaphore()
    for to in zpeer[1:] + ypeer[1:] + xpeer[1:] + [partner]:
        pl.semaphore_signal(bar, inc=1, device_id=to, device_id_type=MESH)

    @pl.when(swapped)
    def _():
        for to in home:
            pl.semaphore_signal(bar, inc=1, device_id=to, device_id_type=MESH)

    zs[...] = jnp.zeros((4, 8, ZW), F32)
    qw = qw_ref[0].astype(F32)
    uw = uw_ref[0].astype(F32)
    for i in range(4):
        pieces = []
        for h in range(3):
            at = 192 * i + 64 * h
            pieces += [qw[:, 768 + at : 832 + at], qw[:, 1536 + at : 1600 + at]]
        pieces += [qw[:, 192 * i : 192 * i + 192], jnp.zeros((6, 64), F32)]
        zs[i, 0:6, :QKV] = jnp.concatenate(pieces, axis=1)
        zs[i, 0:6, QKV : QKV + UP] = uw[:, UP * i : UP * i + UP]
        zs[i, 0:1, QKV + UP :] = sv_ref[0:1, :]

    pl.semaphore_wait(bar, 10 + 4 * ((xhi + c) % 2))

    zsends = [rcopy(zs.at[(z + k) % 4], zb.at[z], wz_s.at[k], wz_r.at[4 - k], zpeer[k]) for k in range(1, 4)]
    for d in zsends:
        d.start()
    swaps = [rcopy(src, dst.at[z], swap_s.at[t], swap_r.at[t], home[0]) for t, (src, dst) in enumerate(((x_ref, xa), (g_ref, ga)))]

    @pl.when(swapped)
    def _():
        swaps[0].start()
        swaps[1].start()

    @pl.when(xhi == c)
    def _():
        xa[z] = x_ref[...]
        ga[z] = g_ref[...]

    zb[z] = zs[z]
    j = ids((1, 1024), 1)
    nat = jnp.where(j % 8 < 6, 192 * (j // 8 % 4) + 6 * (j // 32) + j % 8, -1)
    s[...] = one_hot(ids((768, 1024), 0) == nat)
    i8 = ids((1, 256), 1)
    nat8 = jnp.where(i8 % 8 < 6, 6 * (i8 // 8) + i8 % 8, -1)
    for h in range(3):
        dim = ids((128, 256), 0)
        s3[h] = one_hot((dim >= 64) & (dim + (64 * h - 64) == nat8))

    for d in zsends:
        d.wait()
    big[0:32, :QKV] = zb[:, :, :QKV].reshape(32, QKV)
    out8 = jnp.concatenate([ow_ref[0].astype(F32), jnp.zeros((2, 768), F32)], axis=0)
    for i in range(3):
        big[8 * i : 8 * i + 8, QKV:WQ] = out8[:, 256 * i : 256 * i + 256]
    big[24:32, QKV:WQ] = jnp.zeros((8, 256), F32)
    for i in range(4):
        big[24 + i : 25 + i, QKV : QKV + 128] = zb[i, 0:1, QKV + UP :]
    cq[...] = big[0:32, :WQ].astype(BF16)
    cm[:, :UP] = zb[:, :, QKV : QKV + UP].reshape(32, UP).astype(BF16)
    cm[:, UP:] = jnp.concatenate([dw_ref[0].astype(F32), jnp.zeros((8, 768), F32)], axis=0).astype(BF16)
    wq[y, x, c] = cq[...]
    wm[y, x, c] = cm[...]

    class Ring:
        def __init__(self, own, arr, s1, s2, s3s, rr, pr):
            self.own, self.arr, self.s1, self.s2, self.s3, self.rr, self.pr, self.sends = own, arr, s1, s2, s3s, rr, pr, []

        def send(self, src, yy, xx, ss, rs, to):
            d = rcopy(src, self.arr.at[yy, xx, c], ss, rs, to)
            d.start()
            self.sends.append(d)

        def begin(self):
            for k in range(1, 4):
                self.send(self.own, y, x, self.s1.at[k], self.rr.at[4 - k, 0], first[k])
            for k in range(1, 4):
                self.send(self.own, y, x, self.s2.at[0, k], self.rr.at[0, 4 - k], second[k])
            self.send(self.own, y, x, self.s3.at[0, 0], self.pr.at[0, 0], partner)

        def arrived(self, k1, k2, rs, cc):
            yy, xx = slot(k1, k2)
            ref = self.arr.at[yy, xx, cc]
            rcopy(ref, ref, self.s3.at[k1, k2], rs, partner).wait_recv()
            return yy, xx

        def forward(self, k1, k2, on):
            yy, xx = self.arrived(k1, k2, self.rr.at[k1, k2], c)
            src = self.arr.at[yy, xx, c]
            if on:
                for k in range(1, 4):
                    self.send(src, yy, xx, self.s2.at[k1, k], self.rr.at[k1, 4 - k], second[k])
            self.send(src, yy, xx, self.s3.at[k1, k2], self.pr.at[k1, k2], partner)

        def finish(self):
            for k1 in range(4):
                for k2 in range(4):
                    yy, xx = (y + k1 * (1 - c) + k2 * c) % 4, (x + k1 * c + k2 * (1 - c)) % 4
                    ref = self.arr.at[yy, xx, 1 - c]
                    rcopy(ref, ref, self.s3.at[k1, k2], self.pr.at[k1, k2], partner).wait_recv()
            for d in self.sends:
                d.wait_send()

    rq = Ring(cq, wq, q1_s, q2_s, q3_s, qr_r, qp_r)
    rm = Ring(cm, wm, m1_s, m2_s, m3_s, mr_r, mp_r)
    rq.begin()

    def spread_tokens(t, arr):
        @pl.when(swapped)
        def _():
            swaps[t].wait()

        ds = [rcopy(arr.at[z], arr.at[z], tz_s.at[t, k], tz_r.at[t, 4 - k], zpeer[k]) for k in range(1, 4)]
        for d in ds:
            d.start()
        return ds

    xtok = spread_tokens(0, xa)
    rm.begin()
    for k1 in range(1, 4):
        rq.forward(k1, 0, True)
    gtok = spread_tokens(1, ga)
    for k1 in range(1, 4):
        rm.forward(k1, 0, True)
    for d in xtok:
        d.wait()

    big[:, :1024] = mm(xa[...].reshape(512, 768), s[...])
    for k2 in range(1, 4):
        for k1 in range(4):
            rq.forward(k1, k2, False)
    real = jnp.where(j % 8 < 6, 1.0, 0.0).astype(F32)
    for i in range(4):
        r = slice(128 * i, 128 * i + 128)
        v = big[r, :1024]
        mean = jnp.sum(v, axis=1, keepdims=True) * (1.0 / 768.0)
        cen = (v - mean) * real
        var = jnp.sum(cen * cen, axis=1, keepdims=True) * (1.0 / 768.0)
        xh[r, :] = cen * lax.rsqrt(var + 1e-5)
    rq.finish()
    packed = wq[:, :, :, 24:32, QKV : QKV + 128].reshape(256, 128)
    norm_at, qkv_at, up_at, out_at = vector_places(z)
    for i in range(4):
        vec[i : i + 1, :] = spread(packed, norm_at[i])
    for i in range(4):
        r = slice(128 * i, 128 * i + 128)
        na[r, :] = (xh[r, :] * vec[0:1, :] + vec[1:2, :]).astype(BF16)
        nm[r, :] = (xh[r, :] * vec[2:3, :] + vec[3:4, :]).astype(BF16)

    qkv = slice(1024, 1024 + QKV)
    wqkv = wq[:, :, :, :, :QKV].reshape(1024, QKV)
    big[:, qkv] = mm(na[...], wqkv) + spread(packed, qkv_at)
    low = ids((128, 128), 1) < 64
    yc = 2 * y + c
    for i in range(4):
        r = slice(128 * i, 128 * i + 128)
        cos, plus, minus = cos_ref[r, :], sp_ref[r, :], sm_ref[r, :]
        kc, kp, km = jnp.where(low, cos, 1.0), jnp.where(low, plus, 0.0), jnp.where(low, minus, 0.0)
        for h in range(3):
            kv[h, i, yc] = turn(big[r, 1024 + 128 * h : 1152 + 128 * h], kc, kp, km).astype(BF16)
        q01 = turn(big[r, 1408:1536], cos, plus, minus).astype(BF16).astype(F32) * 0.125
        q2 = turn(big[r, 1536:1664], cos, plus, minus).astype(BF16).astype(F32) * 0.125
        qd[0, r, :] = jnp.where(low, q01, 0.0).astype(BF16)
        qd[1, r, :] = jnp.where(low, pltpu.roll(q01, 64, 1), 0.0).astype(BF16)
        qd[2, r, :] = jnp.where(low, q2, 0.0).astype(BF16)

    kvsends = []
    for h in range(3):
        mine = kv.at[h, :, yc]
        ds = [rcopy(mine, mine, ky_s.at[h, k], ky_r.at[h, 4 - k], ypeer[k]) for k in range(1, 4)]
        ds.append(rcopy(mine, mine, kp_s.at[h, 0], kp_r.at[h, 0], partner))
        for d in ds:
            d.start()
        kvsends += ds

    def pass_on(h):
        for k in (1, 3, 2):
            there = kv.at[h, :, 2 * ((y + k) % 4) + c]
            rcopy(there, there, ky_s.at[h, k], ky_r.at[h, k], partner).wait_recv()
            d = rcopy(there, there, kp_s.at[h, k], kp_r.at[h, k], partner)
            d.start()
            kvsends.append(d)

    def kv_here(h):
        for k in range(4):
            there = kv.at[h, :, 2 * ((y + k) % 4) + 1 - c]
            rcopy(there, there, kp_s.at[h, k], kp_r.at[h, k], partner).wait_recv()

    for k2 in range(1, 4):
        for k1 in range(4):
            rm.forward(k1, k2, False)
    for d in gtok:
        d.wait()
    out8 = wq[:, :, :, :, QKV:WQ].reshape(32, 32, 256).astype(F32)
    for i in range(3):
        ow[:, 256 * i : 256 * i + 256] = out8[:, 8 * i : 8 * i + 8].reshape(256, 256).astype(BF16)
    g = ga[...].reshape(512, 768)
    dof = mm_nt(g, ow[...]).astype(BF16)
    for h in range(3):
        qd[h, 512:, :] = mm_nt(dof, s3[h]).astype(BF16)
    rm.finish()
    dw[...] = wm[:, :, :, :, UP:].reshape(32, 32, 768).astype(F32)[:, :24].reshape(768, 768).astype(BF16)
    wup = wm[:, :, :, :, :UP].reshape(1024, UP)
    lanes = slice(2048, 2048 + UP)
    big[:, lanes] = mm(nm[...], wup) + spread(packed, up_at)
    pass_on(0)
    for i in range(4):
        r = slice(128 * i, 128 * i + 128)
        u = big[r, lanes]
        cdf = 0.5 * (1.0 + lax.erf(u * np.float32(np.sqrt(0.5))))
        pdf = jnp.exp(-0.5 * u * u) * np.float32(1.0 / np.sqrt(2.0 * np.pi))
        hid[r, :] = (u * cdf).astype(BF16)
        big[r, lanes] = cdf + u * pdf
    part[...] = mm(hid[...], dw[...])
    du[...] = (mm_nt(g, dw[...]) * big[:, lanes]).astype(BF16)
    pass_on(1)
    dn = mm_nt(du[...], wup)
    grads = [
        jnp.sum(dn * xh[...], axis=0, keepdims=True),
        jnp.sum(dn, axis=0, keepdims=True),
        jnp.sum(du[...].astype(F32), axis=0, keepdims=True),
    ]
    dxh[...] = dn * vec[2:3, :]
    small = collect(grads[0], norm_at[2]) + collect(grads[1], norm_at[3]) + collect(grads[2], up_at)
    small += collect(jnp.sum(ga[z].astype(F32), axis=0, keepdims=True), out_at)
    dwd = mm_tn(hid[...], g).reshape(32, 24, 768)
    dwd = jnp.concatenate([dwd, jnp.zeros((32, 8, 768), F32)], axis=1).astype(BF16)
    wm[:, :, :, :, UP:] = dwd.reshape(4, 4, 2, 32, 768)
    wm[:, :, :, :, :UP] = mm_tn(nm[...], du[...]).astype(BF16).reshape(4, 4, 2, 32, UP)
    msend = rcopy(wm.at[:, :, 1 - c], mb1, ma_s.at[0], ma_r.at[0], partner)
    msend.start()
    pass_on(2)

    msends = []

    def m_pairs():
        msend.wait_recv()
        for k in range(1, 4):
            xx = (x + k) % 4
            for yy in range(4):
                mpair[k, yy] = (wm[yy, xx, c].astype(F32) + mb1[yy, xx].astype(F32)).astype(BF16)
            d = rcopy(mpair.at[k], mb2.at[4 - k], mb_s.at[k], mb_r.at[4 - k], xpeer[k])
            d.start()
            msends.append(d)
        for yy in range(4):
            mpair[0, yy] = (wm[yy, x, c].astype(F32) + mb1[yy, x].astype(F32)).astype(BF16)

    def m_quads():
        for k in range(1, 4):
            rcopy(mpair.at[k], mb2.at[k], mb_s.at[k], mb_r.at[k], partner).wait_recv()
        for k in (1, 2, 3, 0):
            yy = (y + k) % 4
            total = mpair[0, yy].astype(F32) + mb2[1, yy].astype(F32) + mb2[2, yy].astype(F32) + mb2[3, yy].astype(F32)
            if k:
                mquad[k] = total.astype(BF16)
                d = rcopy(mquad.at[k], mb3.at[4 - k], mc_s.at[k], mc_r.at[4 - k], ypeer[k])
                d.start()
                msends.append(d)
            else:
                fm[...] = total

    def m_last():
        for k in range(1, 4):
            rcopy(mquad.at[k], mb3.at[k], mc_s.at[k], mc_r.at[k], partner).wait_recv()
        fm[...] += mb3[1].astype(F32) + mb3[2].astype(F32) + mb3[3].astype(F32)

    row = yc * 128 + ids((128, 1024), 0)
    key = ids((128, 1024), 1)

    def rep(a):
        return jnp.concatenate([a] * 8, axis=1)

    def fold(a, f):
        r = a[:, :128]
        for i in range(1, 8):
            r = f(r, a[:, 128 * i : 128 * i + 128])
        return r

    def keys_of(h, j):
        return kv[h, j].reshape(1024, 128)

    def lane_sum(a, f):
        return jnp.broadcast_to(f(a, axis=1, keepdims=True), (512, 128))

    def attend(h, middle):
        top[...] = jnp.full((512, 128), OFF, F32)
        tot[...] = jnp.zeros((512, 128), F32)
        acc[...] = jnp.zeros((512, 128), F32)
        for j in range(4):
            r0, cols = 128 * j, slice(1024 * j, 1024 * j + 1024)
            sc = mm_nt(qd[h, r0:512, :], keys_of(h, j))
            near = jnp.where(key <= row, sc[:128], OFF)
            sc = near if j == 3 else jnp.concatenate([near, sc[128:]], axis=0)
            big[r0:, cols] = sc
            top[r0:, :] = jnp.maximum(top[r0:, :], fold(sc, jnp.maximum))
        top[...] = lane_sum(top[...], jnp.max)
        for j in range(4):
            r0, cols = 128 * j, slice(1024 * j, 1024 * j + 1024)
            p = jnp.exp(big[r0:, cols] - rep(top[r0:, :]))
            big[r0:, cols] = p
            tot[r0:, :] += fold(p, jnp.add)
            acc[r0:, :] += mm(p.astype(BF16), keys_of(h, j))
        inv = 1.0 / lane_sum(tot[...], jnp.sum)
        tot[...] = inv
        o = acc[...] * inv
        delta[...] = lane_sum(o * qd[h, 512:, :].astype(F32), jnp.sum)
        acc[...] = jnp.zeros((512, 128), F32)
        middle()
        for j in range(4):
            r0, cols = 128 * j, slice(1024 * j, 1024 * j + 1024)
            kvj = keys_of(h, j)
            p = big[r0:, cols] * rep(tot[r0:, :])
            dp = mm_nt(qd[h, 512 + r0 :, :], kvj)
            ds = (p * (dp - rep(delta[r0:, :]))).astype(BF16)
            acc[r0:, :] += mm(ds, kvj)
            d = mm_tn(qd[h, r0:512, :], ds) + mm_tn(qd[h, 512 + r0 :, :], p.astype(BF16))
            for i in range(8):
                dkv[h, j, i // 2, i % 2] = d[:, 128 * i : 128 * i + 128].astype(BF16)
        return mm(o.astype(BF16), s3[h]), acc[...] * 0.125

    halves, ysends = [], []

    def dkv_begin(h):
        d = rcopy(dkv.at[h, :, :, 1 - c], kb1.at[h], dp_s.at[h], dp_r.at[h], partner)
        d.start()
        halves.append(d)

    def dkv_pairs(h):
        halves[h].wait_recv()
        for k in (2, 1, 3, 0):
            yy = (y + k) % 4
            for i in range(4):
                kpair[h, k, i] = (dkv[h, i, yy, c].astype(F32) + kb1[h, i, yy].astype(F32)).astype(BF16)
            if k:
                d = rcopy(kpair.at[h, k], kb2.at[h, 4 - k], dy_s.at[h, k], dy_r.at[h, 4 - k], ypeer[k])
                d.start()
                ysends.append(d)

    def back_tile(i, first_lane, tile, keys):
        r = slice(128 * i, 128 * i + 128)
        cos, plus, minus = cos_ref[r, :], -sp_ref[r, :], -sm_ref[r, :]
        if keys:
            cos, plus, minus = jnp.where(low, cos, 1.0), jnp.where(low, plus, 0.0), jnp.where(low, minus, 0.0)
        dqkv[r, first_lane : first_lane + 128] = turn(tile, cos, plus, minus).astype(BF16)

    def dkv_last(h):
        for k in range(1, 4):
            rcopy(kpair.at[h, k], kb2.at[h, k], dy_s.at[h, k], dy_r.at[h, k], partner).wait_recv()
        for i in range(4):
            total = kpair[h, 0, i].astype(F32) + kb2[h, 1, i].astype(F32) + kb2[h, 2, i].astype(F32) + kb2[h, 3, i].astype(F32)
            back_tile(i, 128 * h, total.T, True)

    kv_here(0)
    o0, d0 = attend(0, lambda: None)
    dkv_begin(0)
    m_pairs()
    kv_here(1)
    o1, d1 = attend(1, lambda: dkv_pairs(0))
    dkv_begin(1)
    m_quads()
    kv_here(2)
    o2, d2 = attend(2, lambda: dkv_pairs(1))
    dkv_begin(2)
    m_last()

    att[...] = (o0 + o1 + o2).astype(BF16)
    outs = part[...] + mm(att[...], ow[...]) + spread(packed, out_at) * jnp.where(z == 0, 1.0, 0.0)
    outp[...] = outs.astype(BF16).reshape(4, 128, 768)
    toks = []
    for t, (src, dst) in enumerate(((outp, ro), (dxp, rd))):
        toks.append([rcopy(src.at[(z + k) % 4], dst.at[z], t_s.at[t, k], t_r.at[t, k], home[k]) for k in range(4)])
    stays = [pltpu.make_async_copy(outp.at[z], ro.at[z], loc.at[0]), pltpu.make_async_copy(dxp.at[z], rd.at[z], loc.at[1])]

    def send_back(t):
        for k in range(1, 4):
            toks[t][k].start()

        @pl.when(swapped)
        def _():
            toks[t][0].start()

        @pl.when(xhi == c)
        def _():
            stays[t].start()

    send_back(0)
    dkv_pairs(2)
    dwo = mm_tn(att[...], g).reshape(32, 8, 768)
    for i in range(4):
        r = slice(128 * i, 128 * i + 128)
        back_tile(i, 384, jnp.where(low, d0[r], pltpu.roll(d1[r], 64, 1)), False)
        back_tile(i, 512, jnp.where(low, d2[r], 0.0), False)
    for h in range(3):
        dkv_last(h)
    dqb = jnp.sum(dqkv[...].astype(F32), axis=0, keepdims=True)
    dn = mm_nt(dqkv[...], wqkv)
    small += collect(jnp.sum(dn * xh[...], axis=0, keepdims=True), norm_at[0])
    small += collect(jnp.sum(dn, axis=0, keepdims=True), norm_at[1]) + collect(dqb, qkv_at)
    dx = (dxh[...] + dn * vec[0:1, :]).astype(BF16)
    dwq = mm_tn(na[...], dqkv[...]).astype(BF16)
    wq[:, :, :, :, :QKV] = dwq.reshape(4, 4, 2, 32, QKV)
    last = jnp.concatenate([small.reshape(32, 8, 128), jnp.zeros((32, 8, 128), F32)], axis=2)
    tail = jnp.concatenate([dwo[:, :, :256], dwo[:, :, 256:512], dwo[:, :, 512:], last], axis=1)
    wq[:, :, :, :, QKV:] = tail.astype(BF16).reshape(4, 4, 2, 32, 256)

    def qslot(k1, k2, cc):
        return (y + k1 * (1 - cc) + k2 * cc) % 4, (x + k1 * cc + k2 * (1 - cc)) % 4

    order = [(k1, k2) for k1 in (2, 1, 3, 0) for k2 in (2, 1, 3, 0)]
    qsends = []
    for k1, k2 in order:
        yy, xx = qslot(k1, k2, 1 - c)
        d = rcopy(wq.at[yy, xx, 1 - c], qb1.at[k1, k2], qa_s.at[k1, k2], qa_r.at[k1, k2], partner)
        d.start()
        qsends.append(d)
    dxp[...] = mm_nt(dx, s[...]).astype(BF16).reshape(4, 128, 768)
    send_back(1)
    for k1, k2 in order:
        yy, xx = qslot(k1, k2, c)
        rcopy(wq.at[yy, xx, c], qb1.at[k1, k2], qa_s.at[k1, k2], qa_r.at[k1, k2], partner).wait_recv()
        qpair[k1, k2] = (wq[yy, xx, c].astype(F32) + qb1[k1, k2].astype(F32)).astype(BF16)
        if k1:
            d = rcopy(qpair.at[k1, k2], qb2.at[4 - k1, k2], qb_s.at[k1, k2], qb_r.at[4 - k1, k2], second[k1])
            d.start()
            qsends.append(d)
    for k2 in (2, 1, 3, 0):
        for k1 in range(1, 4):
            rcopy(qpair.at[k1, k2], qb2.at[k1, k2], qb_s.at[k1, k2], qb_r.at[k1, k2], partner).wait_recv()
        total = qpair[0, k2].astype(F32) + qb2[1, k2].astype(F32) + qb2[2, k2].astype(F32) + qb2[3, k2].astype(F32)
        if k2:
            qquad[k2] = total.astype(BF16)
            d = rcopy(qquad.at[k2], qb3.at[4 - k2], qc_s.at[k2], qc_r.at[4 - k2], first[k2])
            d.start()
            qsends.append(d)
    for k in range(1, 4):
        rcopy(qquad.at[k], qb3.at[k], qc_s.at[k], qc_r.at[k], partner).wait_recv()
    total = total + qb3[1].astype(F32) + qb3[2].astype(F32) + qb3[3].astype(F32)
    zs[:, :, :QKV] = total[:, :QKV].reshape(4, 8, QKV)
    zs[:, :, QKV : QKV + UP] = fm[:, :UP].reshape(4, 8, UP)
    for i in range(4):
        zs[i, 0:1, QKV + UP :] = total[24 + i : 25 + i, QKV : QKV + 128]
    zsends = [rcopy(zs.at[(z + k) % 4], zr.at[z], ze_s.at[k], ze_r.at[4 - k], zpeer[k]) for k in range(1, 4)]
    for d in zsends:
        d.start()
    zr[z] = zs[z]
    dn_out[...] = fm[:, UP:]
    o8_out[...] = jnp.concatenate([total[0:8, QKV:], total[8:16, QKV:], total[16:24, QKV:]], axis=1)

    for d in qsends + msends + ysends + halves + kvsends + [msend]:
        d.wait_send()
    for t in range(2):
        for k in range(1, 4):
            toks[t][k].wait()

        @pl.when(swapped)
        def _():
            toks[t][0].wait()

        @pl.when(xhi == c)
        def _():
            stays[t].wait()

    for d in zsends:
        d.wait()


def layer(x, g, qw, uw, ow, dw, sv, cos, plus, minus):
    sh = jax.ShapeDtypeStruct

    def vm(*shape, dtype=BF16):
        return pltpu.VMEM(shape, dtype)

    def sem(*shape):
        return pltpu.SemaphoreType.DMA(shape)

    tok = (4, 128, 768)
    scratch = [
        vm(*tok), vm(*tok), vm(4, 4, 2, 32, WQ), vm(4, 4, 2, 32, WM), vm(4, 8, ZW, dtype=F32), vm(4, 8, ZW, dtype=F32),
        vm(32, WQ), vm(32, WM), vm(768, 1024), vm(3, 128, 256), vm(512, 4096, dtype=F32), vm(512, 1024, dtype=F32),
        vm(512, 1024), vm(512, 1024), vm(8, 1024, dtype=F32), vm(3, 4, 8, 128, 128), vm(3, 1024, 128),
        vm(3, 4, 4, 2, 128, 128), vm(512, 768), vm(512, 768), vm(512, 768, dtype=F32), vm(512, 1024, dtype=F32),
        vm(256, 768), vm(768, 768), vm(512, 256), vm(512, QKV), vm(*tok), vm(*tok), vm(32, WM, dtype=F32),
    ] + [vm(512, 128, dtype=F32)] * 4 + [
        vm(3, 4, 4, 128, 128), vm(3, 4, 4, 128, 128), vm(3, 4, 4, 128, 128),
        vm(4, 4, 32, WM), vm(4, 4, 32, WM), vm(4, 4, 32, WM), vm(4, 32, WM), vm(4, 32, WM),
        vm(4, 4, 32, WQ), vm(4, 4, 32, WQ), vm(4, 4, 32, WQ), vm(4, 32, WQ), vm(4, 32, WQ),
        sem(2), sem(2), sem(2), sem(2, 4), sem(2, 4), sem(4), sem(4),
        sem(4), sem(4, 4), sem(4, 4), sem(4, 4), sem(4, 4), sem(4), sem(4, 4), sem(4, 4), sem(4, 4), sem(4, 4),
        sem(3, 4), sem(3, 4), sem(3, 4), sem(3, 4), sem(3), sem(3), sem(3, 4), sem(3, 4),
        sem(1), sem(1), sem(4), sem(4), sem(4), sem(4), sem(4, 4), sem(4, 4), sem(4, 4), sem(4, 4), sem(4), sem(4),
        sem(2, 4), sem(2, 4), sem(4), sem(4),
    ]
    return pl.pallas_call(
        layer_kernel,
        out_shape=(sh(tok, BF16), sh(tok, BF16), sh((4, 8, ZW), F32), sh((32, 768), F32), sh((8, 768), F32)),
        in_specs=[VMEM] * 10,
        out_specs=(HBM, HBM, VMEM, VMEM, VMEM),
        scratch_shapes=scratch,
        compiler_params=pltpu.CompilerParams(vmem_limit_bytes=63 * MIB, collective_id=0, has_side_effects=True),
        name="layer",
    )(x, g, qw, uw, ow, dw, sv, cos, plus, minus)


CUTS = (0, 18, 24, 48, 54, 60, 66, 72, 78)


def finish_kernel(x_ref, g_ref, ro, rd, zr, dn, o8, *outs):
    out, dx_out, qkv, up, out_w, down = outs[:6]
    xf = x_ref[...].astype(F32)
    total = ro[0].astype(F32) + ro[1].astype(F32) + ro[2].astype(F32) + ro[3].astype(F32)
    out[0] = (xf + total).astype(BF16)
    dxh = rd[0].astype(F32) + rd[1].astype(F32) + rd[2].astype(F32) + rd[3].astype(F32)
    cen = xf - jnp.mean(xf, axis=1, keepdims=True)
    rstd = lax.rsqrt(jnp.mean(cen * cen, axis=1, keepdims=True) + 1e-5)
    xn = cen * rstd
    mean, along = jnp.mean(dxh, axis=1, keepdims=True), jnp.mean(dxh * xn, axis=1, keepdims=True)
    dx_out[0] = g_ref[...].astype(F32) + rstd * (dxh - mean - xn * along)
    pieces = [zr[i, 0:6, 384:576] for i in range(4)]
    pieces += [zr[i, 0:6, 128 * h : 128 * h + 64] for i in range(4) for h in range(3)]
    pieces += [zr[i, 0:6, 128 * h + 64 : 128 * h + 128] for i in range(4) for h in range(3)]
    qkv[0] = jnp.concatenate(pieces, axis=1)
    up[0] = jnp.concatenate([zr[i, 0:6, QKV : QKV + UP] for i in range(4)], axis=1)
    out_w[0] = o8[0:6, :]
    down[0] = dn[0:24, :]
    rows = sum(zr[i, 0:1, QKV + UP :] for i in range(4))
    for ref, a, b in zip(outs[6:], CUTS[:-1], CUTS[1:]):
        ref[...] = rows[:, a:b]


def finish(*args):
    def sh(*shape, dtype=F32):
        return jax.ShapeDtypeStruct(shape, dtype)

    shapes = [sh(1, 128, 768, dtype=BF16), sh(1, 128, 768), sh(1, 6, 2304), sh(1, 6, 3072), sh(1, 6, 768), sh(1, 24, 768)]
    shapes += [sh(1, b - a) for a, b in zip(CUTS[:-1], CUTS[1:])]
    return pl.pallas_call(
        finish_kernel,
        out_shape=tuple(shapes),
        in_specs=[VMEM] * 7,
        out_specs=(VMEM,) * 14,
        compiler_params=params(),
        name="finish",
    )(*args)


def rotary(first_block):
    f = 10000.0 ** (-2.0 * jnp.arange(8, dtype=F32) / 16)
    lane = np.arange(128) % 64
    freq = jnp.where(lane < 16, jnp.tile(f, 16), 0.0)
    pos = (first_block * 128 + 1024 * jnp.arange(4)[:, None] + jnp.arange(128)[None, :]).reshape(512).astype(F32)
    angle = pos[:, None] * freq[None, :]
    sin = jnp.sin(angle)
    return jnp.cos(angle), jnp.where(lane >= 8, sin, 0.0), jnp.where(lane < 8, -sin, 0.0)


def body(
    inputs, qkv_weight, qkv_bias, out_weight, out_bias, up_weight, up_bias, down_weight, down_bias,
    attn_gain, attn_shift, mlp_gain, mlp_shift, cotangent,
):
    z, y, xh, xl, c = place()
    x, g = inputs[0], cotangent[0]
    vectors = (qkv_bias, out_bias, up_bias, down_bias, attn_gain, attn_shift, mlp_gain, mlp_shift)
    sv = jnp.concatenate([v[0] for v in vectors] + [jnp.zeros((50,), BF16)]).astype(F32)
    sv = jnp.broadcast_to(sv[None], (8, 128))
    cos, plus, minus = rotary(2 * y + c)
    ro, rd, zr, dn, o8 = layer(x, g, qkv_weight, up_weight, out_weight, down_weight, sv, cos, plus, minus)
    out, dx, qkv, up, ow, dw, *t = finish(x, g, ro, rd, zr, dn, o8)
    return out, dx, qkv, t[0], ow, t[1], up, t[2], dw, t[3], t[4], t[5], t[6], t[7]


def solution(mesh):
    tok = P("fsdp", "ctx", None)
    mat = P(None, ("ctx", "fsdp"), None)
    row = P(None, ("ctx", "fsdp"))
    in_specs = (tok, mat, row, mat, row, mat, row, mat, row, row, row, row, row, tok)
    out_specs = (tok, tok, mat, row, mat, row, mat, row, mat, row, row, row, row, row)
    return jax.shard_map(body, mesh=mesh, in_specs=in_specs, out_specs=out_specs, check_vma=False)
```

time: 1800 us -> 135 us (0.07)
  blocking collectives: 766 us -> 0 us
  waiting for transfers between devices: 480 us -> 0 us
  starting transfers between devices: 257 us -> 0 us
  local copies, waits for them, and re-layouts: 145 us -> 5.78 us
  Pallas kernels: 0 us -> 127 us
  matrix products: 110 us -> 0 us
    unnamed x3 -> x0, blocking collectives: 516 us -> none
    all_gather x8 -> x0, waiting for transfers between devices: 477 us -> none  [the longest x4 182 us: body(): lax.all_gather(for_sending(shards_here), ('ctx', 'fsdp'), axis=0, tiled=T...]
    unnamed x96 -> x0, starting transfers between devices: 256 us -> none
    all_gather x2 -> x0, blocking collectives: 251 us -> none  [the longest x1 171 us: backward_layer(): lax.all_gather(lse_rows, 'ctx', axis=1, tiled=True)]
    pallas_call x0 -> x2, Pallas kernels: none -> 127 us  [the longest x1 124 us: layer(): pl.pallas_call(layer_kernel, out_shape=(sh(tok, BF16), sh(tok, BF16), sh(...]
    dot_general x49 -> x0, matrix products: 110 us -> none  [the longest x8 30.5 us: key_compute(): jnp.einsum('hqk,qhd->khd', grad_scores, queries_part.reshape(rows_now, H,...]
    unnamed x287 -> x29, local copies, waits for them, and re-layouts: 95.8 us -> 4.99 us
    dynamic_slice x18 -> x0, local copies, waits for them, and re-layouts: 28.1 us -> none  [the longest x10 16.1 us: one_turn(): lax.dynamic_slice_in_dim(member, turn_index * sub_rows, sub_rows, 0)]
  transfers between devices with their start and end apart: 105 -> 0, of which waited for: 7 -> 0; matrix products, arithmetic and copies ran while one was open for 36% -> 0% of each run, Pallas kernels for 0% -> 0%
where the time goes in v2:
time: 135 us
  Pallas kernels  127 us (94%)
  local copies, waits for them, and re-layouts  5.78 us (4%)
  other arithmetic  1.95 us (1%)
    pallas_call x1, Pallas kernels, layer(): pl.pallas_call(layer_kernel, out_shape=(sh(tok, BF16), sh(tok, BF16), sh(...  124 us
    unnamed x29, local copies, waits for them, and re-layouts  4.99 us
    pallas_call x1, Pallas kernels, finish(): pl.pallas_call(finish_kernel, out_shape=tuple(shapes), in_specs=[VMEM] *...  2.94 us

profile of v2, /device:TPU:1, one launch (start us, length us, event | category | flops | bytes accessed | tf_op | source)
XLA Modules:
  0.0 135.0 jit_solution(14426442231650321124)
XLA Ops:
  0.7 0.0 copy-start.10
  0.7 0.0 copy-start.6
  0.7 0.0 copy-start.7
  0.7 0.0 copy-start.8
  0.7 0.0 copy-start.9
  0.8 0.0 copy-start.3
  0.8 0.0 copy-start.4
  0.8 0.0 copy-start.5
  0.8 0.6 copy-done.10
  1.4 0.0 copy-done.6
  1.4 0.0 copy-done.7
  1.4 0.0 copy-done.8
  1.4 0.0 copy-done.9
  1.4 0.0 copy-done.3
  1.4 0.0 copy-done.4
  1.4 0.0 copy-done.5
  1.5 0.1 concatenate.31
  1.6 0.1 convert_bitcast_fusion
  1.6 0.6 broadcast_in_dim.30.sv_ref
  2.2 0.1 copy-done.2
  2.3 0.1 reshape.119
  2.4 0.6 copy-done.11
  3.0 0.0 copy-done.12
  3.0 1.9 %fusion.2 = (f32[512,128]{1,0:T(8,128)}, f32[512,128]{1,0:T(8,128)}, f32[512,128]{1,0:T(8,128)}) fusion(f32[128]{0:T(128)S(1)} %reshape.119, f32[512]{0:T(512)S(1)} %convert_bitcast_fusion, pred[128]{0:T(512)(128)(4,1)S(1)} %copy-done.11, pred[128]{0:T(512)(128)(4,1)S(1)} %copy-done.12), kind=kLoop, calls=%fused_computation.4 | loop fusion | flops 262144 | bytes 789248 | tf_op jit(solution)/shard_map/jit(_where)/select_n | solution.py:690
  4.9 123.6 %layer.1 = (bf16[4,128,768]{2,1,0:T(8,128)(2,1)}, bf16[4,128,768]{2,1,0:T(8,128)(2,1)}, f32[4,8,1536]{2,1,0:T(8,128)}, f32[32,768]{1,0:T(8,128)}, f32[8,768]{1,0:T(8,128)}) custom-call(bf16[128,768]{1,0:T(8,128)(2,1)} %bitcast.12, bf16[128,768]{1,0:T(8,128)(2,1)} %bitcast.14, bf16[1,6,2304]{2,1,0:T(8,128)(2,1)} %qw_ref.1, bf16[1,6,3072]{2,1,0:T(8,128)(2,1)} %uw_ref.1, ...), custom_call_target="tpu_custom_call" | custom-call | tf_op jit(solution)/shard_map/layer/pallas_call | solution.py:630
  128.5 2.9 %finish.1 = (bf16[1,128,768]{2,1,0:T(8,128)(2,1)}, f32[1,128,768]{2,1,0:T(8,128)}, f32[1,6,2304]{2,1,0:T(8,128)}, f32[1,6,3072]{2,1,0:T(8,128)}, f32[1,6,768]{2,...) custom-call(bf16[128,768]{1,0:T(8,128)(2,1)} %bitcast.13, ...), custom_call_target="tpu_custom_call" | custom-call | tf_op jit(solution)/shard_map/finish/pallas_call | solution.py:673
  131.4 0.0 copy-start.1
  131.4 0.0 copy-start
  131.4 0.7 copy-done.1
  132.1 0.6 copy.35
  132.8 1.6 %copy.34 = f32[1,6,2304]{2,0,1:T(1,128)} copy(f32[1,6,2304]{2,1,0:T(8,128)} %get-tuple-element.68) | data formatting | bytes 110592
  134.3 0.7 copy.36
  (8 shorter events, 0.0 us)
Async XLA Ops:
  0.7 0.7 copy-start.10
  0.7 0.7 copy-start.6
  0.7 0.7 copy-start.7
  0.7 0.7 copy-start.8
  0.7 0.7 copy-start.9
  0.8 0.7 copy-start.3
  0.8 0.7 copy-start.4
  0.8 0.7 copy-start.5
  1.6 0.7 copy-start.2
  2.3 0.7 copy-start.11
  2.3 0.7 copy-start.12
  131.4 0.7 copy-start.1
  131.4 2.9 %copy-start = (f32[1,6,3072]{2,1,0:T(8,128)S(1)}, f32[1,6,3072]{2,1,0:T(8,128)}, u32[]{:S(2)}) copy-start(f32[1,6,3072]{2,1,0:T(8,128)} %get-tuple-element.72) | copy-start | bytes 221188

commit v3 on v2

--- a/solution.py
+++ b/solution.py
@@ -16,7 +16,6 @@
 MIB = 1024 * 1024
 
 QKV, UP = 640, 768
-WQ, WM = QKV + 256, 2 * UP
 ZW = QKV + UP + 128
 OFF = -1e30
 
@@ -65,10 +64,15 @@
     return jnp.where(mask, 1.0, 0.0).astype(BF16)
 
 
+def owner(j):
+    p = div(j, 24)
+    return p, j - 24 * p
+
+
 def vector_places(z):
-    j = ids((1, 1024), 1)
-    real = j % 8 < 6
-    norms = [(j // 8 % 4 + 8 * (j // 32), [jnp.where(real, at + j % 8, -1)]) for at in (54, 60, 66, 72)]
+    j = ids((1, 768), 1)
+    p, of = owner(j)
+    norms = [(8 * p + div(of, 6), [at + of - 6 * div(of, 6)]) for at in (54, 60, 66, 72)]
     m = ids((1, QKV), 1)
     is_kv = m < 384
     kind = jnp.where(is_kv, jnp.where(m % 128 < 64, 1, 2), 0)
@@ -111,15 +115,15 @@
 
 
 def layer_kernel(
-    x_ref, g_ref, qw_ref, uw_ref, ow_ref, dw_ref, sv_ref, cos_ref, sp_ref, sm_ref,
+    x_ref, g_ref, qw_ref, uw_ref, ow_ref, dw_ref, v0, v1, v2, v3, v4, v5, v6, v7,
     ro, rd, zr, dn_out, o8_out,
     xa, ga, wq, wm, zs, zb, cq, cm, s, s3, big, xh, na, nm, vec, kv, qd, dkv, hid, du, part, dxh,
-    ow, dw, att, dqkv, outp, dxp, fm, top, tot, acc, delta,
+    ow, dw, wn, att, dqkv, outp, obuf, dxp, fm, cos_ref, sp_ref, sm_ref, top, tot, acc, delta,
     kb1, kpair, kb2, mb1, mpair, mb2, mquad, mb3, qb1, qpair, qb2, qquad, qb3,
     swap_s, swap_r, loc, tz_s, tz_r, wz_s, wz_r,
     q1_s, q2_s, q3_s, qr_r, qp_r, m1_s, m2_s, m3_s, mr_r, mp_r,
     ky_s, ky_r, kp_s, kp_r, dp_s, dp_r, dy_s, dy_r,
-    ma_s, ma_r, mb_s, mb_r, mc_s, mc_r, qa_s, qa_r, qb_s, qb_r, qc_s, qc_r, t_s, t_r, ze_s, ze_r,
+    ma_s, ma_r, mb_s, mb_r, mc_s, mc_r, qa_s, qa_r, qb_s, qb_r, qc_s, qc_r, t_s, t_r, o_s, o_r, ze_s, ze_r,
 ):
     z, y, xhi, xl, c = place()
     x = xhi * 2 + xl
@@ -132,8 +136,11 @@
     partner = dev(z, y, x, 1 - c)
     swapped = xhi != c
 
-    def slot(k1, k2):
-        return (y + k1 * c + k2 * (1 - c)) % 4, (x + k1 * (1 - c) + k2 * c) % 4
+    def q_slot(k1, k2, cc):
+        return (y + k1 * cc + k2 * (1 - cc)) % 4, (x + k1 * (1 - cc) + k2 * cc) % 4
+
+    def m_slot(k1, k2, cc):
+        return (y + k1) % 4, (x + k2) % 4
 
     bar = pltpu.get_barrier_semaphore()
     for to in zpeer[1:] + ypeer[1:] + xpeer[1:] + [partner]:
@@ -147,6 +154,8 @@
     zs[...] = jnp.zeros((4, 8, ZW), F32)
     qw = qw_ref[0].astype(F32)
     uw = uw_ref[0].astype(F32)
+    vectors = [v[...].astype(F32) for v in (v0, v1, v2, v3, v4, v5, v6, v7)]
+    vectors = jnp.concatenate(vectors + [jnp.zeros((1, 50), F32)], axis=1)
     for i in range(4):
         pieces = []
         for h in range(3):
@@ -155,7 +164,7 @@
         pieces += [qw[:, 192 * i : 192 * i + 192], jnp.zeros((6, 64), F32)]
         zs[i, 0:6, :QKV] = jnp.concatenate(pieces, axis=1)
         zs[i, 0:6, QKV : QKV + UP] = uw[:, UP * i : UP * i + UP]
-        zs[i, 0:1, QKV + UP :] = sv_ref[0:1, :]
+        zs[i, 0:1, QKV + UP :] = vectors
 
     pl.semaphore_wait(bar, 10 + 4 * ((xhi + c) % 2))
 
@@ -175,9 +184,9 @@
         ga[z] = g_ref[...]
 
     zb[z] = zs[z]
-    j = ids((1, 1024), 1)
-    nat = jnp.where(j % 8 < 6, 192 * (j // 8 % 4) + 6 * (j // 32) + j % 8, -1)
-    s[...] = one_hot(ids((768, 1024), 0) == nat)
+    p, of = owner(ids((1, 768), 1))
+    nat = 192 * div(of, 6) + 6 * p + of - 6 * div(of, 6)
+    s[...] = one_hot(ids((768, 768), 0) == nat)
     i8 = ids((1, 256), 1)
     nat8 = jnp.where(i8 % 8 < 6, 6 * (i8 // 8) + i8 % 8, -1)
     for h in range(3):
@@ -186,21 +195,20 @@
 
     for d in zsends:
         d.wait()
-    big[0:32, :QKV] = zb[:, :, :QKV].reshape(32, QKV)
-    out8 = jnp.concatenate([ow_ref[0].astype(F32), jnp.zeros((2, 768), F32)], axis=0)
-    for i in range(3):
-        big[8 * i : 8 * i + 8, QKV:WQ] = out8[:, 256 * i : 256 * i + 256]
-    big[24:32, QKV:WQ] = jnp.zeros((8, 256), F32)
-    for i in range(4):
-        big[24 + i : 25 + i, QKV : QKV + 128] = zb[i, 0:1, QKV + UP :]
-    cq[...] = big[0:32, :WQ].astype(BF16)
-    cm[:, :UP] = zb[:, :, QKV : QKV + UP].reshape(32, UP).astype(BF16)
-    cm[:, UP:] = jnp.concatenate([dw_ref[0].astype(F32), jnp.zeros((8, 768), F32)], axis=0).astype(BF16)
+    rows = [zb[i, 0:6, :] for i in range(4)]
+    rows = jnp.concatenate(rows, axis=0)
+    out8 = ow_ref[0].astype(F32)
+    tails = [out8[i : i + 1, 640:] for i in range(6)]
+    row6 = jnp.concatenate(tails[:5], axis=1)
+    row7 = jnp.concatenate(tails[5:] + [zb[i, 0:1, QKV + UP :] for i in range(4)], axis=1)
+    cq[...] = jnp.concatenate([rows[:, :QKV], out8[:, :640], row6, row7], axis=0).astype(BF16)
+    cm[...] = jnp.concatenate([rows[:, QKV : QKV + UP], dw_ref[0].astype(F32)], axis=0).astype(BF16)
     wq[y, x, c] = cq[...]
     wm[y, x, c] = cm[...]
 
     class Ring:
-        def __init__(self, own, arr, s1, s2, s3s, rr, pr):
+        def __init__(self, own, arr, slot, one, two, s1, s2, s3s, rr, pr):
+            self.slot, self.one, self.two = slot, one, two
             self.own, self.arr, self.s1, self.s2, self.s3, self.rr, self.pr, self.sends = own, arr, s1, s2, s3s, rr, pr, []
 
         def send(self, src, yy, xx, ss, rs, to):
@@ -210,13 +218,13 @@
 
         def begin(self):
             for k in range(1, 4):
-                self.send(self.own, y, x, self.s1.at[k], self.rr.at[4 - k, 0], first[k])
+                self.send(self.own, y, x, self.s1.at[k], self.rr.at[4 - k, 0], self.one[k])
             for k in range(1, 4):
-                self.send(self.own, y, x, self.s2.at[0, k], self.rr.at[0, 4 - k], second[k])
+                self.send(self.own, y, x, self.s2.at[0, k], self.rr.at[0, 4 - k], self.two[k])
             self.send(self.own, y, x, self.s3.at[0, 0], self.pr.at[0, 0], partner)
 
         def arrived(self, k1, k2, rs, cc):
-            yy, xx = slot(k1, k2)
+            yy, xx = self.slot(k1, k2, cc)
             ref = self.arr.at[yy, xx, cc]
             rcopy(ref, ref, self.s3.at[k1, k2], rs, partner).wait_recv()
             return yy, xx
@@ -226,20 +234,20 @@
             src = self.arr.at[yy, xx, c]
             if on:
                 for k in range(1, 4):
-                    self.send(src, yy, xx, self.s2.at[k1, k], self.rr.at[k1, 4 - k], second[k])
+                    self.send(src, yy, xx, self.s2.at[k1, k], self.rr.at[k1, 4 - k], self.two[k])
             self.send(src, yy, xx, self.s3.at[k1, k2], self.pr.at[k1, k2], partner)
 
         def finish(self):
             for k1 in range(4):
                 for k2 in range(4):
-                    yy, xx = (y + k1 * (1 - c) + k2 * c) % 4, (x + k1 * c + k2 * (1 - c)) % 4
+                    yy, xx = self.slot(k1, k2, 1 - c)
                     ref = self.arr.at[yy, xx, 1 - c]
                     rcopy(ref, ref, self.s3.at[k1, k2], self.pr.at[k1, k2], partner).wait_recv()
             for d in self.sends:
                 d.wait_send()
 
-    rq = Ring(cq, wq, q1_s, q2_s, q3_s, qr_r, qp_r)
-    rm = Ring(cm, wm, m1_s, m2_s, m3_s, mr_r, mp_r)
+    rq = Ring(cq, wq, q_slot, first, second, q1_s, q2_s, q3_s, qr_r, qp_r)
+    rm = Ring(cm, wm, m_slot, ypeer, xpeer, m1_s, m2_s, m3_s, mr_r, mp_r)
     rq.begin()
 
     def spread_tokens(t, arr):
@@ -259,23 +267,36 @@
     gtok = spread_tokens(1, ga)
     for k1 in range(1, 4):
         rm.forward(k1, 0, True)
+
+    lane = ids((128, 128), 1) % 64
+    freq = jnp.exp((lane % 8).astype(F32) * np.float32(-2.0 / 16 * np.log(10000.0)))
+    freq = jnp.where(lane < 16, freq, 0.0)
+    yc = 2 * y + c
+    for i in range(4):
+        r = slice(128 * i, 128 * i + 128)
+        angle = ((8 * i + yc) * 128 + ids((128, 128), 0)).astype(F32) * freq
+        sin = jnp.sin(angle)
+        cos_ref[r, :] = jnp.cos(angle)
+        sp_ref[r, :] = jnp.where(lane >= 8, sin, 0.0)
+        sm_ref[r, :] = jnp.where(lane < 8, -sin, 0.0)
     for d in xtok:
         d.wait()
-
-    big[:, :1024] = mm(xa[...].reshape(512, 768), s[...])
+    big[:, :768] = mm(xa[...].reshape(512, 768), s[...])
     for k2 in range(1, 4):
         for k1 in range(4):
             rq.forward(k1, k2, False)
-    real = jnp.where(j % 8 < 6, 1.0, 0.0).astype(F32)
     for i in range(4):
         r = slice(128 * i, 128 * i + 128)
-        v = big[r, :1024]
-        mean = jnp.sum(v, axis=1, keepdims=True) * (1.0 / 768.0)
-        cen = (v - mean) * real
+        v = big[r, :768]
+        cen = v - jnp.sum(v, axis=1, keepdims=True) * (1.0 / 768.0)
         var = jnp.sum(cen * cen, axis=1, keepdims=True) * (1.0 / 768.0)
         xh[r, :] = cen * lax.rsqrt(var + 1e-5)
     rq.finish()
-    packed = wq[:, :, :, 24:32, QKV : QKV + 128].reshape(256, 128)
+    rest = wq[...].reshape(32, 32, QKV).astype(F32)
+    wqkv = rest[:, :24].reshape(768, QKV).astype(BF16)
+    rest = rest[:, 24:]
+    packed = [rest[:, 7:8, 128 + 128 * i : 256 + 128 * i] for i in range(4)] + [jnp.zeros((32, 4, 128), F32)]
+    packed = jnp.concatenate(packed, axis=1).reshape(256, 128).astype(BF16)
     norm_at, qkv_at, up_at, out_at = vector_places(z)
     for i in range(4):
         vec[i : i + 1, :] = spread(packed, norm_at[i])
@@ -284,11 +305,9 @@
         na[r, :] = (xh[r, :] * vec[0:1, :] + vec[1:2, :]).astype(BF16)
         nm[r, :] = (xh[r, :] * vec[2:3, :] + vec[3:4, :]).astype(BF16)
 
-    qkv = slice(1024, 1024 + QKV)
-    wqkv = wq[:, :, :, :, :QKV].reshape(1024, QKV)
-    big[:, qkv] = mm(na[...], wqkv) + spread(packed, qkv_at)
+    wn[...] = wqkv
+    big[:, 1024 : 1024 + QKV] = mm(na[...], wqkv) + spread(packed, qkv_at)
     low = ids((128, 128), 1) < 64
-    yc = 2 * y + c
     for i in range(4):
         r = slice(128 * i, 128 * i + 128)
         cos, plus, minus = cos_ref[r, :], sp_ref[r, :], sm_ref[r, :]
@@ -328,45 +347,15 @@
             rm.forward(k1, k2, False)
     for d in gtok:
         d.wait()
-    out8 = wq[:, :, :, :, QKV:WQ].reshape(32, 32, 256).astype(F32)
-    for i in range(3):
-        ow[:, 256 * i : 256 * i + 256] = out8[:, 8 * i : 8 * i + 8].reshape(256, 256).astype(BF16)
+    tails = [rest[:, 6:7, 128 * i : 128 * i + 128] for i in range(5)] + [rest[:, 7:8, :128], jnp.zeros((32, 2, 128), F32)]
+    ow[:, :640] = rest.reshape(256, 640).astype(BF16)
+    ow[:, 640:] = jnp.concatenate(tails, axis=1).reshape(256, 128).astype(BF16)
     g = ga[...].reshape(512, 768)
     dof = mm_nt(g, ow[...]).astype(BF16)
     for h in range(3):
         qd[h, 512:, :] = mm_nt(dof, s3[h]).astype(BF16)
+    pass_on(0)
     rm.finish()
-    dw[...] = wm[:, :, :, :, UP:].reshape(32, 32, 768).astype(F32)[:, :24].reshape(768, 768).astype(BF16)
-    wup = wm[:, :, :, :, :UP].reshape(1024, UP)
-    lanes = slice(2048, 2048 + UP)
-    big[:, lanes] = mm(nm[...], wup) + spread(packed, up_at)
-    pass_on(0)
-    for i in range(4):
-        r = slice(128 * i, 128 * i + 128)
-        u = big[r, lanes]
-        cdf = 0.5 * (1.0 + lax.erf(u * np.float32(np.sqrt(0.5))))
-        pdf = jnp.exp(-0.5 * u * u) * np.float32(1.0 / np.sqrt(2.0 * np.pi))
-        hid[r, :] = (u * cdf).astype(BF16)
-        big[r, lanes] = cdf + u * pdf
-    part[...] = mm(hid[...], dw[...])
-    du[...] = (mm_nt(g, dw[...]) * big[:, lanes]).astype(BF16)
-    pass_on(1)
-    dn = mm_nt(du[...], wup)
-    grads = [
-        jnp.sum(dn * xh[...], axis=0, keepdims=True),
-        jnp.sum(dn, axis=0, keepdims=True),
-        jnp.sum(du[...].astype(F32), axis=0, keepdims=True),
-    ]
-    dxh[...] = dn * vec[2:3, :]
-    small = collect(grads[0], norm_at[2]) + collect(grads[1], norm_at[3]) + collect(grads[2], up_at)
-    small += collect(jnp.sum(ga[z].astype(F32), axis=0, keepdims=True), out_at)
-    dwd = mm_tn(hid[...], g).reshape(32, 24, 768)
-    dwd = jnp.concatenate([dwd, jnp.zeros((32, 8, 768), F32)], axis=1).astype(BF16)
-    wm[:, :, :, :, UP:] = dwd.reshape(4, 4, 2, 32, 768)
-    wm[:, :, :, :, :UP] = mm_tn(nm[...], du[...]).astype(BF16).reshape(4, 4, 2, 32, UP)
-    msend = rcopy(wm.at[:, :, 1 - c], mb1, ma_s.at[0], ma_r.at[0], partner)
-    msend.start()
-    pass_on(2)
 
     msends = []
 
@@ -490,55 +479,87 @@
     kv_here(0)
     o0, d0 = attend(0, lambda: None)
     dkv_begin(0)
-    m_pairs()
+    pass_on(1)
+
+    w48 = wm[...].reshape(32, 48, 768).astype(F32)
+    dw[...] = w48[:, 24:].reshape(768, 768).astype(BF16)
+    wup = w48[:, :24].reshape(768, UP).astype(BF16)
+    lanes = slice(2048, 2048 + UP)
+    big[:, lanes] = mm(nm[...], wup) + spread(packed, up_at)
+    for i in range(4):
+        r = slice(128 * i, 128 * i + 128)
+        u = big[r, lanes]
+        cdf = 0.5 * (1.0 + lax.erf(u * np.float32(np.sqrt(0.5))))
+        pdf = jnp.exp(-0.5 * u * u) * np.float32(1.0 / np.sqrt(2.0 * np.pi))
+        hid[r, :] = (u * cdf).astype(BF16)
+        big[r, lanes] = cdf + u * pdf
+    part[...] = mm(hid[...], dw[...])
+    du[...] = (mm_nt(g, dw[...]) * big[:, lanes]).astype(BF16)
+    dn = mm_nt(du[...], wup)
+    grads = [
+        jnp.sum(dn * xh[...], axis=0, keepdims=True),
+        jnp.sum(dn, axis=0, keepdims=True),
+        jnp.sum(du[...].astype(F32), axis=0, keepdims=True),
+    ]
+    dxh[...] = dn * vec[2:3, :]
+    small = collect(grads[0], norm_at[2]) + collect(grads[1], norm_at[3]) + collect(grads[2], up_at)
+    small += collect(jnp.sum(ga[z].astype(F32), axis=0, keepdims=True), out_at)
+    dwu = mm_tn(nm[...], du[...]).reshape(32, 24, 768)
+    dwd = mm_tn(hid[...], g).reshape(32, 24, 768)
+    wm[...] = jnp.concatenate([dwu, dwd], axis=1).astype(BF16).reshape(4, 4, 2, 48, 768)
+    msend = rcopy(wm.at[:, :, 1 - c], mb1, ma_s.at[0], ma_r.at[0], partner)
+    msend.start()
+    pass_on(2)
+    dkv_pairs(0)
     kv_here(1)
-    o1, d1 = attend(1, lambda: dkv_pairs(0))
+    o1, d1 = attend(1, m_pairs)
     dkv_begin(1)
-    m_quads()
     kv_here(2)
     o2, d2 = attend(2, lambda: dkv_pairs(1))
     dkv_begin(2)
-    m_last()
 
     att[...] = (o0 + o1 + o2).astype(BF16)
     outs = part[...] + mm(att[...], ow[...]) + spread(packed, out_at) * jnp.where(z == 0, 1.0, 0.0)
     outp[...] = outs.astype(BF16).reshape(4, 128, 768)
-    toks = []
-    for t, (src, dst) in enumerate(((outp, ro), (dxp, rd))):
-        toks.append([rcopy(src.at[(z + k) % 4], dst.at[z], t_s.at[t, k], t_r.at[t, k], home[k]) for k in range(4)])
-    stays = [pltpu.make_async_copy(outp.at[z], ro.at[z], loc.at[0]), pltpu.make_async_copy(dxp.at[z], rd.at[z], loc.at[1])]
-
-    def send_back(t):
-        for k in range(1, 4):
-            toks[t][k].start()
-
-        @pl.when(swapped)
-        def _():
-            toks[t][0].start()
-
-        @pl.when(xhi == c)
-        def _():
-            stays[t].start()
-
-    send_back(0)
+    osends = [rcopy(outp.at[(z + k) % 4], obuf.at[z], o_s.at[k], o_r.at[4 - k], zpeer[k]) for k in range(1, 4)]
+    for d in osends:
+        d.start()
     dkv_pairs(2)
     dwo = mm_tn(att[...], g).reshape(32, 8, 768)
     for i in range(4):
         r = slice(128 * i, 128 * i + 128)
         back_tile(i, 384, jnp.where(low, d0[r], pltpu.roll(d1[r], 64, 1)), False)
         back_tile(i, 512, jnp.where(low, d2[r], 0.0), False)
-    for h in range(3):
+    dkv_last(0)
+    for d in osends:
+        d.wait()
+    obuf[z] = outp[z]
+    outs = obuf[0].astype(F32) + obuf[1].astype(F32) + obuf[2].astype(F32) + obuf[3].astype(F32)
+    outp[0] = (xa[z].astype(F32) + outs).astype(BF16)
+    out_swap = rcopy(outp.at[0], ro, o_s.at[0], o_r.at[0], home[0])
+    out_stay = pltpu.make_async_copy(outp.at[0], ro, loc.at[0])
+
+    @pl.when(swapped)
+    def _():
+        out_swap.start()
+
+    @pl.when(xhi == c)
+    def _():
+        out_stay.start()
+
+    m_quads()
+    for h in (1, 2):
         dkv_last(h)
     dqb = jnp.sum(dqkv[...].astype(F32), axis=0, keepdims=True)
-    dn = mm_nt(dqkv[...], wqkv)
+    dn = mm_nt(dqkv[...], wn[...])
     small += collect(jnp.sum(dn * xh[...], axis=0, keepdims=True), norm_at[0])
     small += collect(jnp.sum(dn, axis=0, keepdims=True), norm_at[1]) + collect(dqb, qkv_at)
     dx = (dxh[...] + dn * vec[0:1, :]).astype(BF16)
-    dwq = mm_tn(na[...], dqkv[...]).astype(BF16)
-    wq[:, :, :, :, :QKV] = dwq.reshape(4, 4, 2, 32, QKV)
-    last = jnp.concatenate([small.reshape(32, 8, 128), jnp.zeros((32, 8, 128), F32)], axis=2)
-    tail = jnp.concatenate([dwo[:, :, :256], dwo[:, :, 256:512], dwo[:, :, 512:], last], axis=1)
-    wq[:, :, :, :, QKV:] = tail.astype(BF16).reshape(4, 4, 2, 32, 256)
+    dwq = mm_tn(na[...], dqkv[...]).reshape(32, 24, QKV)
+    small = small.reshape(32, 8, 128)
+    row6 = jnp.concatenate([dwo[:, i : i + 1, 640:] for i in range(5)], axis=2)
+    row7 = jnp.concatenate([dwo[:, 5:6, 640:]] + [small[:, i : i + 1] for i in range(4)], axis=2)
+    wq[...] = jnp.concatenate([dwq, dwo[:, :6, :640], row6, row7], axis=1).astype(BF16).reshape(4, 4, 2, 32, QKV)
 
     def qslot(k1, k2, cc):
         return (y + k1 * (1 - cc) + k2 * cc) % 4, (x + k1 * cc + k2 * (1 - cc)) % 4
@@ -551,7 +572,19 @@
         d.start()
         qsends.append(d)
     dxp[...] = mm_nt(dx, s[...]).astype(BF16).reshape(4, 128, 768)
-    send_back(1)
+    toks = [rcopy(dxp.at[(z + k) % 4], rd.at[z], t_s.at[k], t_r.at[k], home[k]) for k in range(4)]
+    stay = pltpu.make_async_copy(dxp.at[z], rd.at[z], loc.at[1])
+    for k in range(1, 4):
+        toks[k].start()
+
+    @pl.when(swapped)
+    def _():
+        toks[0].start()
+
+    @pl.when(xhi == c)
+    def _():
+        stay.start()
+
     for k1, k2 in order:
         yy, xx = qslot(k1, k2, c)
         rcopy(wq.at[yy, xx, c], qb1.at[k1, k2], qa_s.at[k1, k2], qa_r.at[k1, k2], partner).wait_recv()
@@ -571,37 +604,39 @@
             qsends.append(d)
     for k in range(1, 4):
         rcopy(qquad.at[k], qb3.at[k], qc_s.at[k], qc_r.at[k], partner).wait_recv()
+    m_last()
     total = total + qb3[1].astype(F32) + qb3[2].astype(F32) + qb3[3].astype(F32)
-    zs[:, :, :QKV] = total[:, :QKV].reshape(4, 8, QKV)
-    zs[:, :, QKV : QKV + UP] = fm[:, :UP].reshape(4, 8, UP)
-    for i in range(4):
-        zs[i, 0:1, QKV + UP :] = total[24 + i : 25 + i, QKV : QKV + 128]
+    for i in range(4):
+        zs[i, 0:6, :QKV] = total[6 * i : 6 * i + 6]
+        zs[i, 0:6, QKV : QKV + UP] = fm[6 * i : 6 * i + 6, :]
+        zs[i, 0:1, QKV + UP :] = total[31:32, 128 + 128 * i : 256 + 128 * i]
     zsends = [rcopy(zs.at[(z + k) % 4], zr.at[z], ze_s.at[k], ze_r.at[4 - k], zpeer[k]) for k in range(1, 4)]
     for d in zsends:
         d.start()
     zr[z] = zs[z]
-    dn_out[...] = fm[:, UP:]
-    o8_out[...] = jnp.concatenate([total[0:8, QKV:], total[8:16, QKV:], total[16:24, QKV:]], axis=1)
+    dn_out[...] = fm[24:, :]
+    o8_out[...] = total[24:32]
 
     for d in qsends + msends + ysends + halves + kvsends + [msend]:
         d.wait_send()
-    for t in range(2):
-        for k in range(1, 4):
-            toks[t][k].wait()
-
-        @pl.when(swapped)
-        def _():
-            toks[t][0].wait()
-
-        @pl.when(xhi == c)
-        def _():
-            stays[t].wait()
+    for k in range(1, 4):
+        toks[k].wait()
+
+    @pl.when(swapped)
+    def _():
+        out_swap.wait()
+        toks[0].wait()
+
+    @pl.when(xhi == c)
+    def _():
+        out_stay.wait()
+        stay.wait()
 
     for d in zsends:
         d.wait()
 
 
-def layer(x, g, qw, uw, ow, dw, sv, cos, plus, minus):
+def layer(*args):
     sh = jax.ShapeDtypeStruct
 
     def vm(*shape, dtype=BF16):
@@ -612,30 +647,30 @@
 
     tok = (4, 128, 768)
     scratch = [
-        vm(*tok), vm(*tok), vm(4, 4, 2, 32, WQ), vm(4, 4, 2, 32, WM), vm(4, 8, ZW, dtype=F32), vm(4, 8, ZW, dtype=F32),
-        vm(32, WQ), vm(32, WM), vm(768, 1024), vm(3, 128, 256), vm(512, 4096, dtype=F32), vm(512, 1024, dtype=F32),
-        vm(512, 1024), vm(512, 1024), vm(8, 1024, dtype=F32), vm(3, 4, 8, 128, 128), vm(3, 1024, 128),
-        vm(3, 4, 4, 2, 128, 128), vm(512, 768), vm(512, 768), vm(512, 768, dtype=F32), vm(512, 1024, dtype=F32),
-        vm(256, 768), vm(768, 768), vm(512, 256), vm(512, QKV), vm(*tok), vm(*tok), vm(32, WM, dtype=F32),
-    ] + [vm(512, 128, dtype=F32)] * 4 + [
+        vm(*tok), vm(*tok), vm(4, 4, 2, 32, QKV), vm(4, 4, 2, 48, 768), vm(4, 8, ZW, dtype=F32), vm(4, 8, ZW, dtype=F32),
+        vm(32, QKV), vm(48, 768), vm(768, 768), vm(3, 128, 256), vm(512, 4096, dtype=F32), vm(512, 768, dtype=F32),
+        vm(512, 768), vm(512, 768), vm(8, 768, dtype=F32), vm(3, 4, 8, 128, 128), vm(3, 1024, 128),
+        vm(3, 4, 4, 2, 128, 128), vm(512, 768), vm(512, 768), vm(512, 768, dtype=F32), vm(512, 768, dtype=F32),
+        vm(256, 768), vm(768, 768), vm(768, QKV), vm(512, 256), vm(512, QKV), vm(*tok), vm(*tok), vm(*tok), vm(48, 768, dtype=F32),
+    ] + [vm(512, 128, dtype=F32)] * 7 + [
         vm(3, 4, 4, 128, 128), vm(3, 4, 4, 128, 128), vm(3, 4, 4, 128, 128),
-        vm(4, 4, 32, WM), vm(4, 4, 32, WM), vm(4, 4, 32, WM), vm(4, 32, WM), vm(4, 32, WM),
-        vm(4, 4, 32, WQ), vm(4, 4, 32, WQ), vm(4, 4, 32, WQ), vm(4, 32, WQ), vm(4, 32, WQ),
+        vm(4, 4, 48, 768), vm(4, 4, 48, 768), vm(4, 4, 48, 768), vm(4, 48, 768), vm(4, 48, 768),
+        vm(4, 4, 32, QKV), vm(4, 4, 32, QKV), vm(4, 4, 32, QKV), vm(4, 32, QKV), vm(4, 32, QKV),
         sem(2), sem(2), sem(2), sem(2, 4), sem(2, 4), sem(4), sem(4),
         sem(4), sem(4, 4), sem(4, 4), sem(4, 4), sem(4, 4), sem(4), sem(4, 4), sem(4, 4), sem(4, 4), sem(4, 4),
         sem(3, 4), sem(3, 4), sem(3, 4), sem(3, 4), sem(3), sem(3), sem(3, 4), sem(3, 4),
         sem(1), sem(1), sem(4), sem(4), sem(4), sem(4), sem(4, 4), sem(4, 4), sem(4, 4), sem(4, 4), sem(4), sem(4),
-        sem(2, 4), sem(2, 4), sem(4), sem(4),
+        sem(4), sem(4), sem(4), sem(4), sem(4), sem(4),
     ]
     return pl.pallas_call(
         layer_kernel,
-        out_shape=(sh(tok, BF16), sh(tok, BF16), sh((4, 8, ZW), F32), sh((32, 768), F32), sh((8, 768), F32)),
-        in_specs=[VMEM] * 10,
+        out_shape=(sh((128, 768), BF16), sh(tok, BF16), sh((4, 8, ZW), F32), sh((24, 768), F32), sh((8, 640), F32)),
+        in_specs=[VMEM] * 14,
         out_specs=(HBM, HBM, VMEM, VMEM, VMEM),
         scratch_shapes=scratch,
         compiler_params=pltpu.CompilerParams(vmem_limit_bytes=63 * MIB, collective_id=0, has_side_effects=True),
         name="layer",
-    )(x, g, qw, uw, ow, dw, sv, cos, plus, minus)
+    )(*args)
 
 
 CUTS = (0, 18, 24, 48, 54, 60, 66, 72, 78)
@@ -644,8 +679,7 @@
 def finish_kernel(x_ref, g_ref, ro, rd, zr, dn, o8, *outs):
     out, dx_out, qkv, up, out_w, down = outs[:6]
     xf = x_ref[...].astype(F32)
-    total = ro[0].astype(F32) + ro[1].astype(F32) + ro[2].astype(F32) + ro[3].astype(F32)
-    out[0] = (xf + total).astype(BF16)
+    out[0] = ro[...]
     dxh = rd[0].astype(F32) + rd[1].astype(F32) + rd[2].astype(F32) + rd[3].astype(F32)
     cen = xf - jnp.mean(xf, axis=1, keepdims=True)
     rstd = lax.rsqrt(jnp.mean(cen * cen, axis=1, keepdims=True) + 1e-5)
@@ -655,10 +689,11 @@
     pieces = [zr[i, 0:6, 384:576] for i in range(4)]
     pieces += [zr[i, 0:6, 128 * h : 128 * h + 64] for i in range(4) for h in range(3)]
     pieces += [zr[i, 0:6, 128 * h + 64 : 128 * h + 128] for i in range(4) for h in range(3)]
-    qkv[0] = jnp.concatenate(pieces, axis=1)
-    up[0] = jnp.concatenate([zr[i, 0:6, QKV : QKV + UP] for i in range(4)], axis=1)
-    out_w[0] = o8[0:6, :]
-    down[0] = dn[0:24, :]
+    qkv[:, 0, :] = jnp.concatenate(pieces, axis=1)
+    up[:, 0, :] = jnp.concatenate([zr[i, 0:6, QKV : QKV + UP] for i in range(4)], axis=1)
+    tails = [o8[6:7, 128 * i : 128 * i + 128] for i in range(5)] + [o8[7:8, :128]]
+    out_w[:, 0, :] = jnp.concatenate([o8[0:6, :], jnp.concatenate(tails, axis=0)], axis=1)
+    down[0] = dn[...]
     rows = sum(zr[i, 0:1, QKV + UP :] for i in range(4))
     for ref, a, b in zip(outs[6:], CUTS[:-1], CUTS[1:]):
         ref[...] = rows[:, a:b]
@@ -668,7 +703,7 @@
     def sh(*shape, dtype=F32):
         return jax.ShapeDtypeStruct(shape, dtype)
 
-    shapes = [sh(1, 128, 768, dtype=BF16), sh(1, 128, 768), sh(1, 6, 2304), sh(1, 6, 3072), sh(1, 6, 768), sh(1, 24, 768)]
+    shapes = [sh(1, 128, 768, dtype=BF16), sh(1, 128, 768), sh(6, 1, 2304), sh(6, 1, 3072), sh(6, 1, 768), sh(1, 24, 768)]
     shapes += [sh(1, b - a) for a, b in zip(CUTS[:-1], CUTS[1:])]
     return pl.pallas_call(
         finish_kernel,
@@ -680,28 +715,15 @@
     )(*args)
 
 
-def rotary(first_block):
-    f = 10000.0 ** (-2.0 * jnp.arange(8, dtype=F32) / 16)
-    lane = np.arange(128) % 64
-    freq = jnp.where(lane < 16, jnp.tile(f, 16), 0.0)
-    pos = (first_block * 128 + 1024 * jnp.arange(4)[:, None] + jnp.arange(128)[None, :]).reshape(512).astype(F32)
-    angle = pos[:, None] * freq[None, :]
-    sin = jnp.sin(angle)
-    return jnp.cos(angle), jnp.where(lane >= 8, sin, 0.0), jnp.where(lane < 8, -sin, 0.0)
-
-
 def body(
     inputs, qkv_weight, qkv_bias, out_weight, out_bias, up_weight, up_bias, down_weight, down_bias,
     attn_gain, attn_shift, mlp_gain, mlp_shift, cotangent,
 ):
-    z, y, xh, xl, c = place()
     x, g = inputs[0], cotangent[0]
     vectors = (qkv_bias, out_bias, up_bias, down_bias, attn_gain, attn_shift, mlp_gain, mlp_shift)
-    sv = jnp.concatenate([v[0] for v in vectors] + [jnp.zeros((50,), BF16)]).astype(F32)
-    sv = jnp.broadcast_to(sv[None], (8, 128))
-    cos, plus, minus = rotary(2 * y + c)
-    ro, rd, zr, dn, o8 = layer(x, g, qkv_weight, up_weight, out_weight, down_weight, sv, cos, plus, minus)
+    ro, rd, zr, dn, o8 = layer(x, g, qkv_weight, up_weight, out_weight, down_weight, *vectors)
     out, dx, qkv, up, ow, dw, *t = finish(x, g, ro, rd, zr, dn, o8)
+    qkv, up, ow = qkv.transpose(1, 0, 2), up.transpose(1, 0, 2), ow.transpose(1, 0, 2)
     return out, dx, qkv, t[0], ow, t[1], up, t[2], dw, t[3], t[4], t[5], t[6], t[7]
 
 

time: 135 us -> 106 us (0.79)
  Pallas kernels: 127 us -> 105 us
  local copies, waits for them, and re-layouts: 5.78 us -> 0 us
  other arithmetic: 1.95 us -> 0 us
    pallas_call x1, Pallas kernels: 124 us -> 102 us  [layer(): pl.pallas_call(layer_kernel, out_shape=(sh((128, 768), BF16), sh(tok, BF1...]
    unnamed x29 -> x0, local copies, waits for them, and re-layouts: 4.99 us -> none
    select_n x2 -> x0, other arithmetic: 1.87 us -> none  [the longest x1 1.86 us: rotary(): jnp.where(lane < 8, -sin, 0.0)]
where the time goes in v3:
time: 106 us
  Pallas kernels  105 us (99%)
    pallas_call x1, Pallas kernels, layer(): pl.pallas_call(layer_kernel, out_shape=(sh((128, 768), BF16), sh(tok, BF1...  102 us
    pallas_call x1, Pallas kernels, finish(): pl.pallas_call(finish_kernel, out_shape=tuple(shapes), in_specs=[VMEM] *...  2.69 us

profile of v3, /device:TPU:1, one launch (start us, length us, event | category | flops | bytes accessed | tf_op | source)
XLA Modules:
  0.0 105.5 jit_solution(17494147832721849446)
XLA Ops:
  0.6 102.0 %layer.1 = (bf16[128,768]{1,0:T(8,128)(2,1)}, bf16[4,128,768]{2,1,0:T(8,128)(2,1)}, f32[4,8,1536]{2,1,0:T(8,128)}, f32[24,768]{1,0:T(8,128)}, f32[8,640]{1,0:T(8,128)}) custom-call(bf16[128,768]{1,0:T(8,128)(2,1)} %bitcast.5, bf16[128,768]{1,0:T(8,128)(2,1)} %bitcast.7, bf16[1,6,2304]{2,1,0:T(8,128)(2,1)} %qw_ref.1, bf16[1,6,3072]{2,1,0:T(8,128)(2,1)} %uw_ref.1, ...), custom_call_target="tpu_custom_call" | custom-call | tf_op jit(solution)/shard_map/layer/pallas_call | solution.py:665
  102.7 2.7 %finish.1 = (bf16[1,128,768]{2,1,0:T(8,128)(2,1)}, f32[1,128,768]{2,1,0:T(8,128)}, f32[6,1,2304]{2,1,0:T(1,128)}, f32[6,1,3072]{2,1,0:T(1,128)}, f32[6,1,768]{2,...) custom-call(bf16[128,768]{1,0:T(8,128)(2,1)} %bitcast.6, ...), custom_call_target="tpu_custom_call" | custom-call | tf_op jit(solution)/shard_map/finish/pallas_call | solution.py:708

commit v4 on v3

--- a/solution.py
+++ b/solution.py
@@ -16,6 +16,8 @@
 MIB = 1024 * 1024
 
 QKV, UP = 640, 768
+EARLY = 512
+KV_AT, Q_AT = (0, 128, 512), 256
 ZW = QKV + UP + 128
 OFF = -1e30
 
@@ -74,11 +76,12 @@
     p, of = owner(j)
     norms = [(8 * p + div(of, 6), [at + of - 6 * div(of, 6)]) for at in (54, 60, 66, 72)]
     m = ids((1, QKV), 1)
-    is_kv = m < 384
-    kind = jnp.where(is_kv, jnp.where(m % 128 < 64, 1, 2), 0)
-    col = kind * 768 + 192 * z + jnp.where(is_kv, 64 * (m // 128) + m % 64, m - 384)
+    is_q = (m >= Q_AT) & (m < EARLY)
+    kind = jnp.where(is_q, 0, jnp.where(m % 128 < 64, 1, 2))
+    head = jnp.where(m < EARLY, m // 128, 2)
+    col = kind * 768 + 192 * z + jnp.where(is_q, m - Q_AT, 64 * head + m % 64)
     own = div(col, 18)
-    qkv = ((own % 32) * 8 + own // 32, [jnp.where(m < 576, col - 18 * own, -1)])
+    qkv = ((own % 32) * 8 + own // 32, [jnp.where(is_q & (m >= Q_AT + 192), -1, col - 18 * own)])
     f = ids((1, UP), 1)
     p = div(f, 24)
     up = (p * 8 + z, [24 + f - 24 * p])
@@ -118,12 +121,13 @@
     x_ref, g_ref, qw_ref, uw_ref, ow_ref, dw_ref, v0, v1, v2, v3, v4, v5, v6, v7,
     ro, rd, zr, dn_out, o8_out,
     xa, ga, wq, wm, zs, zb, cq, cm, s, s3, big, xh, na, nm, vec, kv, qd, dkv, hid, du, part, dxh,
-    ow, dw, wn, att, dqkv, outp, obuf, dxp, fm, cos_ref, sp_ref, sm_ref, top, tot, acc, delta,
-    kb1, kpair, kb2, mb1, mpair, mb2, mquad, mb3, qb1, qpair, qb2, qquad, qb3,
+    ow, dw, wn, att, dqkv, outp, obuf, dxp, cos_ref, sp_ref, sm_ref, top, tot, acc, delta,
+    kb1, kpair, kb2, mb1, mpair, mb2, mquad, mb3, eb1, epair, eb2, equad, eb3, lb1, lpair, lb2, lquad, lb3,
     swap_s, swap_r, loc, tz_s, tz_r, wz_s, wz_r,
     q1_s, q2_s, q3_s, qr_r, qp_r, m1_s, m2_s, m3_s, mr_r, mp_r,
-    ky_s, ky_r, kp_s, kp_r, dp_s, dp_r, dy_s, dy_r,
-    ma_s, ma_r, mb_s, mb_r, mc_s, mc_r, qa_s, qa_r, qb_s, qb_r, qc_s, qc_r, t_s, t_r, o_s, o_r, ze_s, ze_r,
+    ky_s, ky_r, kh_s, kh_r, kp_s, kp_r, dp_s, dp_r, dy_s, dy_r,
+    ma_s, ma_r, mb_s, mb_r, mc_s, mc_r, ea_s, ea_r, eb_s, eb_r, ec_s, ec_r, la_s, la_r, lb_s, lb_r, lc_s, lc_r,
+    t_s, t_r, o_s, o_r, ze_s, ze_r,
 ):
     z, y, xhi, xl, c = place()
     x = xhi * 2 + xl
@@ -139,9 +143,6 @@
     def q_slot(k1, k2, cc):
         return (y + k1 * cc + k2 * (1 - cc)) % 4, (x + k1 * (1 - cc) + k2 * cc) % 4
 
-    def m_slot(k1, k2, cc):
-        return (y + k1) % 4, (x + k2) % 4
-
     bar = pltpu.get_barrier_semaphore()
     for to in zpeer[1:] + ypeer[1:] + xpeer[1:] + [partner]:
         pl.semaphore_signal(bar, inc=1, device_id=to, device_id_type=MESH)
@@ -161,7 +162,7 @@
         for h in range(3):
             at = 192 * i + 64 * h
             pieces += [qw[:, 768 + at : 832 + at], qw[:, 1536 + at : 1600 + at]]
-        pieces += [qw[:, 192 * i : 192 * i + 192], jnp.zeros((6, 64), F32)]
+        pieces[4:4] = [qw[:, 192 * i : 192 * i + 192], jnp.zeros((6, 64), F32)]
         zs[i, 0:6, :QKV] = jnp.concatenate(pieces, axis=1)
         zs[i, 0:6, QKV : QKV + UP] = uw[:, UP * i : UP * i + UP]
         zs[i, 0:1, QKV + UP :] = vectors
@@ -247,7 +248,7 @@
                 d.wait_send()
 
     rq = Ring(cq, wq, q_slot, first, second, q1_s, q2_s, q3_s, qr_r, qp_r)
-    rm = Ring(cm, wm, m_slot, ypeer, xpeer, m1_s, m2_s, m3_s, mr_r, mp_r)
+    rm = Ring(cm, wm, q_slot, first, second, m1_s, m2_s, m3_s, mr_r, mp_r)
     rq.begin()
 
     def spread_tokens(t, arr):
@@ -313,38 +314,47 @@
         cos, plus, minus = cos_ref[r, :], sp_ref[r, :], sm_ref[r, :]
         kc, kp, km = jnp.where(low, cos, 1.0), jnp.where(low, plus, 0.0), jnp.where(low, minus, 0.0)
         for h in range(3):
-            kv[h, i, yc] = turn(big[r, 1024 + 128 * h : 1152 + 128 * h], kc, kp, km).astype(BF16)
-        q01 = turn(big[r, 1408:1536], cos, plus, minus).astype(BF16).astype(F32) * 0.125
-        q2 = turn(big[r, 1536:1664], cos, plus, minus).astype(BF16).astype(F32) * 0.125
+            kv[h, i, yc] = turn(big[r, 1024 + KV_AT[h] : 1152 + KV_AT[h]], kc, kp, km).astype(BF16)
+        q01 = turn(big[r, 1024 + Q_AT : 1152 + Q_AT], cos, plus, minus).astype(BF16).astype(F32) * 0.125
+        q2 = turn(big[r, 1152 + Q_AT : 1280 + Q_AT], cos, plus, minus).astype(BF16).astype(F32) * 0.125
         qd[0, r, :] = jnp.where(low, q01, 0.0).astype(BF16)
         qd[1, r, :] = jnp.where(low, pltpu.roll(q01, 64, 1), 0.0).astype(BF16)
         qd[2, r, :] = jnp.where(low, q2, 0.0).astype(BF16)
 
     kvsends = []
+
+    def kv_send(src, ss, rs, to):
+        d = rcopy(src, src, ss, rs, to)
+        d.start()
+        kvsends.append(d)
+
     for h in range(3):
         mine = kv.at[h, :, yc]
-        ds = [rcopy(mine, mine, ky_s.at[h, k], ky_r.at[h, 4 - k], ypeer[k]) for k in range(1, 4)]
-        ds.append(rcopy(mine, mine, kp_s.at[h, 0], kp_r.at[h, 0], partner))
-        for d in ds:
-            d.start()
-        kvsends += ds
+        kv_send(mine, ky_s.at[h, 1], ky_r.at[h, 3], ypeer[1])
+        kv_send(mine, ky_s.at[h, 3], ky_r.at[h, 1], ypeer[3])
+        kv_send(mine, kp_s.at[h, 0], kp_r.at[h, 0], partner)
 
     def pass_on(h):
-        for k in (1, 3, 2):
-            there = kv.at[h, :, 2 * ((y + k) % 4) + c]
+        for k in (1, 3):
+            at = 2 * ((y + k) % 4) + c
+            there = kv.at[h, :, at]
             rcopy(there, there, ky_s.at[h, k], ky_r.at[h, k], partner).wait_recv()
-            d = rcopy(there, there, kp_s.at[h, k], kp_r.at[h, k], partner)
-            d.start()
-            kvsends.append(d)
+            part_of = kv.at[h, 0:2, at] if k == 3 else kv.at[h, 2:4, at]
+            kv_send(part_of, kh_s.at[h, k], kh_r.at[h, k], ypeer[4 - k])
+            kv_send(there, kp_s.at[h, k], kp_r.at[h, k], partner)
+
+    def pass_far(h):
+        at = 2 * ((y + 2) % 4) + c
+        for k in (1, 3):
+            part_of = kv.at[h, 0:2, at] if k == 3 else kv.at[h, 2:4, at]
+            rcopy(part_of, part_of, kh_s.at[h, k], kh_r.at[h, k], partner).wait_recv()
+        kv_send(kv.at[h, :, at], kp_s.at[h, 2], kp_r.at[h, 2], partner)
 
     def kv_here(h):
         for k in range(4):
             there = kv.at[h, :, 2 * ((y + k) % 4) + 1 - c]
             rcopy(there, there, kp_s.at[h, k], kp_r.at[h, k], partner).wait_recv()
 
-    for k2 in range(1, 4):
-        for k1 in range(4):
-            rm.forward(k1, k2, False)
     for d in gtok:
         d.wait()
     tails = [rest[:, 6:7, 128 * i : 128 * i + 128] for i in range(5)] + [rest[:, 7:8, :128], jnp.zeros((32, 2, 128), F32)]
@@ -354,41 +364,100 @@
     dof = mm_nt(g, ow[...]).astype(BF16)
     for h in range(3):
         qd[h, 512:, :] = mm_nt(dof, s3[h]).astype(BF16)
+    for k2 in range(1, 4):
+        for k1 in range(4):
+            rm.forward(k1, k2, False)
     pass_on(0)
     rm.finish()
-
-    msends = []
-
-    def m_pairs():
-        msend.wait_recv()
-        for k in range(1, 4):
-            xx = (x + k) % 4
-            for yy in range(4):
-                mpair[k, yy] = (wm[yy, xx, c].astype(F32) + mb1[yy, xx].astype(F32)).astype(BF16)
-            d = rcopy(mpair.at[k], mb2.at[4 - k], mb_s.at[k], mb_r.at[4 - k], xpeer[k])
-            d.start()
-            msends.append(d)
-        for yy in range(4):
-            mpair[0, yy] = (wm[yy, x, c].astype(F32) + mb1[yy, x].astype(F32)).astype(BF16)
-
-    def m_quads():
-        for k in range(1, 4):
-            rcopy(mpair.at[k], mb2.at[k], mb_s.at[k], mb_r.at[k], partner).wait_recv()
-        for k in (1, 2, 3, 0):
-            yy = (y + k) % 4
-            total = mpair[0, yy].astype(F32) + mb2[1, yy].astype(F32) + mb2[2, yy].astype(F32) + mb2[3, yy].astype(F32)
-            if k:
-                mquad[k] = total.astype(BF16)
-                d = rcopy(mquad.at[k], mb3.at[4 - k], mc_s.at[k], mc_r.at[4 - k], ypeer[k])
+    pass_on(1)
+
+    class Sum:
+        def __init__(self, arr, lanes, y_first, b1, pair, b2, quad, b3, sems):
+            self.arr, self.lanes, self.b1, self.pair, self.b2, self.quad, self.b3 = arr, lanes, b1, pair, b2, quad, b3
+            self.as_, self.ar, self.bs, self.br, self.cs, self.cr = sems
+            self.sends, self.y_first = [], y_first
+            self.one_peer, self.two_peer = (ypeer, xpeer) if y_first else (xpeer, ypeer)
+
+        def begin(self):
+            src = self.arr.at[:, :, 1 - c, :, self.lanes]
+            self.sends.append(rcopy(src, self.b1, self.as_.at[0], self.ar.at[0], partner))
+            self.sends[0].start()
+
+        def one(self, k1, k2):
+            yy, xx = ((y + k1) % 4, (x + k2) % 4) if self.y_first else ((y + k2) % 4, (x + k1) % 4)
+            return (self.arr[yy, xx, c, :, self.lanes].astype(F32) + self.b1[yy, xx].astype(F32)).astype(BF16)
+
+        def pairs(self):
+            self.sends[0].wait_recv()
+            for k in (2, 1, 3):
+                for k2 in range(4):
+                    self.pair[k, k2] = self.one(k, k2)
+                d = rcopy(self.pair.at[k], self.b2.at[4 - k], self.bs.at[k], self.br.at[4 - k], self.one_peer[k])
                 d.start()
-                msends.append(d)
-            else:
-                fm[...] = total
-
-    def m_last():
-        for k in range(1, 4):
-            rcopy(mquad.at[k], mb3.at[k], mc_s.at[k], mc_r.at[k], partner).wait_recv()
-        fm[...] += mb3[1].astype(F32) + mb3[2].astype(F32) + mb3[3].astype(F32)
+                self.sends.append(d)
+            for k2 in range(4):
+                self.pair[0, k2] = self.one(0, k2)
+
+        def quads(self):
+            for k in range(1, 4):
+                rcopy(self.pair.at[k], self.b2.at[k], self.bs.at[k], self.br.at[k], partner).wait_recv()
+            for k in (2, 1, 3, 0):
+                total = self.pair[0, k].astype(F32)
+                for i in range(1, 4):
+                    total += self.b2[i, k].astype(F32)
+                if k:
+                    self.quad[k] = total.astype(BF16)
+                    d = rcopy(self.quad.at[k], self.b3.at[4 - k], self.cs.at[k], self.cr.at[4 - k], self.two_peer[k])
+                    d.start()
+                    self.sends.append(d)
+            self.mine = total
+
+        def last(self):
+            total = self.mine
+            for k in range(1, 4):
+                rcopy(self.quad.at[k], self.b3.at[k], self.cs.at[k], self.cr.at[k], partner).wait_recv()
+                total += self.b3[k].astype(F32)
+            return total
+
+        def drain(self):
+            for d in self.sends:
+                d.wait_send()
+
+    sum_m = Sum(wm, slice(0, 768), False, mb1, mpair, mb2, mquad, mb3, (ma_s, ma_r, mb_s, mb_r, mc_s, mc_r))
+    sum_e = Sum(wq, slice(0, EARLY), True, eb1, epair, eb2, equad, eb3, (ea_s, ea_r, eb_s, eb_r, ec_s, ec_r))
+    sum_l = Sum(wq, slice(EARLY, QKV), True, lb1, lpair, lb2, lquad, lb3, (la_s, la_r, lb_s, lb_r, lc_s, lc_r))
+
+    w48 = wm[...].reshape(32, 48, 768).astype(F32)
+    dw[...] = w48[:, 24:].reshape(768, 768).astype(BF16)
+    wup = w48[:, :24].reshape(768, UP).astype(BF16)
+    lanes = slice(2048, 2048 + UP)
+    big[:, lanes] = mm(nm[...], wup) + spread(packed, up_at)
+    pass_far(0)
+    pass_on(2)
+    for i in range(4):
+        r = slice(128 * i, 128 * i + 128)
+        u = big[r, lanes]
+        cdf = 0.5 * (1.0 + lax.erf(u * np.float32(np.sqrt(0.5))))
+        pdf = jnp.exp(-0.5 * u * u) * np.float32(1.0 / np.sqrt(2.0 * np.pi))
+        hid[r, :] = (u * cdf).astype(BF16)
+        big[r, lanes] = cdf + u * pdf
+    part[...] = mm(hid[...], dw[...])
+    du[...] = (mm_nt(g, dw[...]) * big[:, lanes]).astype(BF16)
+    pass_far(1)
+    dn = mm_nt(du[...], wup)
+    grads = [
+        jnp.sum(dn * xh[...], axis=0, keepdims=True),
+        jnp.sum(dn, axis=0, keepdims=True),
+        jnp.sum(du[...].astype(F32), axis=0, keepdims=True),
+    ]
+    dxh[...] = dn * vec[2:3, :]
+    small = collect(grads[0], norm_at[2]) + collect(grads[1], norm_at[3]) + collect(grads[2], up_at)
+    small += collect(jnp.sum(ga[z].astype(F32), axis=0, keepdims=True), out_at)
+    dwu = mm_tn(nm[...], du[...]).reshape(32, 24, 768)
+    dwd = mm_tn(hid[...], g).reshape(32, 24, 768)
+    wm[...] = jnp.concatenate([dwu, dwd], axis=1).astype(BF16).reshape(4, 4, 2, 48, 768)
+    sum_m.begin()
+    pass_far(2)
 
     row = yc * 128 + ids((128, 1024), 0)
     key = ids((128, 1024), 1)
@@ -474,45 +543,14 @@
             rcopy(kpair.at[h, k], kb2.at[h, k], dy_s.at[h, k], dy_r.at[h, k], partner).wait_recv()
         for i in range(4):
             total = kpair[h, 0, i].astype(F32) + kb2[h, 1, i].astype(F32) + kb2[h, 2, i].astype(F32) + kb2[h, 3, i].astype(F32)
-            back_tile(i, 128 * h, total.T, True)
+            back_tile(i, KV_AT[h], total.T, True)
 
     kv_here(0)
     o0, d0 = attend(0, lambda: None)
     dkv_begin(0)
-    pass_on(1)
-
-    w48 = wm[...].reshape(32, 48, 768).astype(F32)
-    dw[...] = w48[:, 24:].reshape(768, 768).astype(BF16)
-    wup = w48[:, :24].reshape(768, UP).astype(BF16)
-    lanes = slice(2048, 2048 + UP)
-    big[:, lanes] = mm(nm[...], wup) + spread(packed, up_at)
-    for i in range(4):
-        r = slice(128 * i, 128 * i + 128)
-        u = big[r, lanes]
-        cdf = 0.5 * (1.0 + lax.erf(u * np.float32(np.sqrt(0.5))))
-        pdf = jnp.exp(-0.5 * u * u) * np.float32(1.0 / np.sqrt(2.0 * np.pi))
-        hid[r, :] = (u * cdf).astype(BF16)
-        big[r, lanes] = cdf + u * pdf
-    part[...] = mm(hid[...], dw[...])
-    du[...] = (mm_nt(g, dw[...]) * big[:, lanes]).astype(BF16)
-    dn = mm_nt(du[...], wup)
-    grads = [
-        jnp.sum(dn * xh[...], axis=0, keepdims=True),
-        jnp.sum(dn, axis=0, keepdims=True),
-        jnp.sum(du[...].astype(F32), axis=0, keepdims=True),
-    ]
-    dxh[...] = dn * vec[2:3, :]
-    small = collect(grads[0], norm_at[2]) + collect(grads[1], norm_at[3]) + collect(grads[2], up_at)
-    small += collect(jnp.sum(ga[z].astype(F32), axis=0, keepdims=True), out_at)
-    dwu = mm_tn(nm[...], du[...]).reshape(32, 24, 768)
-    dwd = mm_tn(hid[...], g).reshape(32, 24, 768)
-    wm[...] = jnp.concatenate([dwu, dwd], axis=1).astype(BF16).reshape(4, 4, 2, 48, 768)
-    msend = rcopy(wm.at[:, :, 1 - c], mb1, ma_s.at[0], ma_r.at[0], partner)
-    msend.start()
-    pass_on(2)
-    dkv_pairs(0)
+    sum_m.pairs()
     kv_here(1)
-    o1, d1 = attend(1, m_pairs)
+    o1, d1 = attend(1, lambda: dkv_pairs(0))
     dkv_begin(1)
     kv_here(2)
     o2, d2 = attend(2, lambda: dkv_pairs(1))
@@ -528,9 +566,48 @@
     dwo = mm_tn(att[...], g).reshape(32, 8, 768)
     for i in range(4):
         r = slice(128 * i, 128 * i + 128)
-        back_tile(i, 384, jnp.where(low, d0[r], pltpu.roll(d1[r], 64, 1)), False)
-        back_tile(i, 512, jnp.where(low, d2[r], 0.0), False)
+        back_tile(i, Q_AT, jnp.where(low, d0[r], pltpu.roll(d1[r], 64, 1)), False)
+        back_tile(i, Q_AT + 128, jnp.where(low, d2[r], 0.0), False)
     dkv_last(0)
+    dkv_last(1)
+    dwq = mm_tn(na[...], dqkv[:, :EARLY]).reshape(32, 24, EARLY)
+    tail = [dwo[:, i : i + 1, EARLY:] for i in range(6)]
+    early = [dwq, dwo[:, :6, :EARLY], jnp.concatenate(tail[0:2], axis=2), jnp.concatenate(tail[2:4], axis=2)]
+    wq[:, :, :, :, :EARLY] = jnp.concatenate(early, axis=1).astype(BF16).reshape(4, 4, 2, 32, EARLY)
+    sum_e.begin()
+    big[:, :768] = mm_nt(dqkv[:, :EARLY], wn[:, :EARLY])
+    sum_e.pairs()
+    dkv_last(2)
+
+    toks = [rcopy(dxp.at[(z + k) % 4], rd.at[z], t_s.at[k], t_r.at[k], home[k]) for k in range(4)]
+    stay = pltpu.make_async_copy(dxp.at[z], rd.at[z], loc.at[1])
+    along, plain = jnp.zeros((1, 768), F32), jnp.zeros((1, 768), F32)
+    for k in (2, 1, 3, 0):
+        i = (z + k) % 4
+        r = pl.ds(pl.multiple_of(128 * i, 128), 128)
+        dn = big[r, :768] + mm_nt(dqkv[r, EARLY:], wn[:, EARLY:])
+        along += jnp.sum(dn * xh[r, :], axis=0, keepdims=True)
+        plain += jnp.sum(dn, axis=0, keepdims=True)
+        dx = (dxh[r, :] + dn * vec[0:1, :]).astype(BF16)
+        dxp[i] = mm_nt(dx, s[...]).astype(BF16)
+        if k:
+            toks[k].start()
+
+    @pl.when(swapped)
+    def _():
+        toks[0].start()
+
+    @pl.when(xhi == c)
+    def _():
+        stay.start()
+
+    dqb = jnp.sum(dqkv[...].astype(F32), axis=0, keepdims=True)
+    small += collect(along, norm_at[0]) + collect(plain, norm_at[1]) + collect(dqb, qkv_at)
+    dwl = mm_tn(na[...], dqkv[:, EARLY:]).reshape(32, 24, 128)
+    rows = [dwl, small.reshape(32, 8, 128)[:, :4]] + [t[:, :, 128 * i : 128 * i + 128] for t in tail[4:] for i in range(2)]
+    wq[:, :, :, :, EARLY:] = jnp.concatenate(rows, axis=1).astype(BF16).reshape(4, 4, 2, 32, 128)
+    sum_l.begin()
+    sum_m.quads()
     for d in osends:
         d.wait()
     obuf[z] = outp[z]
@@ -547,78 +624,31 @@
     def _():
         out_stay.start()
 
-    m_quads()
-    for h in (1, 2):
-        dkv_last(h)
-    dqb = jnp.sum(dqkv[...].astype(F32), axis=0, keepdims=True)
-    dn = mm_nt(dqkv[...], wn[...])
-    small += collect(jnp.sum(dn * xh[...], axis=0, keepdims=True), norm_at[0])
-    small += collect(jnp.sum(dn, axis=0, keepdims=True), norm_at[1]) + collect(dqb, qkv_at)
-    dx = (dxh[...] + dn * vec[0:1, :]).astype(BF16)
-    dwq = mm_tn(na[...], dqkv[...]).reshape(32, 24, QKV)
-    small = small.reshape(32, 8, 128)
-    row6 = jnp.concatenate([dwo[:, i : i + 1, 640:] for i in range(5)], axis=2)
-    row7 = jnp.concatenate([dwo[:, 5:6, 640:]] + [small[:, i : i + 1] for i in range(4)], axis=2)
-    wq[...] = jnp.concatenate([dwq, dwo[:, :6, :640], row6, row7], axis=1).astype(BF16).reshape(4, 4, 2, 32, QKV)
-
-    def qslot(k1, k2, cc):
-        return (y + k1 * (1 - cc) + k2 * cc) % 4, (x + k1 * cc + k2 * (1 - cc)) % 4
-
-    order = [(k1, k2) for k1 in (2, 1, 3, 0) for k2 in (2, 1, 3, 0)]
-    qsends = []
-    for k1, k2 in order:
-        yy, xx = qslot(k1, k2, 1 - c)
-        d = rcopy(wq.at[yy, xx, 1 - c], qb1.at[k1, k2], qa_s.at[k1, k2], qa_r.at[k1, k2], partner)
-        d.start()
-        qsends.append(d)
-    dxp[...] = mm_nt(dx, s[...]).astype(BF16).reshape(4, 128, 768)
-    toks = [rcopy(dxp.at[(z + k) % 4], rd.at[z], t_s.at[k], t_r.at[k], home[k]) for k in range(4)]
-    stay = pltpu.make_async_copy(dxp.at[z], rd.at[z], loc.at[1])
-    for k in range(1, 4):
-        toks[k].start()
-
-    @pl.when(swapped)
-    def _():
-        toks[0].start()
-
-    @pl.when(xhi == c)
-    def _():
-        stay.start()
-
-    for k1, k2 in order:
-        yy, xx = qslot(k1, k2, c)
-        rcopy(wq.at[yy, xx, c], qb1.at[k1, k2], qa_s.at[k1, k2], qa_r.at[k1, k2], partner).wait_recv()
-        qpair[k1, k2] = (wq[yy, xx, c].astype(F32) + qb1[k1, k2].astype(F32)).astype(BF16)
-        if k1:
-            d = rcopy(qpair.at[k1, k2], qb2.at[4 - k1, k2], qb_s.at[k1, k2], qb_r.at[4 - k1, k2], second[k1])
-            d.start()
-            qsends.append(d)
-    for k2 in (2, 1, 3, 0):
-        for k1 in range(1, 4):
-            rcopy(qpair.at[k1, k2], qb2.at[k1, k2], qb_s.at[k1, k2], qb_r.at[k1, k2], partner).wait_recv()
-        total = qpair[0, k2].astype(F32) + qb2[1, k2].astype(F32) + qb2[2, k2].astype(F32) + qb2[3, k2].astype(F32)
-        if k2:
-            qquad[k2] = total.astype(BF16)
-            d = rcopy(qquad.at[k2], qb3.at[4 - k2], qc_s.at[k2], qc_r.at[4 - k2], first[k2])
-            d.start()
-            qsends.append(d)
-    for k in range(1, 4):
-        rcopy(qquad.at[k], qb3.at[k], qc_s.at[k], qc_r.at[k], partner).wait_recv()
-    m_last()
-    total = total + qb3[1].astype(F32) + qb3[2].astype(F32) + qb3[3].astype(F32)
-    for i in range(4):
-        zs[i, 0:6, :QKV] = total[6 * i : 6 * i + 6]
-        zs[i, 0:6, QKV : QKV + UP] = fm[6 * i : 6 * i + 6, :]
-        zs[i, 0:1, QKV + UP :] = total[31:32, 128 + 128 * i : 256 + 128 * i]
+    sum_e.quads()
+    sum_l.pairs()
+    fm = sum_m.last()
+    sum_l.quads()
+    fe = sum_e.last()
+    dn_out[...] = fm[24:, :]
+    fl = sum_l.last()
+
+    for i in range(4):
+        r = slice(6 * i, 6 * i + 6)
+        zs[i, 0:6, :EARLY] = fe[r]
+        zs[i, 0:6, EARLY:QKV] = fl[r]
+        zs[i, 0:6, QKV : QKV + UP] = fm[r]
+        zs[i, 0:1, QKV + UP :] = fl[24 + i : 25 + i]
     zsends = [rcopy(zs.at[(z + k) % 4], zr.at[z], ze_s.at[k], ze_r.at[4 - k], zpeer[k]) for k in range(1, 4)]
     for d in zsends:
         d.start()
     zr[z] = zs[z]
-    dn_out[...] = fm[24:, :]
-    o8_out[...] = total[24:32]
-
-    for d in qsends + msends + ysends + halves + kvsends + [msend]:
+    o8_out[:, :EARLY] = fe[24:32]
+    o8_out[:, EARLY:] = fl[24:32]
+
+    for d in ysends + halves + kvsends:
         d.wait_send()
+    for each in (sum_m, sum_e, sum_l):
+        each.drain()
     for k in range(1, 4):
         toks[k].wait()
 
@@ -651,15 +681,16 @@
         vm(32, QKV), vm(48, 768), vm(768, 768), vm(3, 128, 256), vm(512, 4096, dtype=F32), vm(512, 768, dtype=F32),
         vm(512, 768), vm(512, 768), vm(8, 768, dtype=F32), vm(3, 4, 8, 128, 128), vm(3, 1024, 128),
         vm(3, 4, 4, 2, 128, 128), vm(512, 768), vm(512, 768), vm(512, 768, dtype=F32), vm(512, 768, dtype=F32),
-        vm(256, 768), vm(768, 768), vm(768, QKV), vm(512, 256), vm(512, QKV), vm(*tok), vm(*tok), vm(*tok), vm(48, 768, dtype=F32),
+        vm(256, 768), vm(768, 768), vm(768, QKV), vm(512, 256), vm(512, QKV), vm(*tok), vm(*tok), vm(*tok),
     ] + [vm(512, 128, dtype=F32)] * 7 + [
         vm(3, 4, 4, 128, 128), vm(3, 4, 4, 128, 128), vm(3, 4, 4, 128, 128),
         vm(4, 4, 48, 768), vm(4, 4, 48, 768), vm(4, 4, 48, 768), vm(4, 48, 768), vm(4, 48, 768),
-        vm(4, 4, 32, QKV), vm(4, 4, 32, QKV), vm(4, 4, 32, QKV), vm(4, 32, QKV), vm(4, 32, QKV),
+        vm(4, 4, 32, EARLY), vm(4, 4, 32, EARLY), vm(4, 4, 32, EARLY), vm(4, 32, EARLY), vm(4, 32, EARLY),
+        vm(4, 4, 32, 128), vm(4, 4, 32, 128), vm(4, 4, 32, 128), vm(4, 32, 128), vm(4, 32, 128),
         sem(2), sem(2), sem(2), sem(2, 4), sem(2, 4), sem(4), sem(4),
         sem(4), sem(4, 4), sem(4, 4), sem(4, 4), sem(4, 4), sem(4), sem(4, 4), sem(4, 4), sem(4, 4), sem(4, 4),
-        sem(3, 4), sem(3, 4), sem(3, 4), sem(3, 4), sem(3), sem(3), sem(3, 4), sem(3, 4),
-        sem(1), sem(1), sem(4), sem(4), sem(4), sem(4), sem(4, 4), sem(4, 4), sem(4, 4), sem(4, 4), sem(4), sem(4),
+        sem(3, 4), sem(3, 4), sem(3, 4), sem(3, 4), sem(3, 4), sem(3, 4), sem(3), sem(3), sem(3, 4), sem(3, 4),
+    ] + [sem(1), sem(1), sem(4), sem(4), sem(4), sem(4)] * 3 + [
         sem(4), sem(4), sem(4), sem(4), sem(4), sem(4),
     ]
     return pl.pallas_call(
@@ -686,13 +717,14 @@
     xn = cen * rstd
     mean, along = jnp.mean(dxh, axis=1, keepdims=True), jnp.mean(dxh * xn, axis=1, keepdims=True)
     dx_out[0] = g_ref[...].astype(F32) + rstd * (dxh - mean - xn * along)
-    pieces = [zr[i, 0:6, 384:576] for i in range(4)]
-    pieces += [zr[i, 0:6, 128 * h : 128 * h + 64] for i in range(4) for h in range(3)]
-    pieces += [zr[i, 0:6, 128 * h + 64 : 128 * h + 128] for i in range(4) for h in range(3)]
+    pieces = [zr[i, 0:6, Q_AT : Q_AT + 192] for i in range(4)]
+    pieces += [zr[i, 0:6, KV_AT[h] : KV_AT[h] + 64] for i in range(4) for h in range(3)]
+    pieces += [zr[i, 0:6, KV_AT[h] + 64 : KV_AT[h] + 128] for i in range(4) for h in range(3)]
     qkv[:, 0, :] = jnp.concatenate(pieces, axis=1)
     up[:, 0, :] = jnp.concatenate([zr[i, 0:6, QKV : QKV + UP] for i in range(4)], axis=1)
-    tails = [o8[6:7, 128 * i : 128 * i + 128] for i in range(5)] + [o8[7:8, :128]]
-    out_w[:, 0, :] = jnp.concatenate([o8[0:6, :], jnp.concatenate(tails, axis=0)], axis=1)
+    tails = [o8[6:7, 0:256], o8[6:7, 256:512], o8[7:8, 0:256], o8[7:8, 256:512]]
+    tails += [jnp.concatenate([o8[i : i + 1, 512:], o8[i + 1 : i + 2, 512:]], axis=1) for i in (4, 6)]
+    out_w[:, 0, :] = jnp.concatenate([o8[0:6, :512], jnp.concatenate(tails, axis=0)], axis=1)
     down[0] = dn[...]
     rows = sum(zr[i, 0:1, QKV + UP :] for i in range(4))
     for ref, a, b in zip(outs[6:], CUTS[:-1], CUTS[1:]):

time: 106 us -> 103 us (0.972)
  Pallas kernels: 105 us -> 102 us
    pallas_call x1, Pallas kernels: 102 us -> 99.1 us  [layer(): pl.pallas_call(layer_kernel, out_shape=(sh((128, 768), BF16), sh(tok, BF1...]
where the time goes in v4:
time: 103 us
  Pallas kernels  102 us (99%)
    pallas_call x1, Pallas kernels, layer(): pl.pallas_call(layer_kernel, out_shape=(sh((128, 768), BF16), sh(tok, BF1...  99.1 us
    pallas_call x1, Pallas kernels, finish(): pl.pallas_call(finish_kernel, out_shape=tuple(shapes), in_specs=[VMEM] *...  2.69 us

profile of v4, /device:TPU:1, one launch (start us, length us, event | category | flops | bytes accessed | tf_op | source)
XLA Modules:
  0.0 102.6 jit_solution(2382603317635963647)
XLA Ops:
  0.6 99.1 %layer.1 = (bf16[128,768]{1,0:T(8,128)(2,1)}, bf16[4,128,768]{2,1,0:T(8,128)(2,1)}, f32[4,8,1536]{2,1,0:T(8,128)}, f32[24,768]{1,0:T(8,128)}, f32[8,640]{1,0:T(8,128)}) custom-call(bf16[128,768]{1,0:T(8,128)(2,1)} %bitcast.5, bf16[128,768]{1,0:T(8,128)(2,1)} %bitcast.7, bf16[1,6,2304]{2,1,0:T(8,128)(2,1)} %qw_ref.1, bf16[1,6,3072]{2,1,0:T(8,128)(2,1)} %uw_ref.1, ...), custom_call_target="tpu_custom_call" | custom-call | tf_op jit(solution)/shard_map/layer/pallas_call | solution.py:696
  99.8 2.7 %finish.1 = (bf16[1,128,768]{2,1,0:T(8,128)(2,1)}, f32[1,128,768]{2,1,0:T(8,128)}, f32[6,1,2304]{2,1,0:T(1,128)}, f32[6,1,3072]{2,1,0:T(1,128)}, f32[6,1,768]{2,...) custom-call(bf16[128,768]{1,0:T(8,128)(2,1)} %bitcast.6, ...), custom_call_target="tpu_custom_call" | custom-call | tf_op jit(solution)/shard_map/finish/pallas_call | solution.py:740
